TPU v7x, 256 devices: a whole 4x4x8 slice. The times are simulated.
256 devices in a mesh: var: 16 (over y, x_lo, core), seq: 16 (over x_hi, z).
Axes of the slice: x: 4 (x_hi: 2, x_lo: 2; x = x_hi * 2 + x_lo), y: 4, z: 8, core: 2. Of those that a mesh axis runs over, the one named last changes fastest.
Arguments:
- patches: bfloat16 [96, 2048, 64], P('var', 'seq'), may hold values from -6 to 6
- patch_weight: bfloat16 [96, 64, 4096], P('var'), may hold values from -0.75 to 0.75
- var_embed: bfloat16 [96, 4096], P('var'), may hold values from -1.71 to 4.5
- agg_query: bfloat16 [4096, 32], replicated, may hold values from -1.5 to 1000
- norm_gain: bfloat16 [4096], replicated, may hold values from 0.5 to 1.5
- qkv_weight: bfloat16 [4096, 3, 4096], P(None, None, 'var'), may hold values from -0.21875 to 0.21875
- out_weight: bfloat16 [4096, 4096], P('var'), may hold values from -0.09375 to 0.09375
- head_cot: bfloat16 [2048, 6144], P('seq', 'var'), may hold values from -0.125 to 0.125
Outputs:
- head_grad: float32 [4096, 6144], P('seq', 'var')
All inputs are finite; a program needn't handle non-finite values.
Results may differ from a plain program's by a relative error of at most 0.033.
The roundings to bfloat16 on the way count: a program that leaves them out, or rounds other values in their place, can miss the bound.
Values may be sent and summed in bfloat16 or wider, within the bound.
No kernel may reach another device: no remote copies, remote signals or barrier semaphores. Data moves between devices by JAX's collectives and lax.ppermute only.
A program may use at most 128 MiB of HBM per device.

v0:
```python
import math

import jax
import jax.numpy as jnp
from jax import lax
from jax.sharding import PartitionSpec as P

eps = 1e-05


def merged(array, axis, combine):
    everything = jax.tree.map(lambda part: lax.all_gather(part, axis), array)
    initial = jax.tree.map(lambda part: part[0], everything)

    def turn(k, so_far):
        return combine(so_far, jax.tree.map(lambda part: part[k], everything))

    return lax.fori_loop(1, lax.axis_size(axis), turn, initial)


def layer_norm(tokens, gain):
    values = tokens.astype(jnp.float32)
    center = jnp.mean(values, axis=-1, keepdims=True)
    shifted = values - center
    spread = jnp.mean(shifted * shifted, axis=-1, keepdims=True)
    return (shifted * lax.rsqrt(spread + eps) * gain.astype(jnp.float32)).astype(jnp.bfloat16)


def combine_parts(first_part, second_part):
    top_a, total_a, numer_a = first_part
    top_b, total_b, numer_b = second_part
    top = jnp.maximum(top_a, top_b)
    scale_a = jnp.exp(top_a - top)
    scale_b = jnp.exp(top_b - top)
    total = total_a * scale_a + total_b * scale_b
    numer = numer_a * scale_a[..., None] + numer_b * scale_b[..., None]
    return (top, total, numer)


def body(patches, patch_weight, var_embed, agg_query, norm_gain, qkv_weight, out_weight, head_cot):
    count, tok_rows, pixels = patches.shape
    width = patch_weight.shape[2]
    heads = agg_query.shape[1]
    head_size = width // heads
    share = tok_rows // lax.axis_size("var")
    first_row = lax.axis_index("var") * share
    embedded = jnp.einsum("vrp,vpd->vrd", patches, patch_weight, preferred_element_type=jnp.float32)
    embedded = (embedded + var_embed.astype(jnp.float32)[:, None, :]).astype(jnp.bfloat16)
    scores = jnp.dot(
        embedded.reshape(count * tok_rows, width), agg_query, preferred_element_type=jnp.float32
    )
    scores = scores.reshape(count, tok_rows, heads) / math.sqrt(head_size)
    peak = jnp.max(scores, axis=0)
    weights = jnp.exp(scores - peak[None])
    total = jnp.sum(weights, axis=0)
    numer = jnp.zeros((tok_rows, heads, head_size), jnp.float32)
    for member in range(count):
        numer = numer + weights[member][..., None] * embedded[member].reshape(
            tok_rows, heads, head_size
        ).astype(jnp.float32)
    total, numer = (total, numer)
    top, total, numer = merged((peak, total, numer), "var", combine_parts)
    whole = (numer / total[..., None]).reshape(tok_rows, width).astype(jnp.bfloat16)
    own_rows = lax.dynamic_slice_in_dim(whole, first_row, share, 0)
    normed = layer_norm(whole, norm_gain)
    local_cols = qkv_weight.shape[2]
    local_heads = local_cols // head_size
    qkv = jnp.dot(
        normed, qkv_weight.reshape(width, 3 * local_cols), preferred_element_type=jnp.float32
    )
    qkv = qkv.astype(jnp.bfloat16).reshape(tok_rows, 3, local_heads, head_size)
    query = qkv[:, 0]
    keys = qkv[:, 1]
    values = qkv[:, 2]
    top = jnp.full((tok_rows, local_heads), -jnp.inf, jnp.float32)
    total = jnp.zeros((tok_rows, local_heads), jnp.float32)
    mixed = jnp.zeros((tok_rows, local_heads, head_size), jnp.float32)
    key_piece = lax.all_gather(keys, "seq", axis=0, tiled=True)
    value_piece = lax.all_gather(values, "seq", axis=0, tiled=True)
    block_scores = jnp.einsum(
        "thd,rhd->thr", query, key_piece, preferred_element_type=jnp.float32
    ) / math.sqrt(head_size)
    new_top = jnp.max(block_scores, axis=-1)
    scale = jnp.exp(top - new_top)
    weights = jnp.exp(block_scores - new_top[..., None])
    total = total * scale + jnp.sum(weights, axis=-1)
    update = jnp.einsum(
        "thr,rhd->thd",
        weights.astype(jnp.bfloat16),
        value_piece,
        preferred_element_type=jnp.float32,
    )
    mixed = mixed * scale[..., None] + update
    top, total, mixed = (new_top, total, mixed)
    attended = (mixed / total[..., None]).reshape(tok_rows, local_cols).astype(jnp.bfloat16)
    part = attended
    summed = lax.psum_scatter(
        jnp.dot(part, out_weight, preferred_element_type=jnp.float32).astype(jnp.bfloat16),
        "var",
        scatter_dimension=0,
        tiled=True,
    ).astype(jnp.float32)
    layer_part = (own_rows.astype(jnp.float32) + summed).astype(jnp.bfloat16)
    layer = lax.all_gather(layer_part, "var", axis=0, tiled=True)
    part = layer
    return lax.psum_scatter(
        lax.dot_general(
            part, head_cot, (((0,), (0,)), ((), ())), preferred_element_type=jnp.float32
        ).astype(jnp.bfloat16),
        "seq",
        scatter_dimension=0,
        tiled=True,
    ).astype(jnp.float32)


def solution(mesh):
    return jax.shard_map(
        body,
        mesh=mesh,
        in_specs=(
            P("var", "seq", None),
            P("var", None, None),
            P("var", None),
            P(),
            P(),
            P(None, None, "var"),
            P("var", None),
            P("seq", "var"),
        ),
        out_specs=P("seq", "var"),
        check_vma=False,
    )
```

profile of v0, /device:TPU:1, one launch (start us, length us, event | category | flops | bytes accessed | tf_op | source)
XLA Modules:
  0.0 766.2 jit_solution(15687009025931721361)
XLA Ops:
  6.5 1.0 convert_element_type.136
  8.5 2.7 add_convert_fusion
  11.2 4.3 convert_bitcast_fusion.5
  15.5 2.0 fusion.30
  18.1 2.1 copy.58
  20.7 1.2 copy-done.4
  22.3 1.2 copy-done.3
  23.9 1.2 copy-done.2
  25.8 5.3 fusion.9
  31.2 22.3 %all-gather.1 = f32[2048,32]{0,1:T(8,128)S(1)} all-gather(f32[128,32]{0,1:T(8,128)S(1)} %get-tuple-element.211), channel_id=3, replica_groups=mesh['var'=16,'seq'=16] {'var'}, dimensions={0}, use_global_device_ids=true | all-gather | bytes 278528 | tf_op jit(solution)/shard_map/all_gather | solution.py:12
  53.5 1.4 copy.49
  54.9 19.6 %all-gather = f32[2048,32]{0,1:T(8,128)S(1)} all-gather(f32[128,32]{0,1:T(8,128)S(1)} %get-tuple-element.230), channel_id=2, replica_groups=mesh['var'=16,'seq'=16] {'var'}, dimensions={0}, use_global_device_ids=true | all-gather | bytes 278528 | tf_op jit(solution)/shard_map/all_gather | solution.py:12
  74.5 1.3 copy.48
  76.1 8.8 %copy.42 = bf16[4096,3,256]{0,2,1:T(8,128)(2,1)} copy(bf16[4096,3,256]{2,0,1:T(8,128)(2,1)} %param.15) | data formatting | bytes 12582912 | tf_op args[5]
  84.9 126.1 %all-gather.9.cloned.1.call-done = f32[16,128,32,128]{3,2,1,0:T(8,128)} async-done(((f32[1,128,32,128]{3,2,1,0:T(8,128)}), f32[16,128,32,128]{3,2,1,0:T(8,128)}) %all-gather.9.cloned.1.call-update) | async-done | bytes 33554448 | tf_op jit(solution)/shard_map/all_gather | solution.py:12
  211.0 1.8 slice_bitcast_fusion
  212.7 70.9 %while.19 = (s32[]{:T(128)}, f32[128,32]{1,0:T(8,128)S(1)}, f32[128,32]{1,0:T(8,128)S(1)}, f32[128,32,128]{2,1,0:T(8,128)S(1)}, f32[16,128,32]{2,1,0:T(8,128)}, ...) while((s32[]{:T(128)}, f32[128,32]{1,0:T(8,128)S(1)}, ...), condition=%wide.region_3.0_spmd, body=%wide.region_2.0_spmd.sunk | while | flops 1597445 | bytes 6455447 | solution.py:18
  212.7 0.9 fusion.42
  213.7 3.8 fusion.43
  217.5 0.9 fusion.42
  218.4 3.8 fusion.43
  223.1 3.8 fusion.43
  227.9 3.8 fusion.43
  232.6 3.8 fusion.43
  237.3 3.8 fusion.43
  242.0 3.8 fusion.43
  246.8 3.8 fusion.43
  251.5 3.8 fusion.43
  256.2 3.8 fusion.43
  260.9 3.8 fusion.43
  265.7 3.8 fusion.43
  270.4 3.8 fusion.43
  275.1 3.8 fusion.43
  279.8 3.8 fusion.43
  283.6 2.1 convert_reduce_fusion
  285.7 1.9 fusion.6
  288.1 5.0 convolution_convert_fusion.2
  294.8 75.1 %all-gather.13.cloned.1.call-done = bf16[2048,1,2,128]{3,0,2,1:T(8,128)(2,1)} async-done(((bf16[128,1,2,128]{3,0,2,1:T(8,128)(2,1)}), bf16[2048,1,2,128]{3,0,2,1:T(8,128)(2,1)}) %all-gather.13.cloned.1.call-update) | async-done | bytes 1048592 | tf_op jit(solution)/shard_map/all_gather | solution.py:78
  369.9 1.7 fusion.31
  371.9 73.0 %all-gather.15.cloned.1.call-done = bf16[2048,1,2,128]{0,3,2,1:T(8,128)(2,1)} async-done(((bf16[128,1,2,128]{0,3,2,1:T(8,128)(2,1)}), bf16[2048,1,2,128]{0,3,2,1:T(8,128)(2,1)}) %all-gather.15.cloned.1.call-update) | async-done | bytes 1048592 | tf_op jit(solution)/shard_map/all_gather | solution.py:79
  444.9 1.9 fusion.18
  446.8 1.5 convolution_convert_fusion.1
  448.8 60.0 %reduce-scatter.3.cloned.1.call-done = bf16[8,4096]{1,0:T(8,128)(2,1)} async-done(((bf16[128,4096]{1,0:T(8,128)(2,1)}), bf16[8,4096]{1,0:T(8,128)(2,1)}) %reduce-scatter.3.cloned.1.call-update) | async-done | bytes 65552 | tf_op jit(solution)/shard_map/reduce_scatter | solution.py:97
  508.8 1.5 add_convert_fusion.1
  510.3 37.4 %all-gather.11.cloned.1.call-done = bf16[128,4096]{1,0:T(8,128)(2,1)} async-done(((bf16[8,4096]{1,0:T(8,128)(2,1)}), bf16[128,4096]{1,0:T(8,128)(2,1)}) %all-gather.11.cloned.1.call-update) | async-done | bytes 1048592 | tf_op jit(solution)/shard_map/all_gather | solution.py:104
  547.7 4.0 convolution_convert_fusion
  551.8 205.9 %reduce-scatter.5.cloned.1.call-done = bf16[256,384]{1,0:T(8,128)(2,1)} async-done(((bf16[4096,384]{1,0:T(8,128)(2,1)}), bf16[256,384]{1,0:T(8,128)(2,1)}) %reduce-scatter.5.cloned.1.call-update) | async-done | bytes 196624 | tf_op jit(solution)/shard_map/reduce_scatter | solution.py:106
  757.6 1.7 convert_element_type.164
  (70 shorter events, 19.0 us)
Async XLA Ops:
  6.5 1.9 copy-start
  6.5 204.4 %all-gather.9.cloned.1.call-start = ((), (), s32[]{:S(2)}) async-start(), calls=%async_computation.2 | async-start | bytes 35651584 | tf_op jit(solution)/shard_map/all_gather | solution.py:12
  11.2 4.3 copy-start.7
  18.1 2.2 copy-start.5
  20.3 1.6 copy-start.4
  21.9 1.6 copy-start.3
  23.5 1.6 copy-start.2
  31.2 338.7 %all-gather.13.cloned.1.call-start = ((), (), s32[]{:S(2)}) async-start(), calls=%async_computation.6 | async-start | bytes 1114112 | tf_op jit(solution)/shard_map/all_gather | solution.py:78
  76.1 8.8 %copy-start.9 = (bf16[4096]{0:T(1024)(128)(2,1)S(1)}, bf16[4096]{0:T(1024)(128)(2,1)}, u32[]{:S(2)}) copy-start(bf16[4096]{0:T(1024)(128)(2,1)} %param.14) | copy-start | bytes 24580
  293.9 151.0 %all-gather.15.cloned.1.call-start = ((), (), s32[]{:S(2)}) async-start(), calls=%async_computation.7 | async-start | bytes 1114112 | tf_op jit(solution)/shard_map/all_gather | solution.py:79
  294.7 214.0 %reduce-scatter.3.cloned.1.call-start = ((), (), s32[]{:S(2)}) async-start(), calls=%async_computation.3 | async-start | bytes 1114112 | tf_op jit(solution)/shard_map/reduce_scatter | solution.py:97
  444.9 1.9 copy-start.6
  448.3 99.4 %copy-start.8 = (bf16[128,384]{1,0:T(8,128)(2,1)S(1)}, bf16[128,384]{1,0:T(8,128)(2,1)}, u32[]{:S(2)}) copy-start(bf16[128,384]{1,0:T(8,128)(2,1)} %param.17) | copy-start | bytes 294916
  448.3 99.4 %all-gather.11.cloned.1.call-start = ((), (), s32[]{:S(2)}) async-start(), calls=%async_computation.4 | async-start | bytes 1114112 | tf_op jit(solution)/shard_map/all_gather | solution.py:104
  510.3 247.4 %reduce-scatter.5.cloned.1.call-start = ((), (), s32[]{:S(2)}) async-start(), calls=%async_computation.5 | async-start | bytes 3342336 | tf_op jit(solution)/shard_map/reduce_scatter | solution.py:106
  547.7 211.6 %copy-start.1 = (bf16[6,64,4096]{2,1,0:T(8,128)(2,1)S(1)}, bf16[6,64,4096]{2,1,0:T(8,128)(2,1)}, u32[]{:S(2)}) copy-start(bf16[6,64,4096]{2,1,0:T(8,128)(2,1)} %param.11) | copy-start | bytes 9437188
Sparse Core Ops, SparseCore 0:
  31.3 179.6 all-gather.8
  294.0 75.8 all-gather.12
  372.4 72.4 all-gather.14
  448.4 60.2 reduce-scatter.2
  510.6 37.0 all-gather.10
  552.1 205.4 reduce-scatter.4
where the time goes:
time: 771 us; the launch traced here: 766 us
  waiting for transfers between devices  578 us (75%)
  other arithmetic  89 us (12%)
  blocking collectives  41.9 us (5%)
  local copies, waits for them, and re-layouts  24.7 us (3%)
  matrix products  18.7 us (2%)
  between operations  13.7 us (2%)
    reduce_scatter x1, waiting for transfers between devices, body(): lax.psum_scatter(lax.dot_general(part, head_cot, (((0,), (0,)), ((), ()))...  206 us
    all_gather x1, waiting for transfers between devices, merged(): everything = jax.tree.map(lambda part: lax.all_gather(part, axis), array)  126 us
    all_gather x1, waiting for transfers between devices, body(): key_piece = lax.all_gather(keys, 'seq', axis=0, tiled=True)  75.1 us
    all_gather x1, waiting for transfers between devices, body(): value_piece = lax.all_gather(values, 'seq', axis=0, tiled=True)  73 us
    reduce_scatter x1, waiting for transfers between devices, body(): lax.psum_scatter(jnp.dot(part, out_weight, preferred_element_type=jnp.flo...  60 us
    add x15, other arithmetic, combine_parts(): numer = numer_a * scale_a[..., None] + numer_b * scale_b[..., None]  56.3 us
    all_gather x2, blocking collectives, merged(): everything = jax.tree.map(lambda part: lax.all_gather(part, axis), array)  41.9 us
    all_gather x1, waiting for transfers between devices, body(): layer = lax.all_gather(layer_part, 'var', axis=0, tiled=True)  37.4 us
  transfers between devices with their start and end apart: 6, of which 6 were waited for; matrix products, arithmetic and copies ran while one was open for 2% of the time, Pallas kernels for 0%

commit v1 on v0

v1 whole, which is shorter than its diff:
```python
import math

import jax
import jax.numpy as jnp
from jax import lax
from jax.experimental import pallas as pl
from jax.experimental.pallas import tpu as pltpu
from jax.sharding import Mesh, PartitionSpec as P

EPS = 1e-05
HD = 128
F32 = jnp.float32
BF16 = jnp.bfloat16
VAR = ("y", "xl", "c")
CHIPS = ("y", "xl")
SEQ = ("xh", "z")
NT = (((1,), (1,)), ((), ()))
TN = (((0,), (0,)), ((), ()))
NN = (((1,), (0,)), ((), ()))
MB = 1024 * 1024


def dot(a, b, dims):
    return lax.dot_general(a, b, dims, preferred_element_type=F32)


def params():
    return pltpu.CompilerParams(vmem_limit_bytes=40 * MB)


def in_three(x):
    high = x.astype(BF16).astype(F32)
    rest = x - high
    middle = rest.astype(BF16).astype(F32)
    return high, middle, rest - middle


def embed_kernel(pixels_ref, weight_ref, shift_ref, query_ref, out_ref, embedded, scores):
    member = pl.program_id(0)
    count = embedded.shape[0]
    width = weight_ref.shape[2]
    heads = query_ref.shape[0]
    rows = pixels_ref.shape[2]
    chosen = lax.broadcasted_iota(jnp.int32, shift_ref.shape, 0) == member
    shift = jnp.sum(jnp.where(chosen, shift_ref[...].astype(F32), 0.0), axis=0, keepdims=True)
    step = 1024
    total = jnp.zeros((rows, heads), F32)
    for at in range(0, width, step):
        block = dot(pixels_ref[0], weight_ref[0, :, at : at + step], TN)
        block = (block + shift[:, at : at + step]).astype(BF16)
        embedded[member, :, at : at + step] = block
        total = total + dot(block, query_ref[:, at : at + step], NT)
    scores[member] = total / math.sqrt(HD)

    @pl.when(member == count - 1)
    def _():
        every = scores[...]
        peak = jnp.max(every, axis=0)
        weights = jnp.exp(every - peak[None])
        total = jnp.sum(weights, axis=0)
        for h in range(heads):
            cols = slice(h * HD, (h + 1) * HD)
            numer = weights[0][:, h : h + 1] * embedded[0, :, cols].astype(F32)
            for v in range(1, count):
                numer = numer + weights[v][:, h : h + 1] * embedded[v, :, cols].astype(F32)
            out_ref[:, cols] = numer.astype(BF16)
        p0, p1, p2 = in_three(peak)
        t0, t1, t2 = in_three(total)
        blank = jnp.zeros_like(peak)
        out_ref[:, width : width + 128] = jnp.concatenate([p0, p1, p2, t0], axis=1).astype(BF16)
        out_ref[:, width + 128 : width + 256] = jnp.concatenate(
            [t1, t2, blank, blank], axis=1
        ).astype(BF16)


def embed(pixels, weight, shift, query):
    count, depth, rows = pixels.shape
    width = weight.shape[2]
    heads = query.shape[0]
    return pl.pallas_call(
        embed_kernel,
        grid=(count,),
        in_specs=[
            pl.BlockSpec((1, depth, rows), lambda v: (v, 0, 0)),
            pl.BlockSpec((1, depth, width), lambda v: (v, 0, 0)),
            pl.BlockSpec((count, width), lambda v: (0, 0)),
            pl.BlockSpec((heads, width), lambda v: (0, 0)),
        ],
        out_specs=pl.BlockSpec((rows, width + 256), lambda v: (0, 0)),
        out_shape=jax.ShapeDtypeStruct((rows, width + 256), BF16),
        scratch_shapes=[
            pltpu.VMEM((count, rows, width), BF16),
            pltpu.VMEM((count, rows, heads), F32),
        ],
        compiler_params=params(),
        name="embed",
    )(pixels, weight, shift, query)


def merge_kernel(parts_ref, gain_ref, normed_ref, kept_ref, whole):
    rows, padded = parts_ref.shape
    width = padded - 256
    heads = width // HD
    share = 8
    sources = rows // share
    stats = parts_ref[:, width:].astype(F32)
    peak = stats[:, 0:32] + stats[:, 32:64] + stats[:, 64:96]
    total = stats[:, 96:128] + stats[:, 128:160] + stats[:, 160:192]
    peak = peak.reshape(sources, share, heads)
    total = total.reshape(sources, share, heads)
    top = jnp.max(peak, axis=0)
    scale = jnp.exp(peak - top[None])
    total = jnp.sum(total * scale, axis=0)
    scale = scale.reshape(rows, heads)
    sums = jnp.zeros((share, HD), F32)
    last = None
    for h in range(heads):
        cols = slice(h * HD, (h + 1) * HD)
        numer = jnp.zeros((share, HD), F32)
        for at in range(0, rows, 16):
            block = parts_ref[at : at + 16, cols].astype(F32) * scale[at : at + 16, h : h + 1]
            numer = numer + block[:8] + block[8:]
        value = (numer / total[:, h : h + 1]).astype(BF16).astype(F32)
        whole[:, cols] = value
        sums = sums + value
        if h % 2 == 0:
            last = value
        else:
            kept_ref[(h // 2) * 16 : (h // 2) * 16 + 16, :] = jnp.concatenate(
                [last, value], axis=0
            ).astype(BF16)
    center = jnp.sum(sums, axis=1, keepdims=True) / width
    squares = jnp.zeros((share, HD), F32)
    for h in range(heads):
        shifted = whole[:, h * HD : (h + 1) * HD] - center
        squares = squares + shifted * shifted
    factor = lax.rsqrt(jnp.sum(squares, axis=1, keepdims=True) / width + EPS)
    for h in range(heads):
        cols = slice(h * HD, (h + 1) * HD)
        value = (whole[:, cols] - center) * factor * gain_ref[:, cols].astype(F32)
        twice = jnp.concatenate([value, value], axis=0).astype(BF16)
        for at in range(0, normed_ref.shape[0], 16):
            normed_ref[at : at + 16, cols] = twice


def merge(parts, gain, copies):
    rows, padded = parts.shape
    width = padded - 256
    return pl.pallas_call(
        merge_kernel,
        out_shape=(
            jax.ShapeDtypeStruct((copies * 8, width), BF16),
            jax.ShapeDtypeStruct((width // 16, HD), BF16),
        ),
        scratch_shapes=[pltpu.VMEM((8, width), F32)],
        compiler_params=params(),
        name="merge",
    )(parts, gain)


def qkv_kernel(place_ref, mine_ref, other_ref, weight_ref, kv_ref, keep_ref, send_ref, tokens, made):
    step = pl.program_id(0)
    core = place_ref[0]
    parity = place_ref[1]
    half = mine_ref.shape[0]

    @pl.when(step == 0)
    def _():
        tokens[pl.ds(pl.multiple_of(core * half, half), half), :] = mine_ref[...]
        tokens[pl.ds(pl.multiple_of((1 - core) * half, half), half), :] = other_ref[...]

    made[step] = dot(tokens[...], weight_ref[0], NN).astype(BF16)

    @pl.when(step == 2)
    def _():
        query = made[0]
        first, second = query[:, :HD], query[:, HD:]
        keep_ref[...] = jnp.where(parity == 0, first, second)
        send_ref[...] = jnp.where(parity == 0, second, first)
        rows = 2 * half
        for p in range(2):
            cols = slice(p * HD, (p + 1) * HD)
            keys, values = made[1, :, cols], made[2, :, cols]
            for to in range(p, 16, 2):
                kv_ref[to * rows : (to + 1) * rows, :HD] = keys
                kv_ref[to * rows : (to + 1) * rows, HD:] = values


def project(place, mine, other, weight):
    half, width = mine.shape
    cols = weight.shape[2]
    rows = 2 * half
    whole = lambda s: (0, 0)
    return pl.pallas_call(
        qkv_kernel,
        grid=(3,),
        in_specs=[
            pl.BlockSpec(memory_space=pltpu.SMEM),
            pl.BlockSpec((half, width), whole),
            pl.BlockSpec((half, width), whole),
            pl.BlockSpec((1, width, cols), lambda s: (s, 0, 0)),
        ],
        out_specs=[
            pl.BlockSpec((16 * rows, 2 * HD), whole),
            pl.BlockSpec((rows, HD), whole),
            pl.BlockSpec((rows, HD), whole),
        ],
        out_shape=[
            jax.ShapeDtypeStruct((16 * rows, 2 * HD), BF16),
            jax.ShapeDtypeStruct((rows, HD), BF16),
            jax.ShapeDtypeStruct((rows, HD), BF16),
        ],
        scratch_shapes=[pltpu.VMEM((rows, width), BF16), pltpu.VMEM((3, rows, cols), BF16)],
        compiler_params=params(),
        name="project",
    )(place, mine, other, weight)


def attend_kernel(place_ref, keep_ref, got_ref, kv_ref, out_ref):
    parity = place_ref[1]
    keys, values = kv_ref[:, :HD], kv_ref[:, HD:]
    mixed = []
    for band in range(2):
        query = jnp.where(parity == band, keep_ref[...], got_ref[...])
        scores = dot(query, keys, NT) / math.sqrt(HD)
        peak = jnp.max(scores, axis=1, keepdims=True)
        weights = jnp.exp(scores - peak)
        total = jnp.sum(weights, axis=1, keepdims=True)
        mixed.append(dot(weights.astype(BF16), values, NN) / total)
    for chip in range(8):
        for core in range(2):
            at = core * 64 + chip * 8
            to = (chip * 2 + core) * 16
            out_ref[to : to + 16, :] = jnp.concatenate(
                [mixed[0][at : at + 8], mixed[1][at : at + 8]], axis=0
            ).astype(BF16)


def attend(place, keep, got, kv):
    return pl.pallas_call(
        attend_kernel,
        in_specs=[pl.BlockSpec(memory_space=pltpu.SMEM)] + [pl.BlockSpec(memory_space=pltpu.VMEM)] * 3,
        out_shape=jax.ShapeDtypeStruct((256, HD), BF16),
        compiler_params=params(),
        name="attend",
    )(place, keep, got, kv)


def output_kernel(parts_ref, weight_ref, out_ref, attended):
    for pair in range(8):
        for parity in range(2):
            for source in range(16):
                head = 2 * source + parity
                attended[pair * 16 : pair * 16 + 16, head * HD : (head + 1) * HD] = parts_ref[
                    2 * pair + parity, source * 16 : source * 16 + 16, :
                ]
    product = dot(attended[...], weight_ref[...], NN)
    rows = product.shape[0]
    for band in range(0, 16, 2):
        residual = []
        for b in (band, band + 1):
            kept = parts_ref[b, 256:272, :].astype(F32)
            residual.append(jnp.concatenate([kept[:8], kept[8:]], axis=1))
        at = band * 8
        block = (jnp.concatenate(residual, axis=0) + product[at : at + 16]).astype(BF16)
        for copy in range(out_ref.shape[0] // rows):
            out_ref[copy * rows + at : copy * rows + at + 16, :] = block


def output(parts, weight, copies):
    width, cols = weight.shape
    rows = 128
    return pl.pallas_call(
        output_kernel,
        out_shape=jax.ShapeDtypeStruct((copies * rows, cols), BF16),
        scratch_shapes=[pltpu.VMEM((rows, width), BF16)],
        compiler_params=params(),
        name="output",
    )(parts, weight)


def swap(x, axis, size):
    return lax.ppermute(x, axis, [(k, k ^ 1) for k in range(size)])


def exchange(x, axes):
    return lax.all_to_all(x, axes, 0, 0, tiled=True)


def body(patches, patch_weight, var_embed, agg_query, norm_gain, qkv_weight, out_weight, head_cot):
    core = lax.axis_index("c")
    place = jnp.stack([core, lax.axis_index("z") % 2]).astype(jnp.int32)
    band = lax.axis_index(SEQ)
    width = out_weight.shape[1]

    cols = lax.dynamic_slice_in_dim(out_weight, band * 256, 256, 1)
    cols = lax.all_gather(cols, VAR, axis=0, tiled=True)
    cot = lax.all_gather(head_cot, SEQ, axis=0, tiled=True)
    cot = cot.reshape(16, 8, 2, 8, 384).transpose(2, 1, 0, 3, 4).reshape(2, 1024, 384)

    parts = embed(patches.transpose(0, 2, 1), patch_weight, var_embed, agg_query.T)
    parts = exchange(parts, VAR)
    normed, kept = merge(parts, norm_gain.reshape(1, width), 8)
    normed = exchange(normed, CHIPS)
    other = swap(normed, "c", 2)
    kv, query, query_out = project(place, normed, other, qkv_weight.transpose(1, 0, 2))
    query_in = swap(query_out, "z", 8)
    kv = exchange(kv, SEQ)
    attended = attend(place, query, query_in, kv)
    attended = exchange(attended, VAR)
    sent = jnp.concatenate(
        [jnp.broadcast_to(attended[None], (16, 256, HD)), kept.reshape(16, 16, HD)], axis=1
    )
    got = exchange(sent, SEQ)
    layer = output(got, cols, 8)
    layer = exchange(layer, CHIPS)
    other = swap(layer, "c", 2)
    first = lax.dynamic_index_in_dim(cot, core, 0, keepdims=False)
    second = lax.dynamic_index_in_dim(cot, 1 - core, 0, keepdims=False)
    return dot(layer, first, TN) + dot(other, second, TN)


def solution(mesh):
    whole = Mesh(mesh.devices.reshape(4, 2, 2, 2, 8), ("y", "xl", "c", "xh", "z"))
    return jax.shard_map(
        body,
        mesh=whole,
        in_specs=(
            P(VAR, SEQ, None),
            P(VAR, None, None),
            P(VAR, None),
            P(),
            P(),
            P(None, None, VAR),
            P(VAR, None),
            P(SEQ, VAR),
        ),
        out_specs=P(SEQ, VAR),
        check_vma=False,
    )
```

time: 771 us -> 215 us (0.28)
  waiting for transfers between devices: 578 us -> 104 us
  other arithmetic: 89 us -> 1.14 us
  starting transfers between devices: 0.21 us -> 37.1 us
  blocking collectives: 41.9 us -> 24.4 us
  matrix products: 18.7 us -> 1.7 us
  Pallas kernels: 0 us -> 15.8 us
  local copies, waits for them, and re-layouts: 24.7 us -> 13.7 us
    all_gather x4 -> x2, waiting for transfers between devices: 312 us -> 25 us  [the longest x1 25 us: body(): cot = lax.all_gather(head_cot, SEQ, axis=0, tiled=True)]
    reduce_scatter x2 -> x0, waiting for transfers between devices: 266 us -> none  [the longest x1 206 us: body(): lax.psum_scatter(lax.dot_general(part, head_cot, (((0,), (0,)), ((), ()))...]
    add x31 -> x0, other arithmetic: 75.7 us -> none  [the longest x15 56.3 us: combine_parts(): numer = numer_a * scale_a[..., None] + numer_b * scale_b[..., None]]
    all_to_all x0 -> x4, waiting for transfers between devices: none -> 53.3 us  [exchange(): return lax.all_to_all(x, axes, 0, 0, tiled=True)]
    all_gather x2 -> x0, blocking collectives: 41.9 us -> none  [merged(): everything = jax.tree.map(lambda part: lax.all_gather(part, axis), array)]
    all_to_all x0 -> x4, starting transfers between devices: none -> 28.7 us  [exchange(): return lax.all_to_all(x, axes, 0, 0, tiled=True)]
    ppermute x0 -> x3, waiting for transfers between devices: none -> 25 us  [swap(): return lax.ppermute(x, axis, [(k, k ^ 1) for k in range(size)])]
    all_to_all x0 -> x2, blocking collectives: none -> 24.4 us  [exchange(): return lax.all_to_all(x, axes, 0, 0, tiled=True)]
  transfers between devices with their start and end apart: 6 -> 9, of which waited for: 6 -> 7; matrix products, arithmetic and copies ran while one was open for 2% -> 2% of each run, Pallas kernels for 0% -> 3%
where the time goes in v1:
time: 215 us; the launch traced here: 211 us
  waiting for transfers between devices  104 us (48%)
  starting transfers between devices  37.1 us (17%)
  blocking collectives  24.4 us (11%)
  Pallas kernels  15.8 us (7%)
  local copies, waits for them, and re-layouts  13.7 us (6%)
  between operations  13.6 us (6%)
    all_to_all x4, waiting for transfers between devices, exchange(): return lax.all_to_all(x, axes, 0, 0, tiled=True)  53.3 us
    all_to_all x4, starting transfers between devices, exchange(): return lax.all_to_all(x, axes, 0, 0, tiled=True)  28.7 us
    ppermute x3, waiting for transfers between devices, swap(): return lax.ppermute(x, axis, [(k, k ^ 1) for k in range(size)])  25 us
    all_gather x1, waiting for transfers between devices, body(): cot = lax.all_gather(head_cot, SEQ, axis=0, tiled=True)  25 us
    all_to_all x2, blocking collectives, exchange(): return lax.all_to_all(x, axes, 0, 0, tiled=True)  24.4 us
    unnamed x20, local copies, waits for them, and re-layouts  11.2 us
    pallas_call x1, Pallas kernels, embed(): pl.pallas_call(embed_kernel, grid=(count,), in_specs=[pl.BlockSpec((1, de...  9.41 us
    ppermute x3, starting transfers between devices, swap(): return lax.ppermute(x, axis, [(k, k ^ 1) for k in range(size)])  8.31 us
  transfers between devices with their start and end apart: 9, of which 7 were waited for; matrix products, arithmetic and copies ran while one was open for 2% of the time, Pallas kernels for 3%

profile of v1, /device:TPU:1, one launch (start us, length us, event | category | flops | bytes accessed | tf_op | source)
XLA Modules:
  0.0 211.4 jit_solution(3044824672114727193)
XLA Ops:
  6.5 0.0 copy-start
  6.5 0.0 copy-start.3
  6.5 2.0 copy-done.3
  8.6 0.9 copy-done.6
  9.5 0.9 copy-done.7
  10.4 0.8 copy-done.8
  11.3 9.4 %embed.1 = bf16[128,4352]{1,0:T(8,128)(2,1)S(1)} custom-call(bf16[6,64,128]{2,1,0:T(8,128)(2,1)S(1)} %bitcast.38, bf16[6,64,4096]{2,1,0:T(8,128)(2,1)S(1)} %copy-done.3, bf16[6,4096]{1,0:T(8,128)(2,1)S(1)} %copy-done.8, bf16[32,4096]{1,0:T(8,128)(2,1)S(1)} %bitcast.37), custom_call_target="tpu_custom_call" | custom-call | tf_op jit(solution)/shard_map/embed/pallas_call | solution.py:80
  20.7 0.0 copy-start.2
  20.7 1.0 copy-done.2
  21.7 7.0 %all-to-all-start = ((bf16[16,8,4352]{2,1,0:T(8,128)(2,1)}), bf16[16,8,4352]{2,1,0:T(8,128)(2,1)S(1)}, u32[]{:S(2)}, u32[]{:S(2)}) async-start(bf16[16,8,4352]{2,1,0:T(8,128)(2,1)} %bitcast.30), calls=%async_computation | async-start | bytes 2228224 | tf_op jit(solution)/shard_map/all_to_all | solution.py:287
  28.7 0.0 all-gather.3.cloned.1.call-start
  28.8 0.0 copy-done
  28.8 0.7 constant_dynamic-slice_fusion
  29.5 0.0 all-gather.3.cloned.1.call-update
  29.5 0.0 copy-done.9
  29.5 15.8 %all-to-all-done = bf16[16,8,4352]{2,1,0:T(8,128)(2,1)S(1)} async-done(((bf16[16,8,4352]{2,1,0:T(8,128)(2,1)}), bf16[16,8,4352]{2,1,0:T(8,128)(2,1)S(1)}, u32[]{:S(2)}, u32[]{:S(2)}) %all-to-all-start) | async-done | bytes 1114144 | tf_op jit(solution)/shard_map/all_to_all | solution.py:287
  45.3 1.1 merge.1
  46.5 13.8 %all_to_all.59 = bf16[8,8,4096]{2,1,0:T(8,128)(2,1)S(1)} all-to-all(bf16[8,8,4096]{2,1,0:T(8,128)(2,1)S(1)} %bitcast.36), channel_id=1, replica_groups=mesh['y'=4,'xl'=2,'c'=2,'xh'=2,'z'=8] {'y','xl'}, dimensions={0} | all-to-all | bytes 1048576 | tf_op jit(solution)/shard_map/all_to_all | solution.py:287
  60.3 2.0 collective-permute-start
  62.3 0.1 pad_add_fusion.place_ref
  62.4 1.5 collective-permute-done.other_ref
  63.8 2.8 %copy-done.1 = bf16[4096,3,256]{2,0,1:T(8,128)(2,1)S(1)} copy-done((bf16[4096,3,256]{2,0,1:T(8,128)(2,1)S(1)}, bf16[4096,3,256]{2,0,1:T(8,128)(2,1)}, u32[]{:S(2)}) %copy-start.1) | copy-done | bytes 6291480
  66.7 2.2 %project.1 = (bf16[2048,256]{1,0:T(8,128)(2,1)S(1)}, bf16[128,128]{1,0:T(8,128)(2,1)S(1)}, bf16[128,128]{1,0:T(8,128)(2,1)S(1)}) custom-call(s32[2]{0:T(128)S(1)} %pad_add_fusion.place_ref, bf16[64,4096]{1,0:T(8,128)(2,1)S(1)} %bitcast.34, bf16[64,4096]{1,0:T(8,128)(2,1)S(1)} %collective-permute-done.other_ref, bf16[3,4096,256]{2,1,0:T(8,128)(2,1)S(1)} %bitcast.28), custom_call_target="tpu_custom_call" | custom-call | tf_op jit(solution)/shard_map/project/pallas_call | solution.py:194
  68.9 0.0 copy-start.5
  68.9 1.0 copy-done.5
  69.8 11.0 %all-to-all-start.2 = ((bf16[16,128,256]{2,1,0:T(8,128)(2,1)}), bf16[16,128,256]{2,1,0:T(8,128)(2,1)S(1)}, u32[]{:S(2)}, u32[]{:S(2)}) async-start(bf16[16,128,256]{2,1,0:T(8,128)(2,1)} %bitcast.35), calls=%async_computation.2 | async-start | bytes 2097152 | tf_op jit(solution)/shard_map/all_to_all | solution.py:287
  80.9 1.4 collective-permute-start.1
  82.2 23.5 %collective-permute-done.1.got_ref = bf16[128,128]{1,0:T(8,128)(2,1)S(1)} collective-permute-done((bf16[128,128]{1,0:T(8,128)(2,1)S(1)}, bf16[128,128]{1,0:T(8,128)(2,1)S(1)}, u32[]{:S(2)}, u32[]{:S(2)}) %collective-permute-start.1) | collective-permute-done | bytes 32800 | tf_op jit(solution)/shard_map/ppermute | solution.py:283
  105.8 2.1 %all-to-all-done.2 = bf16[16,128,256]{2,1,0:T(8,128)(2,1)S(1)} async-done(((bf16[16,128,256]{2,1,0:T(8,128)(2,1)}), bf16[16,128,256]{2,1,0:T(8,128)(2,1)S(1)}, u32[]{:S(2)}, u32[]{:S(2)}) %all-to-all-start.2) | async-done | bytes 1048608 | tf_op jit(solution)/shard_map/all_to_all | solution.py:287
  107.9 2.5 %attend.1 = bf16[256,128]{1,0:T(8,128)(2,1)} custom-call(s32[2]{0:T(128)S(1)} %pad_add_fusion.place_ref, bf16[128,128]{1,0:T(8,128)(2,1)S(1)} %get-tuple-element.11.keep_ref, bf16[128,128]{1,0:T(8,128)(2,1)S(1)} %collective-permute-done.1.got_ref, bf16[2048,256]{1,0:T(8,128)(2,1)S(1)} %bitcast.31), custom_call_target="tpu_custom_call" | custom-call | tf_op jit(solution)/shard_map/attend/pallas_call | solution.py:240
  110.4 6.8 %all-to-all-start.3 = ((bf16[16,16,128]{2,1,0:T(8,128)(2,1)}), bf16[16,16,128]{2,1,0:T(8,128)(2,1)S(1)}, u32[]{:S(2)}, u32[]{:S(2)}) async-start(bf16[16,16,128]{2,1,0:T(8,128)(2,1)} %bitcast.11), calls=%async_computation.3 | async-start | bytes 131072 | tf_op jit(solution)/shard_map/all_to_all | solution.py:287
  117.2 0.0 all-gather.5.cloned.1.call-start
  117.2 0.7 all-gather.5.cloned.1.call-update
  117.9 5.1 %all-to-all-done.3 = bf16[16,16,128]{2,1,0:T(8,128)(2,1)S(1)} async-done(((bf16[16,16,128]{2,1,0:T(8,128)(2,1)}), bf16[16,16,128]{2,1,0:T(8,128)(2,1)S(1)}, u32[]{:S(2)}, u32[]{:S(2)}) %all-to-all-start.3) | async-done | bytes 65568 | tf_op jit(solution)/shard_map/all_to_all | solution.py:287
  123.0 0.2 broadcast_in_dim.9
  123.2 1.1 pad_maximum_fusion
  124.3 3.8 %all-to-all-start.4 = ((bf16[16,272,128]{2,1,0:T(8,128)(2,1)}), bf16[16,272,128]{2,1,0:T(8,128)(2,1)S(1)}, u32[]{:S(2)}, u32[]{:S(2)}) async-start(bf16[16,272,128]{2,1,0:T(8,128)(2,1)} %pad_maximum_fusion), calls=%async_computation.4 | async-start | bytes 2228224 | tf_op jit(solution)/shard_map/all_to_all | solution.py:287
  128.1 0.0 all-gather.3.cloned.1.call-done.weight_ref
  128.2 30.3 %all-to-all-done.4.parts_ref = bf16[16,272,128]{2,1,0:T(8,128)(2,1)S(1)} async-done(((bf16[16,272,128]{2,1,0:T(8,128)(2,1)}), bf16[16,272,128]{2,1,0:T(8,128)(2,1)S(1)}, u32[]{:S(2)}, u32[]{:S(2)}) %all-to-all-start.4) | async-done | bytes 1114144 | tf_op jit(solution)/shard_map/all_to_all | solution.py:287
  158.4 1.6 copy-done.4
  160.0 0.6 output.1
  160.6 10.6 %all_to_all.60 = bf16[8,128,256]{2,1,0:T(8,128)(2,1)S(1)} all-to-all(bf16[8,128,256]{2,1,0:T(8,128)(2,1)S(1)} %bitcast.32), channel_id=1, replica_groups=mesh['y'=4,'xl'=2,'c'=2,'xh'=2,'z'=8] {'y','xl'}, dimensions={0} | all-to-all | bytes 1048576 | tf_op jit(solution)/shard_map/all_to_all | solution.py:287
  171.2 4.9 %collective-permute-start.2 = (bf16[1024,256]{1,0:T(8,128)(2,1)S(1)}, bf16[1024,256]{1,0:T(8,128)(2,1)S(1)}, u32[]{:S(2)}, u32[]{:S(2)}) collective-permute-start(bf16[1024,256]{1,0:T(8,128)(2,1)S(1)} %bitcast.42), channel_id=1, source_target_pairs={{0,16},{16,0},{1,17},{17,1},{2,18},{18,2},{3,19},{19,3},{4,20},{20... | collective-permute-start | bytes 1572872 | tf_op jit(solution)/shard_map/ppermute | solution.py:283
  176.2 25.0 %all-gather.5.cloned.1.call-done = bf16[2048,384]{1,0:T(8,128)(2,1)} async-done(((bf16[128,384]{1,0:T(8,128)(2,1)}), bf16[2048,384]{1,0:T(8,128)(2,1)}) %all-gather.5.cloned.1.call-update) | async-done | bytes 1572880 | tf_op jit(solution)/shard_map/all_gather | solution.py:298
  201.2 1.6 copy.9
  202.8 0.5 fusion.1
  203.3 0.0 collective-permute-done.2
  203.3 1.2 convolution_add_fusion
  (7 shorter events, 0.0 us)
Async XLA Ops:
  6.5 22.3 %copy-start = (bf16[256,4096]{1,0:T(8,128)(2,1)S(1)}, bf16[256,4096]{1,0:T(8,128)(2,1)}, u32[]{:S(2)}) copy-start(bf16[256,4096]{1,0:T(8,128)(2,1)} %param.14) | copy-start | bytes 6291460
  6.5 2.0 copy-start.3
  8.6 0.9 copy-start.6
  9.5 0.9 copy-start.7
  10.4 0.8 copy-start.8
  20.7 1.0 copy-start.2
  21.7 7.8 %copy-start.9 = (bf16[4096]{0:T(1024)(128)(2,1)S(1)}, bf16[4096]{0:T(1024)(128)(2,1)}, u32[]{:S(2)}) copy-start(bf16[4096]{0:T(1024)(128)(2,1)} %param.12) | copy-start | bytes 24580
  21.7 23.6 %all-to-all-start = ((bf16[16,8,4352]{2,1,0:T(8,128)(2,1)}), bf16[16,8,4352]{2,1,0:T(8,128)(2,1)S(1)}, u32[]{:S(2)}, u32[]{:S(2)}) async-start(bf16[16,8,4352]{2,1,0:T(8,128)(2,1)} %bitcast.30), calls=%async_computation | async-start | bytes 2228224 | tf_op jit(solution)/shard_map/all_to_all | solution.py:287
  28.7 99.4 %all-gather.3.cloned.1.call-start = ((), (), s32[]{:S(2)}) async-start(), calls=%async_computation.6 | async-start | bytes 2228224 | tf_op jit(solution)/shard_map/all_gather | solution.py:297
  60.3 3.6 %collective-permute-start = (bf16[64,4096]{1,0:T(8,128)(2,1)S(1)}, bf16[64,4096]{1,0:T(8,128)(2,1)S(1)}, u32[]{:S(2)}, u32[]{:S(2)}) collective-permute-start(bf16[64,4096]{1,0:T(8,128)(2,1)S(1)} %bitcast.33), channel_id=1, source_target_pairs={{0,16},{16,0},{1,17},{17,1},{2,18},{18,2},{3,19},{19,3},{4,20},{20... | collective-permute-start | bytes 1572872 | tf_op jit(solution)/shard_map/ppermute | solution.py:283
  63.8 2.9 %copy-start.1 = (bf16[4096,3,256]{2,0,1:T(8,128)(2,1)S(1)}, bf16[4096,3,256]{2,0,1:T(8,128)(2,1)}, u32[]{:S(2)}) copy-start(bf16[4096,3,256]{2,0,1:T(8,128)(2,1)} %param.13) | copy-start | bytes 18874372
  68.9 1.0 copy-start.5
  69.8 38.0 %all-to-all-start.2 = ((bf16[16,128,256]{2,1,0:T(8,128)(2,1)}), bf16[16,128,256]{2,1,0:T(8,128)(2,1)S(1)}, u32[]{:S(2)}, u32[]{:S(2)}) async-start(bf16[16,128,256]{2,1,0:T(8,128)(2,1)} %bitcast.35), calls=%async_computation.2 | async-start | bytes 2097152 | tf_op jit(solution)/shard_map/all_to_all | solution.py:287
  80.9 24.9 %collective-permute-start.1 = (bf16[128,128]{1,0:T(8,128)(2,1)S(1)}, bf16[128,128]{1,0:T(8,128)(2,1)S(1)}, u32[]{:S(2)}, u32[]{:S(2)}) collective-permute-start(bf16[128,128]{1,0:T(8,128)(2,1)S(1)} %get-tuple-element.12), channel_id=1, source_target_pairs={{0,1},{1,0},{2,3},{3,2},{4,5},{5,4},{6,7},{7,6},{8,9},{9,8},{10,11... | collective-permute-start | bytes 98312 | tf_op jit(solution)/shard_map/ppermute | solution.py:283
  110.4 12.7 %all-to-all-start.3 = ((bf16[16,16,128]{2,1,0:T(8,128)(2,1)}), bf16[16,16,128]{2,1,0:T(8,128)(2,1)S(1)}, u32[]{:S(2)}, u32[]{:S(2)}) async-start(bf16[16,16,128]{2,1,0:T(8,128)(2,1)} %bitcast.11), calls=%async_computation.3 | async-start | bytes 131072 | tf_op jit(solution)/shard_map/all_to_all | solution.py:287
  117.2 84.0 %all-gather.5.cloned.1.call-start = ((), (), s32[]{:S(2)}) async-start(), calls=%async_computation.7 | async-start | bytes 1671168 | tf_op jit(solution)/shard_map/all_gather | solution.py:298
  124.3 34.1 %all-to-all-start.4 = ((bf16[16,272,128]{2,1,0:T(8,128)(2,1)}), bf16[16,272,128]{2,1,0:T(8,128)(2,1)S(1)}, u32[]{:S(2)}, u32[]{:S(2)}) async-start(bf16[16,272,128]{2,1,0:T(8,128)(2,1)} %pad_maximum_fusion), calls=%async_computation.4 | async-start | bytes 2228224 | tf_op jit(solution)/shard_map/all_to_all | solution.py:287
  158.4 1.6 copy-start.4
  171.2 32.1 %collective-permute-start.2 = (bf16[1024,256]{1,0:T(8,128)(2,1)S(1)}, bf16[1024,256]{1,0:T(8,128)(2,1)S(1)}, u32[]{:S(2)}, u32[]{:S(2)}) collective-permute-start(bf16[1024,256]{1,0:T(8,128)(2,1)S(1)} %bitcast.42), channel_id=1, source_target_pairs={{0,16},{16,0},{1,17},{17,1},{2,18},{18,2},{3,19},{19,3},{4,20},{20... | collective-permute-start | bytes 1572872 | tf_op jit(solution)/shard_map/ppermute | solution.py:283
Sparse Core Ops, SparseCore 0:
  31.4 42.2 all-gather.2
  120.6 80.5 all-gather.4

commit v2 on v1

v2 whole, which is shorter than its diff:
```python
import math

import jax
import jax.numpy as jnp
from jax import lax
from jax.experimental import pallas as pl
from jax.experimental.pallas import tpu as pltpu
from jax.sharding import Mesh, PartitionSpec as P

EPS = 1e-05
HD = 128
F32 = jnp.float32
BF16 = jnp.bfloat16
VAR = ("y", "xl", "c")
CHIPS = ("y", "xl")
SEQ = ("xh", "z")
NT = (((1,), (1,)), ((), ()))
TN = (((0,), (0,)), ((), ()))
NN = (((1,), (0,)), ((), ()))
MB = 1024 * 1024


def dot(a, b, dims):
    return lax.dot_general(a, b, dims, preferred_element_type=F32)


def params(megabytes):
    return pltpu.CompilerParams(vmem_limit_bytes=megabytes * MB)


def in_three(x):
    high = x.astype(BF16).astype(F32)
    rest = x - high
    middle = rest.astype(BF16).astype(F32)
    return high, middle, rest - middle


def embed_kernel(place_ref, pixels_ref, weight_ref, shift_ref, query_ref, keep_ref, send_ref, embedded, scores):
    member = pl.program_id(0)
    core = place_ref[0]
    count = embedded.shape[0]
    width = weight_ref.shape[2]
    heads = query_ref.shape[0]
    rows = pixels_ref.shape[2]
    chosen = lax.broadcasted_iota(jnp.int32, shift_ref.shape, 0) == member
    shift = jnp.sum(jnp.where(chosen, shift_ref[...].astype(F32), 0.0), axis=0, keepdims=True)
    step = 1024
    total = jnp.zeros((rows, heads), F32)
    for at in range(0, width, step):
        block = dot(pixels_ref[0], weight_ref[0, :, at : at + step], TN)
        block = (block + shift[:, at : at + step]).astype(BF16)
        embedded[member, :, at : at + step] = block
        total = total + dot(block, query_ref[:, at : at + step], NT)
    scores[member] = total / math.sqrt(HD)

    def split(value, cols):
        for at in range(0, rows, 16):
            even, odd = value[at : at + 8], value[at + 8 : at + 16]
            to = at // 2
            keep_ref[to : to + 8, cols] = jnp.where(core == 0, even, odd)
            send_ref[to : to + 8, cols] = jnp.where(core == 0, odd, even)

    @pl.when(member == count - 1)
    def _():
        every = scores[...]
        peak = jnp.max(every, axis=0)
        weights = jnp.exp(every - peak[None])
        total = jnp.sum(weights, axis=0)
        for h in range(heads):
            cols = slice(h * HD, (h + 1) * HD)
            numer = weights[0][:, h : h + 1] * embedded[0, :, cols].astype(F32)
            for v in range(1, count):
                numer = numer + weights[v][:, h : h + 1] * embedded[v, :, cols].astype(F32)
            split(numer, cols)
        blank = jnp.zeros_like(peak)
        split(jnp.concatenate([peak, total, blank, blank], axis=1), slice(width, width + 128))


def embed(place, pixels, weight, shift, query):
    count, depth, rows = pixels.shape
    width = weight.shape[2]
    heads = query.shape[0]
    half = jax.ShapeDtypeStruct((rows // 2, width + 128), F32)
    return pl.pallas_call(
        embed_kernel,
        grid=(count,),
        in_specs=[
            pl.BlockSpec(memory_space=pltpu.SMEM),
            pl.BlockSpec((1, depth, rows), lambda v: (v, 0, 0)),
            pl.BlockSpec((1, depth, width), lambda v: (v, 0, 0)),
            pl.BlockSpec((count, width), lambda v: (0, 0)),
            pl.BlockSpec((heads, width), lambda v: (0, 0)),
        ],
        out_specs=[pl.BlockSpec((rows // 2, width + 128), lambda v: (0, 0))] * 2,
        out_shape=[half, half],
        scratch_shapes=[
            pltpu.VMEM((count, rows, width), BF16),
            pltpu.VMEM((count, rows, heads), F32),
        ],
        compiler_params=params(56),
        name="embed",
    )(place, pixels, weight, shift, query)


def pair_kernel(mine_ref, other_ref, out_ref):
    rows, padded = mine_ref.shape
    width = padded - 128
    heads = width // HD
    mine, other = mine_ref[:, width:], other_ref[:, width:]
    peak_a, total_a = mine[:, :32], mine[:, 32:64]
    peak_b, total_b = other[:, :32], other[:, 32:64]
    top = jnp.maximum(peak_a, peak_b)
    scale_a = jnp.exp(peak_a - top)
    scale_b = jnp.exp(peak_b - top)
    for h in range(heads):
        cols = slice(h * HD, (h + 1) * HD)
        numer = mine_ref[:, cols] * scale_a[:, h : h + 1] + other_ref[:, cols] * scale_b[:, h : h + 1]
        out_ref[:, cols] = numer.astype(BF16)
    p0, p1, p2 = in_three(top)
    t0, t1, t2 = in_three(total_a * scale_a + total_b * scale_b)
    blank = jnp.zeros_like(top)
    out_ref[:, width : width + 128] = jnp.concatenate([p0, p1, p2, t0], axis=1).astype(BF16)
    out_ref[:, width + 128 : width + 256] = jnp.concatenate(
        [t1, t2, blank, blank], axis=1
    ).astype(BF16)


def pair(mine, other):
    rows, padded = mine.shape
    return pl.pallas_call(
        pair_kernel,
        out_shape=jax.ShapeDtypeStruct((rows, padded + 128), BF16),
        compiler_params=params(12),
        name="pair",
    )(mine, other)


def merge_kernel(place_ref, parts_ref, gain_ref, normed_ref, keep_ref, send_ref, whole):
    x_hi = place_ref[1]
    rows, padded = parts_ref.shape
    width = padded - 256
    heads = width // HD
    share = 8
    sources = rows // share
    stats = parts_ref[:, width:].astype(F32)
    peak = stats[:, 0:32] + stats[:, 32:64] + stats[:, 64:96]
    total = stats[:, 96:128] + stats[:, 128:160] + stats[:, 160:192]
    peak = peak.reshape(sources, share, heads)
    total = total.reshape(sources, share, heads)
    top = jnp.max(peak, axis=0)
    scale = jnp.exp(peak - top[None])
    total = jnp.sum(total * scale, axis=0)
    scale = scale.reshape(rows, heads)
    sums = jnp.zeros((share, HD), F32)
    for h in range(heads):
        cols = slice(h * HD, (h + 1) * HD)
        numer = jnp.zeros((share, HD), F32)
        for at in range(0, rows, 16):
            block = parts_ref[at : at + 16, cols].astype(F32) * scale[at : at + 16, h : h + 1]
            numer = numer + block[:8] + block[8:]
        value = (numer / total[:, h : h + 1]).astype(BF16).astype(F32)
        whole[:, cols] = value
        sums = sums + value
    half = width // 2
    for at in range(0, half, 512):
        for side in range(2):
            low = slice(at + side * 128, at + side * 128 + 128)
            high = slice(at + side * 128 + 256, at + side * 128 + 384)
            first = jnp.concatenate([whole[:, low], whole[:, high]], axis=0)
            low = slice(half + at + side * 128, half + at + side * 128 + 128)
            high = slice(half + at + side * 128 + 256, half + at + side * 128 + 384)
            second = jnp.concatenate([whole[:, low], whole[:, high]], axis=0)
            to = at // 512 * 16
            cols = slice(side * 128, side * 128 + 128)
            keep_ref[to : to + 16, cols] = jnp.where(x_hi == 0, first, second).astype(BF16)
            send_ref[to : to + 16, cols] = jnp.where(x_hi == 0, second, first).astype(BF16)
    center = jnp.sum(sums, axis=1, keepdims=True) / width
    squares = jnp.zeros((share, HD), F32)
    for h in range(heads):
        shifted = whole[:, h * HD : (h + 1) * HD] - center
        squares = squares + shifted * shifted
    factor = lax.rsqrt(jnp.sum(squares, axis=1, keepdims=True) / width + EPS)
    for h in range(heads):
        cols = slice(h * HD, (h + 1) * HD)
        value = (whole[:, cols] - center) * factor * gain_ref[:, cols].astype(F32)
        twice = jnp.concatenate([value, value], axis=0).astype(BF16)
        for at in range(0, normed_ref.shape[0], 16):
            normed_ref[at : at + 16, cols] = twice


def merge(place, parts, gain, copies):
    rows, padded = parts.shape
    width = padded - 256
    vmem = pl.BlockSpec(memory_space=pltpu.VMEM)
    return pl.pallas_call(
        merge_kernel,
        in_specs=[pl.BlockSpec(memory_space=pltpu.SMEM), vmem, vmem],
        out_shape=(
            jax.ShapeDtypeStruct((copies * 8, width), BF16),
            jax.ShapeDtypeStruct((64, 256), BF16),
            jax.ShapeDtypeStruct((64, 256), BF16),
        ),
        scratch_shapes=[pltpu.VMEM((8, width), F32)],
        compiler_params=params(12),
        name="merge",
    )(place, parts, gain)


def qkv_kernel(place_ref, mine_ref, other_ref, weight_ref, keep_q, keep_kv, send_q, send_kv, tokens):
    step = pl.program_id(0)
    core = place_ref[0]
    x_hi = place_ref[1]
    half = mine_ref.shape[0]

    @pl.when(step == 0)
    def _():
        tokens[pl.ds(pl.multiple_of(core * half, half), half), :] = mine_ref[...]
        tokens[pl.ds(pl.multiple_of((1 - core) * half, half), half), :] = other_ref[...]

    made = dot(tokens[...], weight_ref[0], NN)
    first, second = made[:, :HD], made[:, HD:]
    keep = jnp.where(x_hi == 0, first, second).astype(BF16)
    send = jnp.where(x_hi == 0, second, first).astype(BF16)

    @pl.when(step == 0)
    def _():
        keep_q[...] = keep
        send_q[...] = send

    for part in (1, 2):

        @pl.when(step == part)
        def _():
            cols = slice((part - 1) * HD, part * HD)
            keep_kv[:, cols] = keep
            send_kv[:, cols] = send


def project(place, mine, other, weight):
    half, width = mine.shape
    cols = weight.shape[2]
    rows = 2 * half
    whole = lambda s: (0, 0)
    shapes = [(rows, HD), (rows, 2 * HD)] * 2
    return pl.pallas_call(
        qkv_kernel,
        grid=(3,),
        in_specs=[
            pl.BlockSpec(memory_space=pltpu.SMEM),
            pl.BlockSpec((half, width), whole),
            pl.BlockSpec((half, width), whole),
            pl.BlockSpec((1, width, cols), lambda s: (s, 0, 0)),
        ],
        out_specs=[pl.BlockSpec(shape, whole) for shape in shapes],
        out_shape=[jax.ShapeDtypeStruct(shape, BF16) for shape in shapes],
        scratch_shapes=[pltpu.VMEM((rows, width), BF16)],
        compiler_params=params(16),
        name="project",
    )(place, mine, other, weight)


def attend_kernel(place_ref, keep_ref, got_ref, band_ref, out_ref, kept_ref, scores):
    x_hi = place_ref[1]
    z = place_ref[2]
    bands = band_ref.shape[0]
    mixed = []
    for side in range(2):
        query = jnp.where(x_hi == side, keep_ref[...], got_ref[...])
        for band in range(bands):
            scores[:, band * 256 : band * 256 + 256] = dot(
                query, band_ref[band, :256, :HD], NT
            ) / math.sqrt(HD)
        every = scores[...]
        peak = jnp.max(every, axis=1, keepdims=True)
        weights = jnp.exp(every - peak)
        total = jnp.sum(weights, axis=1, keepdims=True)
        weights = weights.astype(BF16)
        update = jnp.zeros((query.shape[0], HD), F32)
        for band in range(bands):
            update = update + dot(
                weights[:, band * 256 : band * 256 + 256], band_ref[band, :256, HD:], NN
            )
        mixed.append(update / total)
    for chip in range(8):
        for core in range(2):
            at = core * 64 + chip * 8
            to = (chip * 2 + core) * 16
            out_ref[to : to + 16, :] = jnp.concatenate(
                [mixed[0][at : at + 8], mixed[1][at : at + 8]], axis=0
            ).astype(BF16)
    for band in range(bands):
        rows = band_ref[band, pl.ds(pl.multiple_of(256 + z * 16, 16), 16), :].astype(F32)
        mine, other = rows[:8], rows[8:]
        first = jnp.where(x_hi == 0, mine, other)
        second = jnp.where(x_hi == 0, other, mine)
        kept_ref[band * 16 : band * 16 + 16, :] = jnp.concatenate([first, second], axis=0).astype(BF16)


def attend(place, keep, got, bands):
    return pl.pallas_call(
        attend_kernel,
        in_specs=[pl.BlockSpec(memory_space=pltpu.SMEM)] + [pl.BlockSpec(memory_space=pltpu.VMEM)] * 3,
        out_shape=(
            jax.ShapeDtypeStruct((256, HD), BF16),
            jax.ShapeDtypeStruct((128, 256), BF16),
        ),
        scratch_shapes=[pltpu.VMEM((128, 2048), F32)],
        compiler_params=params(16),
        name="attend",
    )(place, keep, got, bands)


def output_kernel(place_ref, parts_ref, kept_ref, mine_ref, other_ref, out_ref, attended):
    core = place_ref[0]
    x_hi = place_ref[1]
    bands = parts_ref.shape[0]
    half = mine_ref.shape[0]
    for side in range(2):
        owner = core if side == 0 else 1 - core
        for chip in range(8):
            for parity in range(2):
                place = jnp.where(x_hi == parity, 0, 256) + (2 * chip + owner) * 16
                place = pl.multiple_of(place, 16)
                to = side * half + chip * 256 + parity * HD
                for band in range(bands):
                    attended[band * 16 : band * 16 + 16, to : to + HD] = parts_ref[
                        band, pl.ds(place, 16), :
                    ]
    product = dot(attended[:, :half], mine_ref[...], NN) + dot(attended[:, half:], other_ref[...], NN)
    layer = (kept_ref[...].astype(F32) + product).astype(BF16)
    rows = layer.shape[0]
    for copy in range(out_ref.shape[0] // rows):
        out_ref[copy * rows : (copy + 1) * rows, :] = layer


def output(place, parts, kept, mine, other, copies):
    half, cols = mine.shape
    rows = kept.shape[0]
    return pl.pallas_call(
        output_kernel,
        in_specs=[pl.BlockSpec(memory_space=pltpu.SMEM)] + [pl.BlockSpec(memory_space=pltpu.VMEM)] * 4,
        out_shape=jax.ShapeDtypeStruct((copies * rows, cols), BF16),
        scratch_shapes=[pltpu.VMEM((rows, 2 * half), BF16)],
        compiler_params=params(12),
        name="output",
    )(place, parts, kept, mine, other)


def swap(x, axis, pieces=1):
    rows = x.shape[0] // pieces
    parts = [
        lax.ppermute(x[k * rows : (k + 1) * rows], axis, [(0, 1), (1, 0)]) for k in range(pieces)
    ]
    return parts[0] if pieces == 1 else jnp.concatenate(parts, axis=0)


def exchange(x, axes):
    return lax.all_to_all(x, axes, 0, 0, tiled=True)


def body(patches, patch_weight, var_embed, agg_query, norm_gain, qkv_weight, out_weight, head_cot):
    core, x_hi, z = lax.axis_index("c"), lax.axis_index("xh"), lax.axis_index("z")
    place = jnp.stack([core, x_hi, z]).astype(jnp.int32)
    width = out_weight.shape[1]

    cot = lax.all_gather(head_cot, "z", axis=0, tiled=True)
    cols = lax.dynamic_slice_in_dim(out_weight, (x_hi * 8 + z) * 256, 256, 1)
    cols = lax.all_gather(cols, CHIPS, axis=0, tiled=True)
    other_cols = swap(cols, "c", 2)
    other_cot = swap(cot, "xh", 4)
    both = jnp.stack([jnp.where(x_hi == 0, cot, other_cot), jnp.where(x_hi == 0, other_cot, cot)])
    both = both.reshape(2, 8, 8, 2, 8, 384).transpose(3, 2, 1, 0, 4, 5).reshape(2, 1024, 384)
    first = lax.dynamic_index_in_dim(both, core, 0, keepdims=False)
    second = lax.dynamic_index_in_dim(both, 1 - core, 0, keepdims=False)

    keep, send = embed(place, patches.transpose(0, 2, 1), patch_weight, var_embed, agg_query.T)
    parts = pair(keep, swap(send, "c"))
    parts = exchange(parts, CHIPS)
    normed, kept, kept_send = merge(place, parts, norm_gain.reshape(1, width), 8)
    kept_got = swap(kept_send, "xh")
    normed = exchange(normed, CHIPS)
    query, kv, query_send, kv_send = project(
        place, normed, swap(normed, "c"), qkv_weight.transpose(1, 0, 2)
    )
    kv_got = swap(kv_send, "xh")
    query_got = swap(query_send, "xh")
    residual = jnp.stack([kept.reshape(8, 8, 256), kept_got.reshape(8, 8, 256)], axis=1)
    block = jnp.concatenate([kv, kv_got, residual.reshape(128, 256)], axis=0)
    bands = lax.all_gather(block, "z", axis=0, tiled=False)
    attended, kept = attend(place, query, query_got, bands)
    attended = exchange(attended, VAR)
    attended = jnp.concatenate([attended, swap(attended, "xh", 2)], axis=0)
    attended = lax.all_gather(attended, "z", axis=0, tiled=False)
    layer = output(place, attended, kept, cols, other_cols, 8)
    layer = exchange(layer, CHIPS)
    return dot(layer, first, TN) + dot(swap(layer, "c"), second, TN)


def solution(mesh):
    whole = Mesh(mesh.devices.reshape(4, 2, 2, 2, 8), ("y", "xl", "c", "xh", "z"))
    return jax.shard_map(
        body,
        mesh=whole,
        in_specs=(
            P(VAR, SEQ, None),
            P(VAR, None, None),
            P(VAR, None),
            P(),
            P(),
            P(None, None, VAR),
            P(VAR, None),
            P(SEQ, VAR),
        ),
        out_specs=P(SEQ, VAR),
        check_vma=False,
    )
```

time: 215 us -> 225 us (1.047); the launches traced: 211 us -> 224 us
  waiting for transfers between devices: 104 us -> 72.4 us
  blocking collectives: 24.4 us -> 50.5 us
  local copies, waits for them, and re-layouts: 13.7 us -> 20.2 us
  Pallas kernels: 15.8 us -> 20.8 us
  other arithmetic: 1.14 us -> 5.68 us
  starting transfers between devices: 37.1 us -> 39.9 us
    all_to_all x4 -> x2, waiting for transfers between devices: 53.3 us -> 10.6 us  [exchange(): return lax.all_to_all(x, axes, 0, 0, tiled=True)]
    all_gather x2 -> x3, waiting for transfers between devices: 25 us -> 49.1 us  [the longest x1 31.6 us: body(): bands = lax.all_gather(block, 'z', axis=0, tiled=False)]
    ppermute x3 -> x14, starting transfers between devices: 8.31 us -> 31.3 us  [swap(): lax.ppermute(x[k * rows:(k + 1) * rows], axis, [(0, 1), (1, 0)])]
    all_gather x0 -> x1, blocking collectives: none -> 22.6 us  [body(): cot = lax.all_gather(head_cot, 'z', axis=0, tiled=True)]
    all_to_all x4 -> x2, starting transfers between devices: 28.7 us -> 8.44 us  [exchange(): return lax.all_to_all(x, axes, 0, 0, tiled=True)]
    ppermute x3 -> x14, waiting for transfers between devices: 25 us -> 12.7 us  [swap(): lax.ppermute(x[k * rows:(k + 1) * rows], axis, [(0, 1), (1, 0)])]
    pallas_call x3 -> x4, Pallas kernels: 11.1 us -> 16.9 us  [the longest x1 12.8 us: embed(): pl.pallas_call(embed_kernel, grid=(count,), in_specs=[pl.BlockSpec(memory...]
    all_to_all x2, blocking collectives: 24.4 us -> 27.9 us  [exchange(): return lax.all_to_all(x, axes, 0, 0, tiled=True)]
  transfers between devices with their start and end apart: 9 -> 19, of which waited for: 7 -> 10; matrix products, arithmetic and copies ran while one was open for 2% -> 7% of each run, Pallas kernels for 3% -> 2%
where the time goes in v2:
time: 225 us; the launch traced here: 224 us
  waiting for transfers between devices  72.4 us (32%)
  blocking collectives  50.5 us (22%)
  starting transfers between devices  39.9 us (18%)
  Pallas kernels  20.8 us (9%)
  local copies, waits for them, and re-layouts  20.2 us (9%)
  between operations  13.3 us (6%)
  other arithmetic  5.68 us (3%)
    all_gather x1, waiting for transfers between devices, body(): bands = lax.all_gather(block, 'z', axis=0, tiled=False)  31.6 us
    ppermute x14, starting transfers between devices, swap(): lax.ppermute(x[k * rows:(k + 1) * rows], axis, [(0, 1), (1, 0)])  31.3 us
    all_to_all x2, blocking collectives, exchange(): return lax.all_to_all(x, axes, 0, 0, tiled=True)  27.9 us
    all_gather x1, blocking collectives, body(): cot = lax.all_gather(head_cot, 'z', axis=0, tiled=True)  22.6 us
    all_gather x1, waiting for transfers between devices, body(): cols = lax.all_gather(cols, CHIPS, axis=0, tiled=True)  16.8 us
    unnamed x29, local copies, waits for them, and re-layouts  14.5 us
    pallas_call x1, Pallas kernels, embed(): pl.pallas_call(embed_kernel, grid=(count,), in_specs=[pl.BlockSpec(memory...  12.8 us
    ppermute x14, waiting for transfers between devices, swap(): lax.ppermute(x[k * rows:(k + 1) * rows], axis, [(0, 1), (1, 0)])  12.7 us
  transfers between devices with their start and end apart: 19, of which 10 were waited for; matrix products, arithmetic and copies ran while one was open for 7% of the time, Pallas kernels for 2%

profile of v2, /device:TPU:1, one launch (start us, length us, event | category | flops | bytes accessed | tf_op | source)
XLA Modules:
  0.0 224.5 jit_solution(2456275482509335927)
XLA Ops:
  7.1 12.8 %embed.1 = (f32[64,4224]{1,0:T(8,128)}, f32[64,4224]{1,0:T(8,128)}) custom-call(s32[3]{0:T(128)} %pad_add_fusion.place_ref, bf16[6,64,128]{2,1,0:T(8,128)(2,1)} %bitcast.57, bf16[6,64,4096]{2,1,0:T(8,128)(2,1)} %weight_ref.1, bf16[6,4096]{1,0:T(8,128)(2,1)} %shift_ref.1, bf16[32,4096]{1,0:T(8,128)(2,1)} %bitcast.56), custom_call_target="tpu_custom_call" | custom-call | tf_op jit(solution)/shard_map/embed/pallas_call | solution.py:84
  20.0 3.2 %collective-permute-start = (f32[64,4224]{1,0:T(8,128)}, f32[64,4224]{1,0:T(8,128)S(1)}, u32[]{:S(2)}, u32[]{:S(2)}) collective-permute-start(f32[64,4224]{1,0:T(8,128)} %get-tuple-element.17), channel_id=1, source_target_pairs={{0,16},{16,0},{1,17},{17,1},{2,18},{18,2},{3,19},{19,3},{4,20},{20... | collective-permute-start | bytes 3244040 | tf_op jit(solution)/shard_map/ppermute | solution.py:352
  23.2 2.5 %collective-permute-done.other_ref = f32[64,4224]{1,0:T(8,128)S(1)} collective-permute-done((f32[64,4224]{1,0:T(8,128)}, f32[64,4224]{1,0:T(8,128)S(1)}, u32[]{:S(2)}, u32[]{:S(2)}) %collective-permute-start) | collective-permute-done | bytes 1081376 | tf_op jit(solution)/shard_map/ppermute | solution.py:352
  25.8 1.2 copy-done.6
  27.0 1.6 pair.1
  28.6 3.5 %all-to-all-start = ((bf16[8,8,4352]{2,1,0:T(8,128)(2,1)}), bf16[8,8,4352]{2,1,0:T(8,128)(2,1)S(1)}, u32[]{:S(2)}, u32[]{:S(2)}) async-start(bf16[8,8,4352]{2,1,0:T(8,128)(2,1)} %bitcast.5), calls=%async_computation | async-start | bytes 1114112 | tf_op jit(solution)/shard_map/all_to_all | solution.py:358
  32.2 9.5 %all-to-all-done = bf16[8,8,4352]{2,1,0:T(8,128)(2,1)S(1)} async-done(((bf16[8,8,4352]{2,1,0:T(8,128)(2,1)}), bf16[8,8,4352]{2,1,0:T(8,128)(2,1)S(1)}, u32[]{:S(2)}, u32[]{:S(2)}) %all-to-all-start) | async-done | bytes 557088 | tf_op jit(solution)/shard_map/all_to_all | solution.py:358
  41.7 1.4 merge.1
  43.1 12.4 %all_to_all.46 = bf16[8,8,4096]{2,1,0:T(8,128)(2,1)S(1)} all-to-all(bf16[8,8,4096]{2,1,0:T(8,128)(2,1)S(1)} %bitcast.45), channel_id=1, replica_groups=mesh['y'=4,'xl'=2,'c'=2,'xh'=2,'z'=8] {'y','xl'}, dimensions={0} | all-to-all | bytes 1048576 | tf_op jit(solution)/shard_map/all_to_all | solution.py:358
  55.5 1.9 collective-permute-start.1
  57.4 2.3 %collective-permute-start.4 = (bf16[64,256]{1,0:T(8,128)(2,1)S(1)}, bf16[64,256]{1,0:T(8,128)(2,1)S(1)}, u32[]{:S(2)}, u32[]{:S(2)}) collective-permute-start(bf16[64,256]{1,0:T(8,128)(2,1)S(1)} %get-tuple-element.24), channel_id=1, source_target_pairs={{0,8},{8,0},{1,9},{9,1},{2,10},{10,2},{3,11},{11,3},{4,12},{12,4},... | collective-permute-start | bytes 98312 | tf_op jit(solution)/shard_map/ppermute | solution.py:352
  59.7 2.8 %copy-done.1 = bf16[4096,3,256]{2,0,1:T(8,128)(2,1)S(1)} copy-done((bf16[4096,3,256]{2,0,1:T(8,128)(2,1)S(1)}, bf16[4096,3,256]{2,0,1:T(8,128)(2,1)}, u32[]{:S(2)}) %copy-start.1) | copy-done | bytes 6291480
  62.5 2.0 project.1
  64.6 1.6 collective-permute-start.3
  66.2 3.1 %collective-permute-done.3 = bf16[128,256]{1,0:T(8,128)(2,1)S(1)} collective-permute-done((bf16[128,256]{1,0:T(8,128)(2,1)S(1)}, bf16[128,256]{1,0:T(8,128)(2,1)S(1)}, u32[]{:S(2)}, u32[]{:S(2)}) %collective-permute-start.3) | collective-permute-done | bytes 65568 | tf_op jit(solution)/shard_map/ppermute | solution.py:352
  70.8 1.6 collective-permute-start.2
  72.4 2.7 %collective-permute-done.2.got_ref = bf16[128,128]{1,0:T(8,128)(2,1)S(1)} collective-permute-done((bf16[128,128]{1,0:T(8,128)(2,1)S(1)}, bf16[128,128]{1,0:T(8,128)(2,1)S(1)}, u32[]{:S(2)}, u32[]{:S(2)}) %collective-permute-start.2) | collective-permute-done | bytes 32800 | tf_op jit(solution)/shard_map/ppermute | solution.py:352
  75.2 31.6 %all-gather.8.cloned.1.call-done = bf16[3072,256]{1,0:T(8,128)(2,1)} async-done(((bf16[384,256]{1,0:T(8,128)(2,1)}), bf16[3072,256]{1,0:T(8,128)(2,1)}) %all-gather.8.cloned.1.call-update) | async-done | bytes 1572880 | tf_op jit(solution)/shard_map/all_gather | solution.py:389
  106.8 1.4 copy-done.5
  108.2 1.8 attend.1
  110.1 15.4 %all_to_all.47 = bf16[16,16,128]{2,1,0:T(8,128)(2,1)S(1)} all-to-all(bf16[16,16,128]{2,1,0:T(8,128)(2,1)S(1)} %bitcast.46), channel_id=1, replica_groups=mesh['y'=4,'xl'=2,'c'=2,'xh'=2,'z'=8] {'y','xl','c'}, dimensions={0} | all-to-all | bytes 131072 | tf_op jit(solution)/shard_map/all_to_all | solution.py:358
  125.5 2.4 %collective-permute-start.5 = (bf16[128,128]{1,0:T(8,128)(2,1)S(1)}, bf16[128,128]{1,0:T(8,128)(2,1)S(1)}, u32[]{:S(2)}, u32[]{:S(2)}) collective-permute-start(bf16[128,128]{1,0:T(8,128)(2,1)S(1)} %bitcast.60), channel_id=1, source_target_pairs={{0,8},{8,0},{1,9},{9,1},{2,10},{10,2},{3,11},{11,3},{4,12},{12,4},... | collective-permute-start | bytes 98312 | tf_op jit(solution)/shard_map/ppermute | solution.py:352
  128.5 1.7 collective-permute-done.5
  130.2 2.7 %collective-permute-done.6 = bf16[128,128]{1,0:T(8,128)(2,1)S(1)} collective-permute-done((bf16[128,128]{1,0:T(8,128)(2,1)S(1)}, bf16[128,128]{1,0:T(8,128)(2,1)S(1)}, u32[]{:S(2)}, u32[]{:S(2)}) %collective-permute-start.6) | collective-permute-done | bytes 32800 | tf_op jit(solution)/shard_map/ppermute | solution.py:352
  133.5 16.8 %all-gather.6.cloned.1.call-done.mine_ref = bf16[2048,256]{1,0:T(8,128)(2,1)} async-done(((bf16[256,256]{1,0:T(8,128)(2,1)}), bf16[2048,256]{1,0:T(8,128)(2,1)}) %all-gather.6.cloned.1.call-update) | async-done | bytes 1048592 | tf_op jit(solution)/shard_map/all_gather | solution.py:368
  150.3 2.3 %fusion.7 = (bf16[1024,256]{1,0:T(8,128)(2,1)}, bf16[1024,256]{1,0:T(8,128)(2,1)}) fusion(bf16[2048,256]{1,0:T(8,128)(2,1)} %all-gather.6.cloned.1.call-done.mine_ref), kind=kLoop, calls=%fused_computation.21 | loop fusion | bytes 2097152 | tf_op jit(solution)/shard_map/slice | solution.py:352
  152.6 5.2 %collective-permute-start.7 = (bf16[1024,256]{1,0:T(8,128)(2,1)}, bf16[1024,256]{1,0:T(8,128)(2,1)}, u32[]{:S(2)}, u32[]{:S(2)}) collective-permute-start(bf16[1024,256]{1,0:T(8,128)(2,1)} %get-tuple-element.29), channel_id=1, source_target_pairs={{0,16},{16,0},{1,17},{17,1},{2,18},{18,2},{3,19},{19,3},{4,20},{20... | collective-permute-start | bytes 1572872 | tf_op jit(solution)/shard_map/ppermute | solution.py:352
  157.8 22.6 %all_gather.23 = bf16[1024,384]{1,0:T(8,128)(2,1)S(1)} all-gather(bf16[128,384]{1,0:T(8,128)(2,1)S(1)} %copy-done.11), channel_id=1, replica_groups=mesh['y'=4,'xl'=2,'c'=2,'xh'=2,'z'=8] {'z'}, dimensions={0}, use_global_device_ids=true | all-gather | bytes 884736 | tf_op jit(solution)/shard_map/all_gather | solution.py:366
  180.4 0.9 copy-done.9
  181.3 0.9 fusion.8
  182.2 1.8 collective-permute-start.9
  184.0 1.2 collective-permute-start.10
  185.2 1.8 collective-permute-start.11
  187.0 1.2 collective-permute-start.12
  188.2 2.3 %pad_maximum_fusion.other_ref = bf16[2048,256]{1,0:T(8,128)(2,1)} fusion(bf16[1024,256]{1,0:T(8,128)(2,1)} %collective-permute-done.8, bf16[1024,256]{1,0:T(8,128)(2,1)} %collective-permute-done.7), kind=kLoop, calls=%fused_computation.2 | loop fusion | flops 2097152 | bytes 2097152 | tf_op jit(solution)/shard_map/concatenate | solution.py:354
  191.1 1.2 copy-done.3
  192.3 1.2 copy-done.7
  193.5 1.1 output.1
  194.7 0.8 copy-done.4
  195.5 4.9 %all-to-all-start.3 = ((bf16[8,128,256]{2,1,0:T(8,128)(2,1)}), bf16[8,128,256]{2,1,0:T(8,128)(2,1)S(1)}, u32[]{:S(2)}, u32[]{:S(2)}) async-start(bf16[8,128,256]{2,1,0:T(8,128)(2,1)} %bitcast.40), calls=%async_computation.3 | async-start | bytes 1048576 | tf_op jit(solution)/shard_map/all_to_all | solution.py:358
  200.4 1.6 constant_dynamic-update-slice_fusion.3
  202.0 1.6 constant_dynamic-update-slice_fusion.2
  203.7 1.6 constant_dynamic-update-slice_fusion.1
  205.3 1.6 constant_dynamic-update-slice_fusion
  206.9 1.0 all-to-all-done.3
  207.9 6.6 %collective-permute-start.13 = (bf16[1024,256]{1,0:T(8,128)(2,1)S(1)}, bf16[1024,256]{1,0:T(8,128)(2,1)S(1)}, u32[]{:S(2)}, u32[]{:S(2)}) collective-permute-start(bf16[1024,256]{1,0:T(8,128)(2,1)S(1)} %bitcast.52), channel_id=1, source_target_pairs={{0,16},{16,0},{1,17},{17,1},{2,18},{18,2},{3,19},{19,3},{4,20},{20... | collective-permute-start | bytes 1572872 | tf_op jit(solution)/shard_map/ppermute | solution.py:352
  214.5 1.3 broadcast_select_fusion.1
  216.7 1.2 convolution_add_fusion
  (47 shorter events, 5.0 us)
Async XLA Ops:
  6.5 63.5 %copy-start = (bf16[256,4096]{1,0:T(8,128)(2,1)S(1)}, bf16[256,4096]{1,0:T(8,128)(2,1)}, u32[]{:S(2)}) copy-start(bf16[256,4096]{1,0:T(8,128)(2,1)} %param.14) | copy-start | bytes 6291460
  20.0 5.8 %collective-permute-start = (f32[64,4224]{1,0:T(8,128)}, f32[64,4224]{1,0:T(8,128)S(1)}, u32[]{:S(2)}, u32[]{:S(2)}) collective-permute-start(f32[64,4224]{1,0:T(8,128)} %get-tuple-element.17), channel_id=1, source_target_pairs={{0,16},{16,0},{1,17},{17,1},{2,18},{18,2},{3,19},{19,3},{4,20},{20... | collective-permute-start | bytes 3244040 | tf_op jit(solution)/shard_map/ppermute | solution.py:352
  25.8 1.2 copy-start.6
  27.0 5.2 %copy-start.12 = (bf16[4096]{0:T(1024)(128)(2,1)S(1)}, bf16[4096]{0:T(1024)(128)(2,1)}, u32[]{:S(2)}) copy-start(bf16[4096]{0:T(1024)(128)(2,1)} %param.12) | copy-start | bytes 24580
  27.0 14.7 %copy-start.8 = (s32[3]{0:T(128)S(1)}, s32[3]{0:T(128)}, u32[]{:S(2)}) copy-start(s32[3]{0:T(128)} %pad_add_fusion.place_ref) | copy-start | bytes 40
  28.6 13.2 %all-to-all-start = ((bf16[8,8,4352]{2,1,0:T(8,128)(2,1)}), bf16[8,8,4352]{2,1,0:T(8,128)(2,1)S(1)}, u32[]{:S(2)}, u32[]{:S(2)}) async-start(bf16[8,8,4352]{2,1,0:T(8,128)(2,1)} %bitcast.5), calls=%async_computation | async-start | bytes 1114112 | tf_op jit(solution)/shard_map/all_to_all | solution.py:358
  32.1 74.7 %all-gather.8.cloned.1.call-start = ((), (), s32[]{:S(2)}) async-start(), calls=%async_computation.5 | async-start | bytes 1769472 | tf_op jit(solution)/shard_map/all_gather | solution.py:389
  55.5 4.2 %collective-permute-start.1 = (bf16[64,4096]{1,0:T(8,128)(2,1)S(1)}, bf16[64,4096]{1,0:T(8,128)(2,1)S(1)}, u32[]{:S(2)}, u32[]{:S(2)}) collective-permute-start(bf16[64,4096]{1,0:T(8,128)(2,1)S(1)} %bitcast.41), channel_id=1, source_target_pairs={{0,16},{16,0},{1,17},{17,1},{2,18},{18,2},{3,19},{19,3},{4,20},{20... | collective-permute-start | bytes 1572872 | tf_op jit(solution)/shard_map/ppermute | solution.py:352
  57.4 8.8 %collective-permute-start.4 = (bf16[64,256]{1,0:T(8,128)(2,1)S(1)}, bf16[64,256]{1,0:T(8,128)(2,1)S(1)}, u32[]{:S(2)}, u32[]{:S(2)}) collective-permute-start(bf16[64,256]{1,0:T(8,128)(2,1)S(1)} %get-tuple-element.24), channel_id=1, source_target_pairs={{0,8},{8,0},{1,9},{9,1},{2,10},{10,2},{3,11},{11,3},{4,12},{12,4},... | collective-permute-start | bytes 98312 | tf_op jit(solution)/shard_map/ppermute | solution.py:352
  59.7 2.8 %copy-start.1 = (bf16[4096,3,256]{2,0,1:T(8,128)(2,1)S(1)}, bf16[4096,3,256]{2,0,1:T(8,128)(2,1)}, u32[]{:S(2)}) copy-start(bf16[4096,3,256]{2,0,1:T(8,128)(2,1)} %param.13) | copy-start | bytes 18874372
  64.6 4.7 %collective-permute-start.3 = (bf16[128,256]{1,0:T(8,128)(2,1)S(1)}, bf16[128,256]{1,0:T(8,128)(2,1)S(1)}, u32[]{:S(2)}, u32[]{:S(2)}) collective-permute-start(bf16[128,256]{1,0:T(8,128)(2,1)S(1)} %get-tuple-element.22), channel_id=1, source_target_pairs={{0,8},{8,0},{1,9},{9,1},{2,10},{10,2},{3,11},{11,3},{4,12},{12,4},... | collective-permute-start | bytes 196616 | tf_op jit(solution)/shard_map/ppermute | solution.py:352
  70.0 80.4 %all-gather.6.cloned.1.call-start = ((), (), s32[]{:S(2)}) async-start(), calls=%async_computation.4 | async-start | bytes 1179648 | tf_op jit(solution)/shard_map/all_gather | solution.py:368
  70.8 120.3 %all-gather.10.cloned.1.call-start = ((), (), s32[]{:S(2)}) async-start(), calls=%async_computation.6 | async-start | bytes 1179648 | tf_op jit(solution)/shard_map/all_gather | solution.py:393
  70.8 4.4 %collective-permute-start.2 = (bf16[128,128]{1,0:T(8,128)(2,1)S(1)}, bf16[128,128]{1,0:T(8,128)(2,1)S(1)}, u32[]{:S(2)}, u32[]{:S(2)}) collective-permute-start(bf16[128,128]{1,0:T(8,128)(2,1)S(1)} %get-tuple-element.20), channel_id=1, source_target_pairs={{0,8},{8,0},{1,9},{9,1},{2,10},{10,2},{3,11},{11,3},{4,12},{12,4},... | collective-permute-start | bytes 98312 | tf_op jit(solution)/shard_map/ppermute | solution.py:352
  106.8 1.4 copy-start.5
  110.1 47.8 %copy-start.11 = (bf16[128,384]{1,0:T(8,128)(2,1)S(1)}, bf16[128,384]{1,0:T(8,128)(2,1)}, u32[]{:S(2)}) copy-start(bf16[128,384]{1,0:T(8,128)(2,1)} %param.15) | copy-start | bytes 294916
  125.5 4.7 %collective-permute-start.5 = (bf16[128,128]{1,0:T(8,128)(2,1)S(1)}, bf16[128,128]{1,0:T(8,128)(2,1)S(1)}, u32[]{:S(2)}, u32[]{:S(2)}) collective-permute-start(bf16[128,128]{1,0:T(8,128)(2,1)S(1)} %bitcast.60), channel_id=1, source_target_pairs={{0,8},{8,0},{1,9},{9,1},{2,10},{10,2},{3,11},{11,3},{4,12},{12,4},... | collective-permute-start | bytes 98312 | tf_op jit(solution)/shard_map/ppermute | solution.py:352
  127.9 4.9 %collective-permute-start.6 = (bf16[128,128]{1,0:T(8,128)(2,1)S(1)}, bf16[128,128]{1,0:T(8,128)(2,1)S(1)}, u32[]{:S(2)}, u32[]{:S(2)}) collective-permute-start(bf16[128,128]{1,0:T(8,128)(2,1)S(1)} %bitcast.59), channel_id=1, source_target_pairs={{0,8},{8,0},{1,9},{9,1},{2,10},{10,2},{3,11},{11,3},{4,12},{12,4},... | collective-permute-start | bytes 98312 | tf_op jit(solution)/shard_map/ppermute | solution.py:352
  152.6 34.3 %collective-permute-start.7 = (bf16[1024,256]{1,0:T(8,128)(2,1)}, bf16[1024,256]{1,0:T(8,128)(2,1)}, u32[]{:S(2)}, u32[]{:S(2)}) collective-permute-start(bf16[1024,256]{1,0:T(8,128)(2,1)} %get-tuple-element.29), channel_id=1, source_target_pairs={{0,16},{16,0},{1,17},{17,1},{2,18},{18,2},{3,19},{19,3},{4,20},{20... | collective-permute-start | bytes 1572872 | tf_op jit(solution)/shard_map/ppermute | solution.py:352
  157.8 30.4 %collective-permute-start.8 = (bf16[1024,256]{1,0:T(8,128)(2,1)}, bf16[1024,256]{1,0:T(8,128)(2,1)}, u32[]{:S(2)}, u32[]{:S(2)}) collective-permute-start(bf16[1024,256]{1,0:T(8,128)(2,1)} %get-tuple-element.30), channel_id=1, source_target_pairs={{0,16},{16,0},{1,17},{17,1},{2,18},{18,2},{3,19},{19,3},{4,20},{20... | collective-permute-start | bytes 1572872 | tf_op jit(solution)/shard_map/ppermute | solution.py:352
  180.4 0.9 copy-start.9
  181.3 9.7 %copy-start.2 = (bf16[2048,256]{1,0:T(8,128)(2,1)S(1)}, bf16[2048,256]{1,0:T(8,128)(2,1)}, u32[]{:S(2)}) copy-start(bf16[2048,256]{1,0:T(8,128)(2,1)} %all-gather.6.cloned.1.call-done.mine_ref) | copy-start | bytes 3145732
  182.2 18.2 %collective-permute-start.9 = (bf16[256,384]{1,0:T(8,128)(2,1)}, bf16[256,384]{1,0:T(8,128)(2,1)}, u32[]{:S(2)}, u32[]{:S(2)}) collective-permute-start(bf16[256,384]{1,0:T(8,128)(2,1)} %get-tuple-element.34), channel_id=1, source_target_pairs={{0,8},{8,0},{1,9},{9,1},{2,10},{10,2},{3,11},{11,3},{4,12},{12,4},... | collective-permute-start | bytes 589832 | tf_op jit(solution)/shard_map/ppermute | solution.py:352
  184.0 18.0 %collective-permute-start.10 = (bf16[256,384]{1,0:T(8,128)(2,1)}, bf16[256,384]{1,0:T(8,128)(2,1)}, u32[]{:S(2)}, u32[]{:S(2)}) collective-permute-start(bf16[256,384]{1,0:T(8,128)(2,1)} %get-tuple-element.33), channel_id=1, source_target_pairs={{0,8},{8,0},{1,9},{9,1},{2,10},{10,2},{3,11},{11,3},{4,12},{12,4},... | collective-permute-start | bytes 589832 | tf_op jit(solution)/shard_map/ppermute | solution.py:352
  185.2 18.5 %collective-permute-start.11 = (bf16[256,384]{1,0:T(8,128)(2,1)}, bf16[256,384]{1,0:T(8,128)(2,1)}, u32[]{:S(2)}, u32[]{:S(2)}) collective-permute-start(bf16[256,384]{1,0:T(8,128)(2,1)} %get-tuple-element.32), channel_id=1, source_target_pairs={{0,8},{8,0},{1,9},{9,1},{2,10},{10,2},{3,11},{11,3},{4,12},{12,4},... | collective-permute-start | bytes 589832 | tf_op jit(solution)/shard_map/ppermute | solution.py:352
  187.0 18.3 %collective-permute-start.12 = (bf16[256,384]{1,0:T(8,128)(2,1)}, bf16[256,384]{1,0:T(8,128)(2,1)}, u32[]{:S(2)}, u32[]{:S(2)}) collective-permute-start(bf16[256,384]{1,0:T(8,128)(2,1)} %get-tuple-element.31), channel_id=1, source_target_pairs={{0,8},{8,0},{1,9},{9,1},{2,10},{10,2},{3,11},{11,3},{4,12},{12,4},... | collective-permute-start | bytes 589832 | tf_op jit(solution)/shard_map/ppermute | solution.py:352
  191.1 1.2 copy-start.3
  192.3 1.2 copy-start.7
  194.7 0.8 copy-start.4
  195.5 19.0 %copy-start.10 = (bf16[1024,384]{1,0:T(8,128)(2,1)S(1)}, bf16[1024,384]{1,0:T(8,128)(2,1)}, u32[]{:S(2)}) copy-start(bf16[1024,384]{1,0:T(8,128)(2,1)} %copy-done.9) | copy-start | bytes 2359300
  195.5 12.4 %all-to-all-start.3 = ((bf16[8,128,256]{2,1,0:T(8,128)(2,1)}), bf16[8,128,256]{2,1,0:T(8,128)(2,1)S(1)}, u32[]{:S(2)}, u32[]{:S(2)}) async-start(bf16[8,128,256]{2,1,0:T(8,128)(2,1)} %bitcast.40), calls=%async_computation.3 | async-start | bytes 1048576 | tf_op jit(solution)/shard_map/all_to_all | solution.py:358
  207.9 8.8 %collective-permute-start.13 = (bf16[1024,256]{1,0:T(8,128)(2,1)S(1)}, bf16[1024,256]{1,0:T(8,128)(2,1)S(1)}, u32[]{:S(2)}, u32[]{:S(2)}) collective-permute-start(bf16[1024,256]{1,0:T(8,128)(2,1)S(1)} %bitcast.52), channel_id=1, source_target_pairs={{0,16},{16,0},{1,17},{17,1},{2,18},{18,2},{3,19},{19,3},{4,20},{20... | collective-permute-start | bytes 1572872 | tf_op jit(solution)/shard_map/ppermute | solution.py:352
Sparse Core Ops, SparseCore 0:
  70.1 36.6 all-gather.7
  108.6 41.6 all-gather.5
  152.1 38.8 all-gather.9

commit v3 on v2

--- a/solution.py
+++ b/solution.py
@@ -135,8 +135,7 @@
     )(mine, other)
 
 
-def merge_kernel(place_ref, parts_ref, gain_ref, normed_ref, keep_ref, send_ref, whole):
-    x_hi = place_ref[1]
+def merge_kernel(parts_ref, gain_ref, normed_ref, kept_ref, whole):
     rows, padded = parts_ref.shape
     width = padded - 256
     heads = width // HD
@@ -152,6 +151,7 @@
     total = jnp.sum(total * scale, axis=0)
     scale = scale.reshape(rows, heads)
     sums = jnp.zeros((share, HD), F32)
+    last = None
     for h in range(heads):
         cols = slice(h * HD, (h + 1) * HD)
         numer = jnp.zeros((share, HD), F32)
@@ -161,19 +161,12 @@
         value = (numer / total[:, h : h + 1]).astype(BF16).astype(F32)
         whole[:, cols] = value
         sums = sums + value
-    half = width // 2
-    for at in range(0, half, 512):
-        for side in range(2):
-            low = slice(at + side * 128, at + side * 128 + 128)
-            high = slice(at + side * 128 + 256, at + side * 128 + 384)
-            first = jnp.concatenate([whole[:, low], whole[:, high]], axis=0)
-            low = slice(half + at + side * 128, half + at + side * 128 + 128)
-            high = slice(half + at + side * 128 + 256, half + at + side * 128 + 384)
-            second = jnp.concatenate([whole[:, low], whole[:, high]], axis=0)
-            to = at // 512 * 16
-            cols = slice(side * 128, side * 128 + 128)
-            keep_ref[to : to + 16, cols] = jnp.where(x_hi == 0, first, second).astype(BF16)
-            send_ref[to : to + 16, cols] = jnp.where(x_hi == 0, second, first).astype(BF16)
+        if h % 2 == 0:
+            last = value
+        else:
+            block = h // 2
+            to = (block % 8 * 2 + block // 8) * 16
+            kept_ref[to : to + 16, :] = jnp.concatenate([last, value], axis=0).astype(BF16)
     center = jnp.sum(sums, axis=1, keepdims=True) / width
     squares = jnp.zeros((share, HD), F32)
     for h in range(heads):
@@ -188,29 +181,29 @@
             normed_ref[at : at + 16, cols] = twice
 
 
-def merge(place, parts, gain, copies):
+def merge(parts, gain, copies):
     rows, padded = parts.shape
     width = padded - 256
-    vmem = pl.BlockSpec(memory_space=pltpu.VMEM)
     return pl.pallas_call(
         merge_kernel,
-        in_specs=[pl.BlockSpec(memory_space=pltpu.SMEM), vmem, vmem],
         out_shape=(
             jax.ShapeDtypeStruct((copies * 8, width), BF16),
-            jax.ShapeDtypeStruct((64, 256), BF16),
-            jax.ShapeDtypeStruct((64, 256), BF16),
+            jax.ShapeDtypeStruct((width // 16, HD), BF16),
         ),
         scratch_shapes=[pltpu.VMEM((8, width), F32)],
         compiler_params=params(12),
         name="merge",
-    )(place, parts, gain)
-
-
-def qkv_kernel(place_ref, mine_ref, other_ref, weight_ref, keep_q, keep_kv, send_q, send_kv, tokens):
+    )(parts, gain)
+
+
+def qkv_kernel(
+    place_ref, mine_ref, other_ref, weight_ref, tie_ref, kv_ref, keep_ref, send_ref, tokens
+):
     step = pl.program_id(0)
     core = place_ref[0]
     x_hi = place_ref[1]
     half = mine_ref.shape[0]
+    rows = 2 * half
 
     @pl.when(step == 0)
     def _():
@@ -219,29 +212,28 @@
 
     made = dot(tokens[...], weight_ref[0], NN)
     first, second = made[:, :HD], made[:, HD:]
-    keep = jnp.where(x_hi == 0, first, second).astype(BF16)
-    send = jnp.where(x_hi == 0, second, first).astype(BF16)
 
     @pl.when(step == 0)
     def _():
-        keep_q[...] = keep
-        send_q[...] = send
+        keep_ref[...] = jnp.where(x_hi == 0, first, second).astype(BF16)
+        send_ref[...] = jnp.where(x_hi == 0, second, first).astype(BF16)
 
     for part in (1, 2):
 
         @pl.when(step == part)
         def _():
             cols = slice((part - 1) * HD, part * HD)
-            keep_kv[:, cols] = keep
-            send_kv[:, cols] = send
-
-
-def project(place, mine, other, weight):
+            for to in range(16):
+                value = first if to < 8 else second
+                kv_ref[to * rows : (to + 1) * rows, cols] = value.astype(BF16)
+
+
+def project(place, mine, other, weight, tie):
     half, width = mine.shape
     cols = weight.shape[2]
     rows = 2 * half
     whole = lambda s: (0, 0)
-    shapes = [(rows, HD), (rows, 2 * HD)] * 2
+    shapes = [(16 * rows, 2 * HD), (rows, HD), (rows, HD)]
     return pl.pallas_call(
         qkv_kernel,
         grid=(3,),
@@ -250,37 +242,30 @@
             pl.BlockSpec((half, width), whole),
             pl.BlockSpec((half, width), whole),
             pl.BlockSpec((1, width, cols), lambda s: (s, 0, 0)),
+            pl.BlockSpec(memory_space=pltpu.HBM),
         ],
         out_specs=[pl.BlockSpec(shape, whole) for shape in shapes],
         out_shape=[jax.ShapeDtypeStruct(shape, BF16) for shape in shapes],
         scratch_shapes=[pltpu.VMEM((rows, width), BF16)],
         compiler_params=params(16),
         name="project",
-    )(place, mine, other, weight)
-
-
-def attend_kernel(place_ref, keep_ref, got_ref, band_ref, out_ref, kept_ref, scores):
+    )(place, mine, other, weight, tie)
+
+
+def attend_kernel(place_ref, keep_ref, got_ref, kv_ref, out_ref, scores):
     x_hi = place_ref[1]
-    z = place_ref[2]
-    bands = band_ref.shape[0]
+    count = kv_ref.shape[0]
+    step = 256
     mixed = []
     for side in range(2):
         query = jnp.where(x_hi == side, keep_ref[...], got_ref[...])
-        for band in range(bands):
-            scores[:, band * 256 : band * 256 + 256] = dot(
-                query, band_ref[band, :256, :HD], NT
-            ) / math.sqrt(HD)
+        for at in range(0, count, step):
+            scores[:, at : at + step] = dot(query, kv_ref[at : at + step, :HD], NT) / math.sqrt(HD)
         every = scores[...]
         peak = jnp.max(every, axis=1, keepdims=True)
         weights = jnp.exp(every - peak)
         total = jnp.sum(weights, axis=1, keepdims=True)
-        weights = weights.astype(BF16)
-        update = jnp.zeros((query.shape[0], HD), F32)
-        for band in range(bands):
-            update = update + dot(
-                weights[:, band * 256 : band * 256 + 256], band_ref[band, :256, HD:], NN
-            )
-        mixed.append(update / total)
+        mixed.append(dot(weights.astype(BF16), kv_ref[:, HD:], NN) / total)
     for chip in range(8):
         for core in range(2):
             at = core * 64 + chip * 8
@@ -288,70 +273,64 @@
             out_ref[to : to + 16, :] = jnp.concatenate(
                 [mixed[0][at : at + 8], mixed[1][at : at + 8]], axis=0
             ).astype(BF16)
-    for band in range(bands):
-        rows = band_ref[band, pl.ds(pl.multiple_of(256 + z * 16, 16), 16), :].astype(F32)
-        mine, other = rows[:8], rows[8:]
-        first = jnp.where(x_hi == 0, mine, other)
-        second = jnp.where(x_hi == 0, other, mine)
-        kept_ref[band * 16 : band * 16 + 16, :] = jnp.concatenate([first, second], axis=0).astype(BF16)
-
-
-def attend(place, keep, got, bands):
+
+
+def attend(place, keep, got, kv):
     return pl.pallas_call(
         attend_kernel,
         in_specs=[pl.BlockSpec(memory_space=pltpu.SMEM)] + [pl.BlockSpec(memory_space=pltpu.VMEM)] * 3,
-        out_shape=(
-            jax.ShapeDtypeStruct((256, HD), BF16),
-            jax.ShapeDtypeStruct((128, 256), BF16),
-        ),
+        out_shape=jax.ShapeDtypeStruct((256, HD), BF16),
         scratch_shapes=[pltpu.VMEM((128, 2048), F32)],
         compiler_params=params(16),
         name="attend",
-    )(place, keep, got, bands)
-
-
-def output_kernel(place_ref, parts_ref, kept_ref, mine_ref, other_ref, out_ref, attended):
-    core = place_ref[0]
-    x_hi = place_ref[1]
+    )(place, keep, got, kv)
+
+
+def output_kernel(parts_ref, weight_ref, out_ref, attended):
     bands = parts_ref.shape[0]
-    half = mine_ref.shape[0]
-    for side in range(2):
-        owner = core if side == 0 else 1 - core
-        for chip in range(8):
-            for parity in range(2):
-                place = jnp.where(x_hi == parity, 0, 256) + (2 * chip + owner) * 16
-                place = pl.multiple_of(place, 16)
-                to = side * half + chip * 256 + parity * HD
-                for band in range(bands):
-                    attended[band * 16 : band * 16 + 16, to : to + HD] = parts_ref[
-                        band, pl.ds(place, 16), :
-                    ]
-    product = dot(attended[:, :half], mine_ref[...], NN) + dot(attended[:, half:], other_ref[...], NN)
-    layer = (kept_ref[...].astype(F32) + product).astype(BF16)
-    rows = layer.shape[0]
-    for copy in range(out_ref.shape[0] // rows):
-        out_ref[copy * rows : (copy + 1) * rows, :] = layer
-
-
-def output(place, parts, kept, mine, other, copies):
-    half, cols = mine.shape
-    rows = kept.shape[0]
+    cols = weight_ref.shape[1]
+    for band in range(0, bands, 2):
+        to = band * 8
+        for source in range(16):
+            at = source * 16
+            a = parts_ref[band, at : at + 16, :].astype(F32)
+            b = parts_ref[band + 1, at : at + 16, :].astype(F32)
+            for x_hi in range(2):
+                head = 2 * source + x_hi
+                rows = slice(x_hi * 8, x_hi * 8 + 8)
+                attended[to : to + 16, head * HD : (head + 1) * HD] = jnp.concatenate(
+                    [a[rows], b[rows]], axis=0
+                ).astype(BF16)
+    product = dot(attended[...], weight_ref[...], NN)
+    half = cols // 2
+    count = out_ref.shape[0] // 64
+    for band in range(0, bands, 2):
+        residual = []
+        for b in (band, band + 1):
+            kept = parts_ref[b, 256:288, :].astype(F32)
+            residual.append(
+                jnp.concatenate([kept[k : k + 8] for k in range(0, 32, 8)], axis=1)
+            )
+        at = band * 8
+        layer = (jnp.concatenate(residual, axis=0) + product[at : at + 16]).astype(BF16)
+        for to in range(count):
+            side = to % 2
+            out_ref[to * 64 + at : to * 64 + at + 16, :] = layer[:, side * half : (side + 1) * half]
+
+
+def output(parts, weight):
+    width, cols = weight.shape
     return pl.pallas_call(
         output_kernel,
-        in_specs=[pl.BlockSpec(memory_space=pltpu.SMEM)] + [pl.BlockSpec(memory_space=pltpu.VMEM)] * 4,
-        out_shape=jax.ShapeDtypeStruct((copies * rows, cols), BF16),
-        scratch_shapes=[pltpu.VMEM((rows, 2 * half), BF16)],
+        out_shape=jax.ShapeDtypeStruct((16 * 64, cols // 2), BF16),
+        scratch_shapes=[pltpu.VMEM((64, width), BF16)],
         compiler_params=params(12),
         name="output",
-    )(place, parts, kept, mine, other)
-
-
-def swap(x, axis, pieces=1):
-    rows = x.shape[0] // pieces
-    parts = [
-        lax.ppermute(x[k * rows : (k + 1) * rows], axis, [(0, 1), (1, 0)]) for k in range(pieces)
-    ]
-    return parts[0] if pieces == 1 else jnp.concatenate(parts, axis=0)
+    )(parts, weight)
+
+
+def swap(x, axis):
+    return lax.ppermute(x, axis, [(0, 1), (1, 0)])
 
 
 def exchange(x, axes):
@@ -363,36 +342,36 @@
     place = jnp.stack([core, x_hi, z]).astype(jnp.int32)
     width = out_weight.shape[1]
 
-    cot = lax.all_gather(head_cot, "z", axis=0, tiled=True)
-    cols = lax.dynamic_slice_in_dim(out_weight, (x_hi * 8 + z) * 256, 256, 1)
-    cols = lax.all_gather(cols, CHIPS, axis=0, tiled=True)
-    other_cols = swap(cols, "c", 2)
-    other_cot = swap(cot, "xh", 4)
-    both = jnp.stack([jnp.where(x_hi == 0, cot, other_cot), jnp.where(x_hi == 0, other_cot, cot)])
-    both = both.reshape(2, 8, 8, 2, 8, 384).transpose(3, 2, 1, 0, 4, 5).reshape(2, 1024, 384)
-    first = lax.dynamic_index_in_dim(both, core, 0, keepdims=False)
-    second = lax.dynamic_index_in_dim(both, 1 - core, 0, keepdims=False)
+    other_cot = swap(head_cot, "xh")
+    cot = jnp.stack([jnp.where(x_hi == 0, head_cot, other_cot), jnp.where(x_hi == 0, other_cot, head_cot)])
+    cot = lax.all_gather(cot.reshape(256, 384), "z", axis=0, tiled=True)
+    cols = jnp.concatenate(
+        [lax.dynamic_slice_in_dim(out_weight, side * 2048 + z * 256, 256, 1) for side in range(2)],
+        axis=1,
+    )
+    cols = lax.all_gather(cols, VAR, axis=0, tiled=True)
 
     keep, send = embed(place, patches.transpose(0, 2, 1), patch_weight, var_embed, agg_query.T)
     parts = pair(keep, swap(send, "c"))
     parts = exchange(parts, CHIPS)
-    normed, kept, kept_send = merge(place, parts, norm_gain.reshape(1, width), 8)
-    kept_got = swap(kept_send, "xh")
+    normed, kept = merge(parts, norm_gain.reshape(1, width), 8)
     normed = exchange(normed, CHIPS)
-    query, kv, query_send, kv_send = project(
-        place, normed, swap(normed, "c"), qkv_weight.transpose(1, 0, 2)
+    kv, query, query_send = project(
+        place, normed, swap(normed, "c"), qkv_weight.transpose(1, 0, 2), cot
     )
-    kv_got = swap(kv_send, "xh")
     query_got = swap(query_send, "xh")
-    residual = jnp.stack([kept.reshape(8, 8, 256), kept_got.reshape(8, 8, 256)], axis=1)
-    block = jnp.concatenate([kv, kv_got, residual.reshape(128, 256)], axis=0)
-    bands = lax.all_gather(block, "z", axis=0, tiled=False)
-    attended, kept = attend(place, query, query_got, bands)
-    attended = exchange(attended, VAR)
-    attended = jnp.concatenate([attended, swap(attended, "xh", 2)], axis=0)
-    attended = lax.all_gather(attended, "z", axis=0, tiled=False)
-    layer = output(place, attended, kept, cols, other_cols, 8)
-    layer = exchange(layer, CHIPS)
+    kv = exchange(kv, SEQ)
+    attended = attend(place, query, query_got, kv)
+    attended = exchange(attended, VAR + ("xh",))
+    sent = jnp.concatenate(
+        [jnp.broadcast_to(attended[None], (8, 256, HD)), kept.reshape(8, 32, HD)], axis=1
+    )
+    got = exchange(sent, "z")
+    layer = output(got, cols)
+    layer = exchange(layer, CHIPS + ("xh",))
+    cot = cot.reshape(8, 2, 8, 2, 8, 384).transpose(3, 2, 1, 0, 4, 5).reshape(2, 1024, 384)
+    first = lax.dynamic_index_in_dim(cot, core, 0, keepdims=False)
+    second = lax.dynamic_index_in_dim(cot, 1 - core, 0, keepdims=False)
     return dot(layer, first, TN) + dot(swap(layer, "c"), second, TN)
 
 

time: 225 us -> 177 us (0.79)
  waiting for transfers between devices: 72.4 us -> 40.8 us
  local copies, waits for them, and re-layouts: 20.2 us -> 8.97 us
  starting transfers between devices: 39.9 us -> 30.2 us
  blocking collectives: 50.5 us -> 56.6 us
  other arithmetic: 5.68 us -> 3.01 us
    all_gather x3 -> x2, waiting for transfers between devices: 49.1 us -> 0.01 us  [the longest x1 0.01 us: body(): cot = lax.all_gather(cot.reshape(256, 384), 'z', axis=0, tiled=True)]
    all_to_all x2 -> x4, blocking collectives: 27.9 us -> 56.6 us  [exchange(): return lax.all_to_all(x, axes, 0, 0, tiled=True)]
    all_gather x1 -> x0, blocking collectives: 22.6 us -> none  [body(): cot = lax.all_gather(head_cot, 'z', axis=0, tiled=True)]
    all_to_all x2, waiting for transfers between devices: 10.6 us -> 27.7 us  [exchange(): return lax.all_to_all(x, axes, 0, 0, tiled=True)]
    ppermute x14 -> x5, starting transfers between devices: 31.3 us -> 16 us  [swap(): return lax.ppermute(x, axis, [(0, 1), (1, 0)])]
    unnamed x29 -> x14, local copies, waits for them, and re-layouts: 14.5 us -> 7.64 us
    all_to_all x2, starting transfers between devices: 8.44 us -> 14.1 us  [exchange(): return lax.all_to_all(x, axes, 0, 0, tiled=True)]
    slice x3 -> x0, local copies, waits for them, and re-layouts: 3.17 us -> none  [swap(): x[k * rows:(k + 1) * rows]]
  transfers between devices with their start and end apart: 19 -> 9, of which waited for: 10 -> 7; matrix products, arithmetic and copies ran while one was open for 7% -> 2% of each run, Pallas kernels for 2% -> 12%
where the time goes in v3:
time: 177 us; the launch traced here: 176 us
  blocking collectives  56.6 us (32%)
  waiting for transfers between devices  40.8 us (23%)
  starting transfers between devices  30.2 us (17%)
  Pallas kernels  21.2 us (12%)
  between operations  13.5 us (8%)
  local copies, waits for them, and re-layouts  8.97 us (5%)
  other arithmetic  3.01 us (2%)
    all_to_all x4, blocking collectives, exchange(): return lax.all_to_all(x, axes, 0, 0, tiled=True)  56.6 us
    all_to_all x2, waiting for transfers between devices, exchange(): return lax.all_to_all(x, axes, 0, 0, tiled=True)  27.7 us
    ppermute x5, starting transfers between devices, swap(): return lax.ppermute(x, axis, [(0, 1), (1, 0)])  16 us
    all_to_all x2, starting transfers between devices, exchange(): return lax.all_to_all(x, axes, 0, 0, tiled=True)  14.1 us
    ppermute x5, waiting for transfers between devices, swap(): return lax.ppermute(x, axis, [(0, 1), (1, 0)])  13.2 us
    pallas_call x1, Pallas kernels, embed(): pl.pallas_call(embed_kernel, grid=(count,), in_specs=[pl.BlockSpec(memory...  12.8 us
    unnamed x14, local copies, waits for them, and re-layouts  7.64 us
  transfers between devices with their start and end apart: 9, of which 7 were waited for; matrix products, arithmetic and copies ran while one was open for 2% of the time, Pallas kernels for 12%

profile of v3, /device:TPU:1, one launch (start us, length us, event | category | flops | bytes accessed | tf_op | source)
XLA Modules:
  0.0 176.1 jit_solution(1182290032111204905)
XLA Ops:
  6.5 0.0 all-gather.3.cloned.1.call-start
  6.5 3.6 %collective-permute-start.2 = (bf16[128,384]{1,0:T(8,128)(2,1)}, bf16[128,384]{1,0:T(8,128)(2,1)S(1)}, u32[]{:S(2)}, u32[]{:S(2)}) collective-permute-start(bf16[128,384]{1,0:T(8,128)(2,1)} %param.15), channel_id=1, source_target_pairs={{0,8},{8,0},{1,9},{9,1},{2,10},{10,2},{3,11},{11,3},{4,12},{12,4},... | collective-permute-start | bytes 294920 | tf_op jit(solution)/shard_map/ppermute | solution.py:333
  10.1 2.2 %collective-permute-done.2 = bf16[128,384]{1,0:T(8,128)(2,1)S(1)} collective-permute-done((bf16[128,384]{1,0:T(8,128)(2,1)}, bf16[128,384]{1,0:T(8,128)(2,1)S(1)}, u32[]{:S(2)}, u32[]{:S(2)}) %collective-permute-start.2) | collective-permute-done | bytes 98336 | tf_op jit(solution)/shard_map/ppermute | solution.py:333
  12.3 0.9 select_bitcast_fusion.1
  13.2 0.7 pad_maximum_fusion.2
  14.0 0.0 all-gather.3.cloned.1.call-update
  14.0 0.0 all-gather.5.cloned.1.call-start
  14.1 1.0 constant_dynamic-slice_fusion.1
  15.1 0.7 pad_maximum_fusion.1
  15.8 0.0 all-gather.5.cloned.1.call-update
  15.8 0.6 pad_add_fusion.place_ref
  16.4 12.8 %embed.1 = (f32[64,4224]{1,0:T(8,128)}, f32[64,4224]{1,0:T(8,128)}) custom-call(s32[3]{0:T(128)} %pad_add_fusion.place_ref, bf16[6,64,128]{2,1,0:T(8,128)(2,1)} %bitcast.51, bf16[6,64,4096]{2,1,0:T(8,128)(2,1)} %weight_ref.1, bf16[6,4096]{1,0:T(8,128)(2,1)} %shift_ref.1, bf16[32,4096]{1,0:T(8,128)(2,1)} %bitcast.50), custom_call_target="tpu_custom_call" | custom-call | tf_op jit(solution)/shard_map/embed/pallas_call | solution.py:84
  29.2 3.8 %collective-permute-start = (f32[64,4224]{1,0:T(8,128)}, f32[64,4224]{1,0:T(8,128)S(1)}, u32[]{:S(2)}, u32[]{:S(2)}) collective-permute-start(f32[64,4224]{1,0:T(8,128)} %get-tuple-element.13), channel_id=1, source_target_pairs={{0,16},{16,0},{1,17},{17,1},{2,18},{18,2},{3,19},{19,3},{4,20},{20... | collective-permute-start | bytes 3244040 | tf_op jit(solution)/shard_map/ppermute | solution.py:333
  33.0 2.5 %collective-permute-done.other_ref = f32[64,4224]{1,0:T(8,128)S(1)} collective-permute-done((f32[64,4224]{1,0:T(8,128)}, f32[64,4224]{1,0:T(8,128)S(1)}, u32[]{:S(2)}, u32[]{:S(2)}) %collective-permute-start) | collective-permute-done | bytes 1081376 | tf_op jit(solution)/shard_map/ppermute | solution.py:333
  35.5 0.0 copy-start.4
  35.5 1.2 copy-done.4
  36.8 0.0 copy-start.6
  36.8 1.6 pair.1
  38.4 0.0 copy-start.5
  38.4 3.7 %all-to-all-start = ((bf16[8,8,4352]{2,1,0:T(8,128)(2,1)}), bf16[8,8,4352]{2,1,0:T(8,128)(2,1)S(1)}, u32[]{:S(2)}, u32[]{:S(2)}) async-start(bf16[8,8,4352]{2,1,0:T(8,128)(2,1)} %bitcast.5), calls=%async_computation | async-start | bytes 1114112 | tf_op jit(solution)/shard_map/all_to_all | solution.py:337
  42.0 0.0 copy-done.6
  42.1 9.6 %all-to-all-done = bf16[8,8,4352]{2,1,0:T(8,128)(2,1)S(1)} async-done(((bf16[8,8,4352]{2,1,0:T(8,128)(2,1)}), bf16[8,8,4352]{2,1,0:T(8,128)(2,1)S(1)}, u32[]{:S(2)}, u32[]{:S(2)}) %all-to-all-start) | async-done | bytes 557088 | tf_op jit(solution)/shard_map/all_to_all | solution.py:337
  51.7 0.8 merge.1
  52.5 12.4 %all_to_all.59 = bf16[8,8,4096]{2,1,0:T(8,128)(2,1)S(1)} all-to-all(bf16[8,8,4096]{2,1,0:T(8,128)(2,1)S(1)} %bitcast.41), channel_id=1, replica_groups=mesh['y'=4,'xl'=2,'c'=2,'xh'=2,'z'=8] {'y','xl'}, dimensions={0} | all-to-all | bytes 1048576 | tf_op jit(solution)/shard_map/all_to_all | solution.py:337
  64.9 1.9 %collective-permute-start.1 = (bf16[64,4096]{1,0:T(8,128)(2,1)S(1)}, bf16[64,4096]{1,0:T(8,128)(2,1)S(1)}, u32[]{:S(2)}, u32[]{:S(2)}) collective-permute-start(bf16[64,4096]{1,0:T(8,128)(2,1)S(1)} %bitcast.38), channel_id=1, source_target_pairs={{0,16},{16,0},{1,17},{17,1},{2,18},{18,2},{3,19},{19,3},{4,20},{20... | collective-permute-start | bytes 1572872 | tf_op jit(solution)/shard_map/ppermute | solution.py:333
  66.8 1.5 collective-permute-done.1.other_ref
  68.4 0.0 all-gather.3.cloned.1.call-done.tie_ref
  68.4 0.0 copy-done.5
  68.4 2.8 %copy-done = bf16[4096,3,256]{2,0,1:T(8,128)(2,1)S(1)} copy-done((bf16[4096,3,256]{2,0,1:T(8,128)(2,1)S(1)}, bf16[4096,3,256]{2,0,1:T(8,128)(2,1)}, u32[]{:S(2)}) %copy-start) | copy-done | bytes 6291480
  71.2 1.4 copy-done.1
  72.6 3.2 %project.1 = (bf16[2048,256]{1,0:T(8,128)(2,1)}, bf16[128,128]{1,0:T(8,128)(2,1)S(1)}, bf16[128,128]{1,0:T(8,128)(2,1)S(1)}) custom-call(s32[3]{0:T(128)S(1)} %copy-done.5, bf16[64,4096]{1,0:T(8,128)(2,1)S(1)} %bitcast.39, bf16[64,4096]{1,0:T(8,128)(2,1)S(1)} %collective-permute-done.1.other_ref, bf16[3,4096,256]{2,1,0:T(8,128)(2,1)S(1)} %bitcast.34, ...), custom_call_target="tpu_custom_call" | custom-call | tf_op jit(solution)/shard_map/project/pallas_call | solution.py:237
  75.8 10.5 %all-to-all-start.2 = ((bf16[16,128,256]{2,1,0:T(8,128)(2,1)}), bf16[16,128,256]{2,1,0:T(8,128)(2,1)S(1)}, u32[]{:S(2)}, u32[]{:S(2)}) async-start(bf16[16,128,256]{2,1,0:T(8,128)(2,1)} %bitcast.13), calls=%async_computation.2 | async-start | bytes 2097152 | tf_op jit(solution)/shard_map/all_to_all | solution.py:337
  86.2 2.9 %collective-permute-start.3 = (bf16[128,128]{1,0:T(8,128)(2,1)S(1)}, bf16[128,128]{1,0:T(8,128)(2,1)S(1)}, u32[]{:S(2)}, u32[]{:S(2)}) collective-permute-start(bf16[128,128]{1,0:T(8,128)(2,1)S(1)} %get-tuple-element.16), channel_id=1, source_target_pairs={{0,8},{8,0},{1,9},{9,1},{2,10},{10,2},{3,11},{11,3},{4,12},{12,4},... | collective-permute-start | bytes 98312 | tf_op jit(solution)/shard_map/ppermute | solution.py:333
  89.1 6.1 %collective-permute-done.3.got_ref = bf16[128,128]{1,0:T(8,128)(2,1)S(1)} collective-permute-done((bf16[128,128]{1,0:T(8,128)(2,1)S(1)}, bf16[128,128]{1,0:T(8,128)(2,1)S(1)}, u32[]{:S(2)}, u32[]{:S(2)}) %collective-permute-start.3) | collective-permute-done | bytes 32800 | tf_op jit(solution)/shard_map/ppermute | solution.py:333
  95.2 18.1 %all-to-all-done.2 = bf16[16,128,256]{2,1,0:T(8,128)(2,1)S(1)} async-done(((bf16[16,128,256]{2,1,0:T(8,128)(2,1)}), bf16[16,128,256]{2,1,0:T(8,128)(2,1)S(1)}, u32[]{:S(2)}, u32[]{:S(2)}) %all-to-all-start.2) | async-done | bytes 1048608 | tf_op jit(solution)/shard_map/all_to_all | solution.py:337
  113.3 1.9 %attend.1 = bf16[256,128]{1,0:T(8,128)(2,1)S(1)} custom-call(s32[3]{0:T(128)S(1)} %copy-done.5, bf16[128,128]{1,0:T(8,128)(2,1)S(1)} %get-tuple-element.15.keep_ref, bf16[128,128]{1,0:T(8,128)(2,1)S(1)} %collective-permute-done.3.got_ref, bf16[2048,256]{1,0:T(8,128)(2,1)S(1)} %bitcast.36), custom_call_target="tpu_custom_call" | custom-call | tf_op jit(solution)/shard_map/attend/pallas_call | solution.py:279
  115.1 12.4 %all_to_all.60 = bf16[32,8,128]{2,1,0:T(8,128)(2,1)S(1)} all-to-all(bf16[32,8,128]{2,1,0:T(8,128)(2,1)S(1)} %bitcast.42), channel_id=1, replica_groups=mesh['y'=4,'xl'=2,'c'=2,'xh'=2,'z'=8] {'y','xl','c','xh'}, dimensions={0} | all-to-all | bytes 131072 | tf_op jit(solution)/shard_map/all_to_all | solution.py:337
  127.5 0.1 broadcast_in_dim.9
  127.6 20.7 %all_to_all.61.parts_ref = bf16[8,288,128]{2,1,0:T(8,128)(2,1)S(1)} all-to-all(bf16[8,288,128]{2,1,0:T(8,128)(2,1)S(1)} %pad_maximum_fusion), channel_id=1, replica_groups=mesh['y'=4,'xl'=2,'c'=2,'xh'=2,'z'=8] {'z'}, dimensions={0} | all-to-all | bytes 1179648 | tf_op jit(solution)/shard_map/all_to_all | solution.py:337
  148.3 2.2 %copy-done.3 = bf16[4096,512]{1,0:T(8,128)(2,1)S(1)} copy-done((bf16[4096,512]{1,0:T(8,128)(2,1)S(1)}, bf16[4096,512]{1,0:T(8,128)(2,1)}, u32[]{:S(2)}) %copy-start.3) | copy-done | bytes 4194328
  150.5 0.9 output.1
  151.4 11.1 %all_to_all.62 = bf16[16,64,256]{2,1,0:T(8,128)(2,1)S(1)} all-to-all(bf16[16,64,256]{2,1,0:T(8,128)(2,1)S(1)} %bitcast.40), channel_id=1, replica_groups=mesh['y'=4,'xl'=2,'c'=2,'xh'=2,'z'=8] {'y','xl','xh'}, dimensions={0} | all-to-all | bytes 1048576 | tf_op jit(solution)/shard_map/all_to_all | solution.py:337
  162.6 3.9 %collective-permute-start.4 = (bf16[1024,256]{1,0:T(8,128)(2,1)S(1)}, bf16[1024,256]{1,0:T(8,128)(2,1)S(1)}, u32[]{:S(2)}, u32[]{:S(2)}) collective-permute-start(bf16[1024,256]{1,0:T(8,128)(2,1)S(1)} %bitcast.46), channel_id=1, source_target_pairs={{0,16},{16,0},{1,17},{17,1},{2,18},{18,2},{3,19},{19,3},{4,20},{20... | collective-permute-start | bytes 1572872 | tf_op jit(solution)/shard_map/ppermute | solution.py:333
  166.5 0.0 copy-done.2
  166.5 0.3 copy.9
  166.8 0.5 fusion.1
  167.2 0.8 collective-permute-done.4
  168.0 1.2 convolution_add_fusion
  (7 shorter events, 0.1 us)
Async XLA Ops:
  6.5 61.8 %all-gather.3.cloned.1.call-start = ((), (), s32[]{:S(2)}) async-start(), calls=%async_computation.6 | async-start | bytes 1769472 | tf_op jit(solution)/shard_map/all_gather | solution.py:347
  6.5 5.8 %collective-permute-start.2 = (bf16[128,384]{1,0:T(8,128)(2,1)}, bf16[128,384]{1,0:T(8,128)(2,1)S(1)}, u32[]{:S(2)}, u32[]{:S(2)}) collective-permute-start(bf16[128,384]{1,0:T(8,128)(2,1)} %param.15), channel_id=1, source_target_pairs={{0,8},{8,0},{1,9},{9,1},{2,10},{10,2},{3,11},{11,3},{4,12},{12,4},... | collective-permute-start | bytes 294920 | tf_op jit(solution)/shard_map/ppermute | solution.py:333
  14.0 134.3 %all-gather.5.cloned.1.call-start = ((), (), s32[]{:S(2)}) async-start(), calls=%async_computation.7 | async-start | bytes 4456448 | tf_op jit(solution)/shard_map/all_gather | solution.py:352
  29.2 6.3 %collective-permute-start = (f32[64,4224]{1,0:T(8,128)}, f32[64,4224]{1,0:T(8,128)S(1)}, u32[]{:S(2)}, u32[]{:S(2)}) collective-permute-start(f32[64,4224]{1,0:T(8,128)} %get-tuple-element.13), channel_id=1, source_target_pairs={{0,16},{16,0},{1,17},{17,1},{2,18},{18,2},{3,19},{19,3},{4,20},{20... | collective-permute-start | bytes 3244040 | tf_op jit(solution)/shard_map/ppermute | solution.py:333
  35.5 1.2 copy-start.4
  36.8 5.3 %copy-start.6 = (bf16[4096]{0:T(1024)(128)(2,1)S(1)}, bf16[4096]{0:T(1024)(128)(2,1)}, u32[]{:S(2)}) copy-start(bf16[4096]{0:T(1024)(128)(2,1)} %param.12) | copy-start | bytes 24580
  38.4 30.0 %copy-start.5 = (s32[3]{0:T(128)S(1)}, s32[3]{0:T(128)}, u32[]{:S(2)}) copy-start(s32[3]{0:T(128)} %pad_add_fusion.place_ref) | copy-start | bytes 40
  38.4 13.3 %all-to-all-start = ((bf16[8,8,4352]{2,1,0:T(8,128)(2,1)}), bf16[8,8,4352]{2,1,0:T(8,128)(2,1)S(1)}, u32[]{:S(2)}, u32[]{:S(2)}) async-start(bf16[8,8,4352]{2,1,0:T(8,128)(2,1)} %bitcast.5), calls=%async_computation | async-start | bytes 1114112 | tf_op jit(solution)/shard_map/all_to_all | solution.py:337
  64.9 3.4 %collective-permute-start.1 = (bf16[64,4096]{1,0:T(8,128)(2,1)S(1)}, bf16[64,4096]{1,0:T(8,128)(2,1)S(1)}, u32[]{:S(2)}, u32[]{:S(2)}) collective-permute-start(bf16[64,4096]{1,0:T(8,128)(2,1)S(1)} %bitcast.38), channel_id=1, source_target_pairs={{0,16},{16,0},{1,17},{17,1},{2,18},{18,2},{3,19},{19,3},{4,20},{20... | collective-permute-start | bytes 1572872 | tf_op jit(solution)/shard_map/ppermute | solution.py:333
  68.4 2.8 %copy-start = (bf16[4096,3,256]{2,0,1:T(8,128)(2,1)S(1)}, bf16[4096,3,256]{2,0,1:T(8,128)(2,1)}, u32[]{:S(2)}) copy-start(bf16[4096,3,256]{2,0,1:T(8,128)(2,1)} %param.13) | copy-start | bytes 18874372
  71.2 1.4 copy-start.1
  75.8 37.5 %all-to-all-start.2 = ((bf16[16,128,256]{2,1,0:T(8,128)(2,1)}), bf16[16,128,256]{2,1,0:T(8,128)(2,1)S(1)}, u32[]{:S(2)}, u32[]{:S(2)}) async-start(bf16[16,128,256]{2,1,0:T(8,128)(2,1)} %bitcast.13), calls=%async_computation.2 | async-start | bytes 2097152 | tf_op jit(solution)/shard_map/all_to_all | solution.py:337
  86.2 9.0 %collective-permute-start.3 = (bf16[128,128]{1,0:T(8,128)(2,1)S(1)}, bf16[128,128]{1,0:T(8,128)(2,1)S(1)}, u32[]{:S(2)}, u32[]{:S(2)}) collective-permute-start(bf16[128,128]{1,0:T(8,128)(2,1)S(1)} %get-tuple-element.16), channel_id=1, source_target_pairs={{0,8},{8,0},{1,9},{9,1},{2,10},{10,2},{3,11},{11,3},{4,12},{12,4},... | collective-permute-start | bytes 98312 | tf_op jit(solution)/shard_map/ppermute | solution.py:333
  148.3 2.2 %copy-start.3 = (bf16[4096,512]{1,0:T(8,128)(2,1)S(1)}, bf16[4096,512]{1,0:T(8,128)(2,1)}, u32[]{:S(2)}) copy-start(bf16[4096,512]{1,0:T(8,128)(2,1)} %all-gather.5.cloned.1.call-done.weight_ref) | copy-start | bytes 12582916
  150.5 16.0 %copy-start.2 = (bf16[2048,384]{1,0:T(8,128)(2,1)S(1)}, bf16[2048,384]{1,0:T(8,128)(2,1)}, u32[]{:S(2)}) copy-start(bf16[2048,384]{1,0:T(8,128)(2,1)} %all-gather.3.cloned.1.call-done.tie_ref) | copy-start | bytes 4718596
  162.6 5.5 %collective-permute-start.4 = (bf16[1024,256]{1,0:T(8,128)(2,1)S(1)}, bf16[1024,256]{1,0:T(8,128)(2,1)S(1)}, u32[]{:S(2)}, u32[]{:S(2)}) collective-permute-start(bf16[1024,256]{1,0:T(8,128)(2,1)S(1)} %bitcast.46), channel_id=1, source_target_pairs={{0,16},{16,0},{1,17},{17,1},{2,18},{18,2},{3,19},{19,3},{4,20},{20... | collective-permute-start | bytes 1572872 | tf_op jit(solution)/shard_map/ppermute | solution.py:333
Sparse Core Ops, SparseCore 0:
  14.1 40.7 all-gather.2
  56.7 48.9 all-gather.4

commit v4 on v3

v4 whole, which is shorter than its diff:
```python
import math

import jax
import jax.numpy as jnp
from jax import lax
from jax.experimental import pallas as pl
from jax.experimental.pallas import tpu as pltpu
from jax.sharding import Mesh, PartitionSpec as P

EPS = 1e-05
HD = 128
F32 = jnp.float32
BF16 = jnp.bfloat16
VAR = ("y", "xl", "c")
CHIPS = ("y", "xl")
SEQ = ("xh", "zq", "z0")
BANDS = ("xh", "zq")
NT = (((1,), (1,)), ((), ()))
TN = (((0,), (0,)), ((), ()))
NN = (((1,), (0,)), ((), ()))
MB = 1024 * 1024


def dot(a, b, dims):
    return lax.dot_general(a, b, dims, preferred_element_type=F32)


def params(megabytes):
    return pltpu.CompilerParams(vmem_limit_bytes=megabytes * MB)


def in_three(x):
    high = x.astype(BF16).astype(F32)
    rest = x - high
    middle = rest.astype(BF16).astype(F32)
    return high, middle, rest - middle


def packed(peak, total):
    p0, p1, p2 = in_three(peak)
    t0, t1, t2 = in_three(total)
    blank = jnp.zeros_like(peak)
    parts = [p0, p1, p2, t0, t1, t2, blank, blank]
    return jnp.concatenate(parts, axis=1).astype(BF16)


def unpacked(stats):
    stats = stats.astype(F32)
    peak = stats[:, 0:32] + stats[:, 32:64] + stats[:, 64:96]
    total = stats[:, 96:128] + stats[:, 128:160] + stats[:, 160:192]
    return peak, total


def embed_kernel(pixels_ref, weight_ref, shift_ref, query_ref, keep_ref, send_ref, embedded, scores, held, sems):
    core = lax.axis_index("c")
    count, rows, width = embedded.shape
    heads = query_ref.shape[0]
    half = rows // 2
    copies = [
        pltpu.make_async_copy(weight_ref.at[v], held.at[v], sems.at[v]) for v in range(count)
    ]
    for copy in copies:
        copy.start()
    new = lax.broadcasted_iota(jnp.int32, (rows, rows), 0)
    old = lax.broadcasted_iota(jnp.int32, (rows, rows), 1)
    group = (new % half) // 8 * 2 + jnp.where(new < half, core, 1 - core)
    order = jnp.where(old == group * 8 + new % 8, 1.0, 0.0).astype(BF16)
    step = 1024
    for v in range(count):
        tokens = dot(order, pixels_ref[v], NT).astype(BF16)
        copies[v].wait()
        total = jnp.zeros((rows, heads), F32)
        for at in range(0, width, step):
            block = dot(tokens, held[v, :, at : at + step], NN)
            shift = shift_ref[v : v + 1, at : at + step].astype(F32)
            block = (block + shift).astype(BF16)
            embedded[v, :, at : at + step] = block
            total = total + dot(block, query_ref[:, at : at + step], NT)
        scores[v] = total / math.sqrt(HD)
    every = scores[...]
    peak = jnp.max(every, axis=0)
    weights = jnp.exp(every - peak[None])
    total = jnp.sum(weights, axis=0)
    for h in range(heads):
        cols = slice(h * HD, (h + 1) * HD)
        numer = weights[0][:, h : h + 1] * embedded[0, :, cols].astype(F32)
        for v in range(1, count):
            numer = numer + weights[v][:, h : h + 1] * embedded[v, :, cols].astype(F32)
        keep_ref[:, cols] = numer[:half]
        send_ref[:, cols] = numer[half:].astype(BF16)
    blank = jnp.zeros((half, 128 - 2 * heads), F32)
    keep_ref[:, width:] = jnp.concatenate([peak[:half], total[:half], blank], axis=1)
    send_ref[:, width:] = packed(peak[half:], total[half:])


def embed(pixels, weight, shift, query):
    count, depth, rows = pixels.shape
    width = weight.shape[2]
    heads = query.shape[0]
    vmem = pl.BlockSpec(memory_space=pltpu.VMEM)
    return pl.pallas_call(
        embed_kernel,
        in_specs=[vmem, pl.BlockSpec(memory_space=pltpu.HBM), vmem, vmem],
        out_shape=(
            jax.ShapeDtypeStruct((rows // 2, width + 128), F32),
            jax.ShapeDtypeStruct((rows // 2, width + 256), BF16),
        ),
        scratch_shapes=[
            pltpu.VMEM((count, rows, width), BF16),
            pltpu.VMEM((count, rows, heads), F32),
            pltpu.VMEM((count, depth, width), BF16),
            pltpu.SemaphoreType.DMA((count,)),
        ],
        compiler_params=params(32),
        name="embed",
    )(pixels, weight, shift, query)


def pair_kernel(mine_ref, other_ref, out_ref):
    rows, padded = mine_ref.shape
    width = padded - 128
    heads = width // HD
    mine = mine_ref[:, width:]
    peak_a, total_a = mine[:, :heads], mine[:, heads : 2 * heads]
    peak_b, total_b = unpacked(other_ref[:, width:])
    top = jnp.maximum(peak_a, peak_b)
    scale_a = jnp.exp(peak_a - top)
    scale_b = jnp.exp(peak_b - top)
    for h in range(heads):
        cols = slice(h * HD, (h + 1) * HD)
        first = mine_ref[:, cols] * scale_a[:, h : h + 1]
        second = other_ref[:, cols].astype(F32) * scale_b[:, h : h + 1]
        out_ref[:, cols] = (first + second).astype(BF16)
    out_ref[:, width:] = packed(top, total_a * scale_a + total_b * scale_b)


def pair(mine, other):
    return pl.pallas_call(
        pair_kernel,
        out_shape=jax.ShapeDtypeStruct(other.shape, BF16),
        compiler_params=params(12),
        name="pair",
    )(mine, other)


def merge_kernel(parts_ref, gain_ref, normed_ref, kept_ref, whole):
    rows, padded = parts_ref.shape
    width = padded - 256
    heads = width // HD
    share = 8
    sources = rows // share
    peak, total = unpacked(parts_ref[:, width:])
    peak = peak.reshape(sources, share, heads)
    total = total.reshape(sources, share, heads)
    top = jnp.max(peak, axis=0)
    scale = jnp.exp(peak - top[None])
    total = jnp.sum(total * scale, axis=0)
    scale = scale.reshape(rows, heads)
    sums = jnp.zeros((share, HD), F32)
    last = None
    for h in range(heads):
        cols = slice(h * HD, (h + 1) * HD)
        numer = jnp.zeros((share, HD), F32)
        for at in range(0, rows, 16):
            block = parts_ref[at : at + 16, cols].astype(F32) * scale[at : at + 16, h : h + 1]
            numer = numer + block[:8] + block[8:]
        value = (numer / total[:, h : h + 1]).astype(BF16).astype(F32)
        whole[:, cols] = value
        sums = sums + value
        if h % 2 == 0:
            last = value
        else:
            to = h // 2 * 16
            kept_ref[to : to + 16, :] = jnp.concatenate([last, value], axis=0).astype(BF16)
    center = jnp.sum(sums, axis=1, keepdims=True) / width
    squares = jnp.zeros((share, HD), F32)
    for h in range(heads):
        shifted = whole[:, h * HD : (h + 1) * HD] - center
        squares = squares + shifted * shifted
    factor = lax.rsqrt(jnp.sum(squares, axis=1, keepdims=True) / width + EPS)
    for h in range(heads):
        cols = slice(h * HD, (h + 1) * HD)
        value = (whole[:, cols] - center) * factor * gain_ref[:, cols].astype(F32)
        twice = jnp.concatenate([value, value], axis=0).astype(BF16)
        for at in range(0, normed_ref.shape[0], 16):
            normed_ref[at : at + 16, cols] = twice


def merge(parts, gain, copies):
    rows, padded = parts.shape
    width = padded - 256
    return pl.pallas_call(
        merge_kernel,
        out_shape=(
            jax.ShapeDtypeStruct((copies * 8, width), BF16),
            jax.ShapeDtypeStruct((width // 16, HD), BF16),
        ),
        scratch_shapes=[pltpu.VMEM((8, width), F32)],
        compiler_params=params(12),
        name="merge",
    )(parts, gain)


def qkv_kernel(mine_ref, other_ref, weight_ref, tie_ref, kv_ref, keep_ref, send_ref, tokens, held, sems):
    core = lax.axis_index("c")
    z0 = lax.axis_index("z0")
    half, width = mine_ref.shape
    rows = 2 * half
    parts = sems.shape[1]
    depth = width // parts
    copies = [
        [
            pltpu.make_async_copy(
                weight_ref.at[k, pl.ds(part * depth, depth), :],
                held.at[k, pl.ds(part * depth, depth), :],
                sems.at[k, part],
            )
            for part in range(parts)
        ]
        for k in range(3)
    ]
    for k in range(3):
        for copy in copies[k]:
            copy.start()
    tokens[pl.ds(pl.multiple_of(core * half, half), half), :] = mine_ref[...]
    tokens[pl.ds(pl.multiple_of((1 - core) * half, half), half), :] = other_ref[...]
    for k in range(3):
        made = jnp.zeros((rows, 2 * HD), F32)
        for part in range(parts):
            copies[k][part].wait()
            at = slice(part * depth, (part + 1) * depth)
            made = made + dot(tokens[:, at], held[k, at, :], NN)
        first, second = made[:, :HD], made[:, HD:]
        if k == 0:
            keep_ref[...] = jnp.where(z0 == 0, first, second).astype(BF16)
            send_ref[...] = jnp.where(z0 == 0, second, first).astype(BF16)
        else:
            cols = slice((k - 1) * HD, k * HD)
            for to in range(16):
                value = first if to % 2 == 0 else second
                kv_ref[to * rows : (to + 1) * rows, cols] = value.astype(BF16)


def project(mine, other, weight, tie):
    half, width = mine.shape
    cols = weight.shape[2]
    rows = 2 * half
    parts = 4
    vmem = pl.BlockSpec(memory_space=pltpu.VMEM)
    hbm = pl.BlockSpec(memory_space=pltpu.HBM)
    shapes = [(16 * rows, 2 * HD), (rows, HD), (rows, HD)]
    return pl.pallas_call(
        qkv_kernel,
        in_specs=[vmem, vmem, hbm, hbm],
        out_shape=[jax.ShapeDtypeStruct(shape, BF16) for shape in shapes],
        scratch_shapes=[
            pltpu.VMEM((rows, width), BF16),
            pltpu.VMEM((3, width, cols), BF16),
            pltpu.SemaphoreType.DMA((3, parts)),
        ],
        compiler_params=params(24),
        name="project",
    )(mine, other, weight, tie)


def attend_kernel(keep_ref, got_ref, kv_ref, out_ref, scores):
    z0 = lax.axis_index("z0")
    count = kv_ref.shape[0]
    step = 256
    mixed = []
    for side in range(2):
        query = jnp.where(z0 == side, keep_ref[...], got_ref[...])
        for at in range(0, count, step):
            scores[:, at : at + step] = dot(query, kv_ref[at : at + step, :HD], NT) / math.sqrt(HD)
        every = scores[...]
        peak = jnp.max(every, axis=1, keepdims=True)
        weights = jnp.exp(every - peak)
        total = jnp.sum(weights, axis=1, keepdims=True)
        mixed.append(dot(weights.astype(BF16), kv_ref[:, HD:], NN) / total)
    for chip in range(8):
        for core in range(2):
            at = core * 64 + chip * 8
            to = (chip * 2 + core) * 16
            out_ref[to : to + 16, :] = jnp.concatenate(
                [mixed[0][at : at + 8], mixed[1][at : at + 8]], axis=0
            ).astype(BF16)


def attend(keep, got, kv):
    return pl.pallas_call(
        attend_kernel,
        out_shape=jax.ShapeDtypeStruct((256, HD), BF16),
        scratch_shapes=[pltpu.VMEM((128, 2048), F32)],
        compiler_params=params(16),
        name="attend",
    )(keep, got, kv)


def output_kernel(parts_ref, weight_ref, out_ref, attended, held, sems):
    bands = parts_ref.shape[0]
    width, cols = weight_ref.shape
    pieces = sems.shape[0]
    depth = width // pieces
    copies = [
        pltpu.make_async_copy(
            weight_ref.at[pl.ds(k * depth, depth), :], held.at[pl.ds(k * depth, depth), :], sems.at[k]
        )
        for k in range(pieces)
    ]
    for copy in copies:
        copy.start()
    for band in range(0, bands, 2):
        to = band * 8
        for source in range(16):
            at = source * 16
            a = parts_ref[band, at : at + 16, :].astype(F32)
            b = parts_ref[band + 1, at : at + 16, :].astype(F32)
            for side in range(2):
                head = 2 * source + side
                rows = slice(side * 8, side * 8 + 8)
                attended[to : to + 16, head * HD : (head + 1) * HD] = jnp.concatenate(
                    [a[rows], b[rows]], axis=0
                ).astype(BF16)
    product = jnp.zeros((attended.shape[0], cols), F32)
    for k in range(pieces):
        copies[k].wait()
        at = slice(k * depth, (k + 1) * depth)
        product = product + dot(attended[:, at], held[at, :], NN)
    half = cols // 2
    count = out_ref.shape[0] // 64
    for band in range(0, bands, 2):
        residual = []
        for b in (band, band + 1):
            kept = parts_ref[b, 256:288, :].astype(F32)
            residual.append(
                jnp.concatenate([kept[k : k + 8] for k in range(0, 32, 8)], axis=1)
            )
        at = band * 8
        layer = (jnp.concatenate(residual, axis=0) + product[at : at + 16]).astype(BF16)
        for to in range(count):
            side = to % 2
            out_ref[to * 64 + at : to * 64 + at + 16, :] = layer[:, side * half : (side + 1) * half]


def output(parts, weight):
    width, cols = weight.shape
    return pl.pallas_call(
        output_kernel,
        in_specs=[pl.BlockSpec(memory_space=pltpu.VMEM), pl.BlockSpec(memory_space=pltpu.HBM)],
        out_shape=jax.ShapeDtypeStruct((16 * 64, cols // 2), BF16),
        scratch_shapes=[
            pltpu.VMEM((64, width), BF16),
            pltpu.VMEM((width, cols), BF16),
            pltpu.SemaphoreType.DMA((8,)),
        ],
        compiler_params=params(16),
        name="output",
    )(parts, weight)


def swap(x, axis):
    return lax.ppermute(x, axis, [(0, 1), (1, 0)])


def exchange(x, axes):
    return lax.all_to_all(x, axes, 0, 0, tiled=True)


def body(patches, patch_weight, var_embed, agg_query, norm_gain, qkv_weight, out_weight, head_cot):
    core, z0 = lax.axis_index("c"), lax.axis_index("z0")
    width = out_weight.shape[1]

    keep, send = embed(patches.transpose(0, 2, 1), patch_weight, var_embed, agg_query.T)
    send, cot, cols = lax.optimization_barrier((send, head_cot, out_weight))
    parts = pair(keep, swap(send, "c"))

    other_cot = swap(cot, "z0")
    cot = jnp.stack([jnp.where(z0 == 0, cot, other_cot), jnp.where(z0 == 0, other_cot, cot)])
    cot = lax.all_gather(cot.reshape(256, 384), BANDS, axis=0, tiled=True)
    cols = lax.dynamic_slice_in_dim(cols, lax.axis_index(BANDS) * 512, 512, 1)
    cols = lax.all_gather(cols, VAR, axis=0, tiled=True)

    parts = exchange(parts, CHIPS)
    normed, kept = merge(parts, norm_gain.reshape(1, width), 8)
    normed = exchange(normed, CHIPS)
    kv, query, query_send = project(normed, swap(normed, "c"), qkv_weight.transpose(1, 0, 2), cot)
    query_got = swap(query_send, "z0")
    kv = exchange(kv, SEQ)
    attended = attend(query, query_got, kv)
    attended = exchange(attended, VAR + ("z0",))
    sent = jnp.concatenate(
        [jnp.broadcast_to(attended[None], (8, 256, HD)), kept.reshape(8, 32, HD)], axis=1
    )
    got = exchange(sent, BANDS)
    layer = output(got, cols)
    layer = exchange(layer, CHIPS + ("z0",))
    cot = cot.reshape(8, 2, 8, 2, 8, 384).transpose(3, 2, 1, 0, 4, 5).reshape(2, 1024, 384)
    first = lax.dynamic_index_in_dim(cot, core, 0, keepdims=False)
    second = lax.dynamic_index_in_dim(cot, 1 - core, 0, keepdims=False)
    return dot(layer, first, TN) + dot(swap(layer, "c"), second, TN)


def solution(mesh):
    whole = Mesh(mesh.devices.reshape(4, 2, 2, 2, 4, 2), ("y", "xl", "c", "xh", "zq", "z0"))
    return jax.shard_map(
        body,
        mesh=whole,
        in_specs=(
            P(VAR, SEQ, None),
            P(VAR, None, None),
            P(VAR, None),
            P(),
            P(),
            P(None, None, VAR),
            P(VAR, None),
            P(SEQ, VAR),
        ),
        out_specs=P(SEQ, VAR),
        check_vma=False,
    )
```

time: 177 us -> 199 us (1.12)
  waiting for transfers between devices: 40.8 us -> 65.5 us
  starting transfers between devices: 30.2 us -> 22.6 us
  local copies, waits for them, and re-layouts: 8.97 us -> 15.4 us
  blocking collectives: 56.6 us -> 60.6 us
  Pallas kernels: 21.2 us -> 18 us
  other arithmetic: 3.01 us -> 0.77 us
    all_gather x1, waiting for transfers between devices: 0.01 us -> 25.1 us  [body(): cot = lax.all_gather(cot.reshape(256, 384), BANDS, axis=0, tiled=True)]
    all_to_all x2, waiting for transfers between devices: 27.7 us -> 11.6 us  [exchange(): return lax.all_to_all(x, axes, 0, 0, tiled=True)]
    ppermute x5, waiting for transfers between devices: 13.2 us -> 28.9 us  [swap(): return lax.ppermute(x, axis, [(0, 1), (1, 0)])]
    all_to_all x2, starting transfers between devices: 14.1 us -> 8.65 us  [exchange(): return lax.all_to_all(x, axes, 0, 0, tiled=True)]
    unnamed x14 -> x24, local copies, waits for them, and re-layouts: 7.64 us -> 12.9 us
    all_to_all x4, blocking collectives: 56.6 us -> 60.6 us  [exchange(): return lax.all_to_all(x, axes, 0, 0, tiled=True)]
    pallas_call x5, Pallas kernels: 20.3 us -> 17.2 us  [the longest x1 9.45 us: embed(): pl.pallas_call(embed_kernel, in_specs=[vmem, pl.BlockSpec(memory_space=pl...]
    ppermute x5, starting transfers between devices: 16 us -> 13.9 us  [swap(): return lax.ppermute(x, axis, [(0, 1), (1, 0)])]
  transfers between devices with their start and end apart: 9 -> 9, of which waited for: 7 -> 7; matrix products, arithmetic and copies ran while one was open for 2% -> 2% of each run, Pallas kernels for 12% -> 4%
where the time goes in v4:
time: 199 us; the launch traced here: 198 us
  waiting for transfers between devices  65.5 us (33%)
  blocking collectives  60.6 us (30%)
  starting transfers between devices  22.6 us (11%)
  Pallas kernels  18 us (9%)
  local copies, waits for them, and re-layouts  15.4 us (8%)
  between operations  13.6 us (7%)
    all_to_all x4, blocking collectives, exchange(): return lax.all_to_all(x, axes, 0, 0, tiled=True)  60.6 us
    ppermute x5, waiting for transfers between devices, swap(): return lax.ppermute(x, axis, [(0, 1), (1, 0)])  28.9 us
    all_gather x1, waiting for transfers between devices, body(): cot = lax.all_gather(cot.reshape(256, 384), BANDS, axis=0, tiled=True)  25.1 us
    ppermute x5, starting transfers between devices, swap(): return lax.ppermute(x, axis, [(0, 1), (1, 0)])  13.9 us
    unnamed x24, local copies, waits for them, and re-layouts  12.9 us
    all_to_all x2, waiting for transfers between devices, exchange(): return lax.all_to_all(x, axes, 0, 0, tiled=True)  11.6 us
    pallas_call x1, Pallas kernels, embed(): pl.pallas_call(embed_kernel, in_specs=[vmem, pl.BlockSpec(memory_space=pl...  9.45 us
    all_to_all x2, starting transfers between devices, exchange(): return lax.all_to_all(x, axes, 0, 0, tiled=True)  8.65 us
  transfers between devices with their start and end apart: 9, of which 7 were waited for; matrix products, arithmetic and copies ran while one was open for 2% of the time, Pallas kernels for 4%

profile of v4, /device:TPU:1, one launch (start us, length us, event | category | flops | bytes accessed | tf_op | source)
XLA Modules:
  0.0 198.1 jit_solution(15308110375544606651)
XLA Ops:
  6.5 0.0 copy-start
  6.5 0.0 all-gather.3.cloned.1.call-start
  6.5 2.0 %copy-done.4 = bf16[6,64,4096]{2,1,0:T(8,128)(2,1)S(1)} copy-done((bf16[6,64,4096]{2,1,0:T(8,128)(2,1)S(1)}, bf16[6,64,4096]{2,1,0:T(8,128)(2,1)}, u32[]{:S(2)}) %copy-start.4) | copy-done | bytes 3145752
  8.6 0.9 copy-done.6
  9.5 0.9 copy-done.7
  10.4 0.8 copy-done.8
  11.3 9.4 %embed.1 = (f32[64,4224]{1,0:T(8,128)S(1)}, bf16[64,4352]{1,0:T(8,128)(2,1)S(1)}) custom-call(bf16[6,64,128]{2,1,0:T(8,128)(2,1)S(1)} %bitcast.42, bf16[6,64,4096]{2,1,0:T(8,128)(2,1)S(1)} %copy-done.4, bf16[6,4096]{1,0:T(8,128)(2,1)S(1)} %copy-done.8, bf16[32,4096]{1,0:T(8,128)(2,1)S(1)} %bitcast.40), custom_call_target="tpu_custom_call" | custom-call | tf_op jit(solution)/shard_map/embed/pallas_call | solution.py:101
  20.7 0.0 copy-start.9
  20.7 0.8 copy-done.9
  21.5 0.0 copy-done.10
  21.5 2.5 %collective-permute-start.2 = (bf16[128,384]{1,0:T(8,128)(2,1)S(1)}, bf16[128,384]{1,0:T(8,128)(2,1)S(1)}, u32[]{:S(2)}, u32[]{:S(2)}) collective-permute-start(bf16[128,384]{1,0:T(8,128)(2,1)S(1)} %copy-done.10), channel_id=1, source_target_pairs={{0,1},{1,0},{2,3},{3,2},{4,5},{5,4},{6,7},{7,6},{8,9},{9,8},{10,11... | collective-permute-start | bytes 294920 | tf_op jit(solution)/shard_map/ppermute | solution.py:362
  24.0 2.0 %collective-permute-done.2 = bf16[128,384]{1,0:T(8,128)(2,1)S(1)} collective-permute-done((bf16[128,384]{1,0:T(8,128)(2,1)S(1)}, bf16[128,384]{1,0:T(8,128)(2,1)S(1)}, u32[]{:S(2)}, u32[]{:S(2)}) %collective-permute-start.2) | collective-permute-done | bytes 98336 | tf_op jit(solution)/shard_map/ppermute | solution.py:362
  26.0 0.7 pad_maximum_fusion.1
  26.7 0.0 all-gather.3.cloned.1.call-update
  26.8 0.0 all-gather.5.cloned.1.call-start
  26.8 0.0 copy-done
  26.8 0.7 constant_dynamic-slice_fusion
  27.6 0.0 all-gather.5.cloned.1.call-update
  27.6 3.5 %collective-permute-start = (bf16[64,4352]{1,0:T(8,128)(2,1)}, bf16[64,4352]{1,0:T(8,128)(2,1)S(1)}, u32[]{:S(2)}, u32[]{:S(2)}) collective-permute-start(bf16[64,4352]{1,0:T(8,128)(2,1)} %copy-done.9), channel_id=1, source_target_pairs={{0,16},{16,0},{1,17},{17,1},{2,18},{18,2},{3,19},{19,3},{4,20},{20... | collective-permute-start | bytes 1671176 | tf_op jit(solution)/shard_map/ppermute | solution.py:362
  31.0 1.8 collective-permute-done.other_ref
  32.8 1.7 pair.1
  34.5 3.5 %all-to-all-start = ((bf16[8,8,4352]{2,1,0:T(8,128)(2,1)}), bf16[8,8,4352]{2,1,0:T(8,128)(2,1)S(1)}, u32[]{:S(2)}, u32[]{:S(2)}) async-start(bf16[8,8,4352]{2,1,0:T(8,128)(2,1)} %bitcast.2), calls=%async_computation | async-start | bytes 1114112 | tf_op jit(solution)/shard_map/all_to_all | solution.py:366
  38.1 9.5 %all-to-all-done = bf16[8,8,4352]{2,1,0:T(8,128)(2,1)S(1)} async-done(((bf16[8,8,4352]{2,1,0:T(8,128)(2,1)}), bf16[8,8,4352]{2,1,0:T(8,128)(2,1)S(1)}, u32[]{:S(2)}, u32[]{:S(2)}) %all-to-all-start) | async-done | bytes 557088 | tf_op jit(solution)/shard_map/all_to_all | solution.py:366
  47.6 0.8 merge.1
  48.4 11.3 %all_to_all.59 = bf16[8,8,4096]{2,1,0:T(8,128)(2,1)S(1)} all-to-all(bf16[8,8,4096]{2,1,0:T(8,128)(2,1)S(1)} %bitcast.39), channel_id=1, replica_groups=mesh['y'=4,'xl'=2,'c'=2,'xh'=2,'zq'=4,'z0'=2] {'y','xl'}, dimensions={0} | all-to-all | bytes 1048576 | tf_op jit(solution)/shard_map/all_to_all | solution.py:366
  59.7 3.0 %collective-permute-start.1 = (bf16[64,4096]{1,0:T(8,128)(2,1)S(1)}, bf16[64,4096]{1,0:T(8,128)(2,1)S(1)}, u32[]{:S(2)}, u32[]{:S(2)}) collective-permute-start(bf16[64,4096]{1,0:T(8,128)(2,1)S(1)} %bitcast.35), channel_id=1, source_target_pairs={{0,16},{16,0},{1,17},{17,1},{2,18},{18,2},{3,19},{19,3},{4,20},{20... | collective-permute-start | bytes 1572872 | tf_op jit(solution)/shard_map/ppermute | solution.py:362
  62.7 1.5 collective-permute-done.1.other_ref
  64.3 25.1 %all-gather.3.cloned.1.call-done.tie_ref = bf16[2048,384]{1,0:T(8,128)(2,1)} async-done(((bf16[256,384]{1,0:T(8,128)(2,1)}), bf16[2048,384]{1,0:T(8,128)(2,1)}) %all-gather.3.cloned.1.call-update) | async-done | bytes 1572880 | tf_op jit(solution)/shard_map/all_gather | solution.py:379
  89.3 2.8 %copy-done.1 = bf16[4096,3,256]{2,0,1:T(8,128)(2,1)S(1)} copy-done((bf16[4096,3,256]{2,0,1:T(8,128)(2,1)S(1)}, bf16[4096,3,256]{2,0,1:T(8,128)(2,1)}, u32[]{:S(2)}) %copy-start.1) | copy-done | bytes 6291480
  92.1 1.4 copy-done.2
  93.5 3.3 %project.1 = (bf16[2048,256]{1,0:T(8,128)(2,1)S(1)}, bf16[128,128]{1,0:T(8,128)(2,1)S(1)}, bf16[128,128]{1,0:T(8,128)(2,1)S(1)}) custom-call(bf16[64,4096]{1,0:T(8,128)(2,1)S(1)} %bitcast.36, bf16[64,4096]{1,0:T(8,128)(2,1)S(1)} %collective-permute-done.1.other_ref, bf16[3,4096,256]{2,1,0:T(8,128)(2,1)S(1)} %bitcast.31, bf16[2048,384]{1,0:T(8,128)(2,1)S(1)} %copy-done.2), custom_call_target="tpu_custom_call" | custom-call | tf_op jit(solution)/shard_map/project/pallas_call | solution.py:252
  96.8 1.0 copy-done.5
  97.8 5.1 %all-to-all-start.2 = ((bf16[16,128,256]{2,1,0:T(8,128)(2,1)}), bf16[16,128,256]{2,1,0:T(8,128)(2,1)S(1)}, u32[]{:S(2)}, u32[]{:S(2)}) async-start(bf16[16,128,256]{2,1,0:T(8,128)(2,1)} %bitcast.38), calls=%async_computation.2 | async-start | bytes 2097152 | tf_op jit(solution)/shard_map/all_to_all | solution.py:366
  102.9 1.4 collective-permute-start.3
  104.3 23.5 %collective-permute-done.3.got_ref = bf16[128,128]{1,0:T(8,128)(2,1)S(1)} collective-permute-done((bf16[128,128]{1,0:T(8,128)(2,1)S(1)}, bf16[128,128]{1,0:T(8,128)(2,1)S(1)}, u32[]{:S(2)}, u32[]{:S(2)}) %collective-permute-start.3) | collective-permute-done | bytes 32800 | tf_op jit(solution)/shard_map/ppermute | solution.py:362
  127.8 2.1 %all-to-all-done.2 = bf16[16,128,256]{2,1,0:T(8,128)(2,1)S(1)} async-done(((bf16[16,128,256]{2,1,0:T(8,128)(2,1)}), bf16[16,128,256]{2,1,0:T(8,128)(2,1)S(1)}, u32[]{:S(2)}, u32[]{:S(2)}) %all-to-all-start.2) | async-done | bytes 1048608 | tf_op jit(solution)/shard_map/all_to_all | solution.py:366
  129.9 1.3 attend.1
  131.2 15.2 %all_to_all.60 = bf16[32,8,128]{2,1,0:T(8,128)(2,1)S(1)} all-to-all(bf16[32,8,128]{2,1,0:T(8,128)(2,1)S(1)} %bitcast.41), channel_id=1, replica_groups=mesh['y'=4,'xl'=2,'c'=2,'xh'=2,'zq'=4,'z0'=2] {'y','xl','c','z0'}, dimensions={0} | all-to-all | bytes 131072 | tf_op jit(solution)/shard_map/all_to_all | solution.py:366
  146.4 0.1 broadcast_in_dim.9
  146.5 24.3 %all_to_all.61.parts_ref = bf16[8,288,128]{2,1,0:T(8,128)(2,1)S(1)} all-to-all(bf16[8,288,128]{2,1,0:T(8,128)(2,1)S(1)} %pad_maximum_fusion), channel_id=1, replica_groups=mesh['y'=4,'xl'=2,'c'=2,'xh'=2,'zq'=4,'z0'=2] {'xh','zq'}, dimensions={0} | all-to-all | bytes 1179648 | tf_op jit(solution)/shard_map/all_to_all | solution.py:366
  170.8 2.2 %copy-done.3 = bf16[4096,512]{1,0:T(8,128)(2,1)S(1)} copy-done((bf16[4096,512]{1,0:T(8,128)(2,1)S(1)}, bf16[4096,512]{1,0:T(8,128)(2,1)}, u32[]{:S(2)}) %copy-start.3) | copy-done | bytes 4194328
  173.0 1.4 output.1
  174.5 9.9 %all_to_all.62 = bf16[16,64,256]{2,1,0:T(8,128)(2,1)S(1)} all-to-all(bf16[16,64,256]{2,1,0:T(8,128)(2,1)S(1)} %bitcast.37), channel_id=1, replica_groups=mesh['y'=4,'xl'=2,'c'=2,'xh'=2,'zq'=4,'z0'=2] {'y','xl','z0'}, dimensions={0} | all-to-all | bytes 1048576 | tf_op jit(solution)/shard_map/all_to_all | solution.py:366
  184.4 3.6 %collective-permute-start.4 = (bf16[1024,256]{1,0:T(8,128)(2,1)S(1)}, bf16[1024,256]{1,0:T(8,128)(2,1)S(1)}, u32[]{:S(2)}, u32[]{:S(2)}) collective-permute-start(bf16[1024,256]{1,0:T(8,128)(2,1)S(1)} %bitcast.46), channel_id=1, source_target_pairs={{0,16},{16,0},{1,17},{17,1},{2,18},{18,2},{3,19},{19,3},{4,20},{20... | collective-permute-start | bytes 1572872 | tf_op jit(solution)/shard_map/ppermute | solution.py:362
  187.9 1.7 copy.9
  189.6 0.5 fusion.1
  190.1 0.0 collective-permute-done.4
  190.1 1.2 convolution_add_fusion
  (15 shorter events, 0.1 us)
Async XLA Ops:
  6.5 20.3 %copy-start = (bf16[256,4096]{1,0:T(8,128)(2,1)S(1)}, bf16[256,4096]{1,0:T(8,128)(2,1)}, u32[]{:S(2)}) copy-start(bf16[256,4096]{1,0:T(8,128)(2,1)} %param.14) | copy-start | bytes 6291460
  6.5 82.8 %all-gather.3.cloned.1.call-start = ((), (), s32[]{:S(2)}) async-start(), calls=%async_computation.6 | async-start | bytes 1769472 | tf_op jit(solution)/shard_map/all_gather | solution.py:379
  6.5 2.0 %copy-start.4 = (bf16[6,64,4096]{2,1,0:T(8,128)(2,1)S(1)}, bf16[6,64,4096]{2,1,0:T(8,128)(2,1)}, u32[]{:S(2)}) copy-start(bf16[6,64,4096]{2,1,0:T(8,128)(2,1)} %weight_ref.1) | copy-start | bytes 9437188
  8.6 0.9 copy-start.6
  9.5 0.9 copy-start.7
  10.4 0.8 copy-start.8
  11.3 10.3 %copy-start.10 = (bf16[128,384]{1,0:T(8,128)(2,1)S(1)}, bf16[128,384]{1,0:T(8,128)(2,1)}, u32[]{:S(2)}) copy-start(bf16[128,384]{1,0:T(8,128)(2,1)} %param.15) | copy-start | bytes 294916
  20.7 0.8 copy-start.9
  21.5 4.5 %collective-permute-start.2 = (bf16[128,384]{1,0:T(8,128)(2,1)S(1)}, bf16[128,384]{1,0:T(8,128)(2,1)S(1)}, u32[]{:S(2)}, u32[]{:S(2)}) collective-permute-start(bf16[128,384]{1,0:T(8,128)(2,1)S(1)} %copy-done.10), channel_id=1, source_target_pairs={{0,1},{1,0},{2,3},{3,2},{4,5},{5,4},{6,7},{7,6},{8,9},{9,8},{10,11... | collective-permute-start | bytes 294920 | tf_op jit(solution)/shard_map/ppermute | solution.py:362
  26.8 144.1 %all-gather.5.cloned.1.call-start = ((), (), s32[]{:S(2)}) async-start(), calls=%async_computation.7 | async-start | bytes 4456448 | tf_op jit(solution)/shard_map/all_gather | solution.py:381
  27.6 5.3 %collective-permute-start = (bf16[64,4352]{1,0:T(8,128)(2,1)}, bf16[64,4352]{1,0:T(8,128)(2,1)S(1)}, u32[]{:S(2)}, u32[]{:S(2)}) collective-permute-start(bf16[64,4352]{1,0:T(8,128)(2,1)} %copy-done.9), channel_id=1, source_target_pairs={{0,16},{16,0},{1,17},{17,1},{2,18},{18,2},{3,19},{19,3},{4,20},{20... | collective-permute-start | bytes 1671176 | tf_op jit(solution)/shard_map/ppermute | solution.py:362
  32.8 5.2 %copy-start.11 = (bf16[4096]{0:T(1024)(128)(2,1)S(1)}, bf16[4096]{0:T(1024)(128)(2,1)}, u32[]{:S(2)}) copy-start(bf16[4096]{0:T(1024)(128)(2,1)} %param.12) | copy-start | bytes 24580
  34.5 13.1 %all-to-all-start = ((bf16[8,8,4352]{2,1,0:T(8,128)(2,1)}), bf16[8,8,4352]{2,1,0:T(8,128)(2,1)S(1)}, u32[]{:S(2)}, u32[]{:S(2)}) async-start(bf16[8,8,4352]{2,1,0:T(8,128)(2,1)} %bitcast.2), calls=%async_computation | async-start | bytes 1114112 | tf_op jit(solution)/shard_map/all_to_all | solution.py:366
  59.7 4.6 %collective-permute-start.1 = (bf16[64,4096]{1,0:T(8,128)(2,1)S(1)}, bf16[64,4096]{1,0:T(8,128)(2,1)S(1)}, u32[]{:S(2)}, u32[]{:S(2)}) collective-permute-start(bf16[64,4096]{1,0:T(8,128)(2,1)S(1)} %bitcast.35), channel_id=1, source_target_pairs={{0,16},{16,0},{1,17},{17,1},{2,18},{18,2},{3,19},{19,3},{4,20},{20... | collective-permute-start | bytes 1572872 | tf_op jit(solution)/shard_map/ppermute | solution.py:362
  89.3 2.8 %copy-start.1 = (bf16[4096,3,256]{2,0,1:T(8,128)(2,1)S(1)}, bf16[4096,3,256]{2,0,1:T(8,128)(2,1)}, u32[]{:S(2)}) copy-start(bf16[4096,3,256]{2,0,1:T(8,128)(2,1)} %param.13) | copy-start | bytes 18874372
  92.1 1.4 copy-start.2
  96.8 1.0 copy-start.5
  97.8 32.1 %all-to-all-start.2 = ((bf16[16,128,256]{2,1,0:T(8,128)(2,1)}), bf16[16,128,256]{2,1,0:T(8,128)(2,1)S(1)}, u32[]{:S(2)}, u32[]{:S(2)}) async-start(bf16[16,128,256]{2,1,0:T(8,128)(2,1)} %bitcast.38), calls=%async_computation.2 | async-start | bytes 2097152 | tf_op jit(solution)/shard_map/all_to_all | solution.py:366
  102.9 24.9 %collective-permute-start.3 = (bf16[128,128]{1,0:T(8,128)(2,1)S(1)}, bf16[128,128]{1,0:T(8,128)(2,1)S(1)}, u32[]{:S(2)}, u32[]{:S(2)}) collective-permute-start(bf16[128,128]{1,0:T(8,128)(2,1)S(1)} %get-tuple-element.21), channel_id=1, source_target_pairs={{0,1},{1,0},{2,3},{3,2},{4,5},{5,4},{6,7},{7,6},{8,9},{9,8},{10,11... | collective-permute-start | bytes 98312 | tf_op jit(solution)/shard_map/ppermute | solution.py:362
  170.8 2.2 %copy-start.3 = (bf16[4096,512]{1,0:T(8,128)(2,1)S(1)}, bf16[4096,512]{1,0:T(8,128)(2,1)}, u32[]{:S(2)}) copy-start(bf16[4096,512]{1,0:T(8,128)(2,1)} %all-gather.5.cloned.1.call-done.weight_ref) | copy-start | bytes 12582916
  184.4 5.7 %collective-permute-start.4 = (bf16[1024,256]{1,0:T(8,128)(2,1)S(1)}, bf16[1024,256]{1,0:T(8,128)(2,1)S(1)}, u32[]{:S(2)}, u32[]{:S(2)}) collective-permute-start(bf16[1024,256]{1,0:T(8,128)(2,1)S(1)} %bitcast.46), channel_id=1, source_target_pairs={{0,16},{16,0},{1,17},{17,1},{2,18},{18,2},{3,19},{19,3},{4,20},{20... | collective-permute-start | bytes 1572872 | tf_op jit(solution)/shard_map/ppermute | solution.py:362
Sparse Core Ops, SparseCore 0:
  26.9 62.4 all-gather.2
  91.2 44.5 all-gather.4

commit v5 on v4

--- a/solution.py
+++ b/solution.py
@@ -86,10 +86,9 @@
         numer = weights[0][:, h : h + 1] * embedded[0, :, cols].astype(F32)
         for v in range(1, count):
             numer = numer + weights[v][:, h : h + 1] * embedded[v, :, cols].astype(F32)
-        keep_ref[:, cols] = numer[:half]
+        keep_ref[:, cols] = numer[:half].astype(BF16)
         send_ref[:, cols] = numer[half:].astype(BF16)
-    blank = jnp.zeros((half, 128 - 2 * heads), F32)
-    keep_ref[:, width:] = jnp.concatenate([peak[:half], total[:half], blank], axis=1)
+    keep_ref[:, width:] = packed(peak[:half], total[:half])
     send_ref[:, width:] = packed(peak[half:], total[half:])
 
 
@@ -98,37 +97,34 @@
     width = weight.shape[2]
     heads = query.shape[0]
     vmem = pl.BlockSpec(memory_space=pltpu.VMEM)
+    part = jax.ShapeDtypeStruct((rows // 2, width + 256), BF16)
     return pl.pallas_call(
         embed_kernel,
         in_specs=[vmem, pl.BlockSpec(memory_space=pltpu.HBM), vmem, vmem],
-        out_shape=(
-            jax.ShapeDtypeStruct((rows // 2, width + 128), F32),
-            jax.ShapeDtypeStruct((rows // 2, width + 256), BF16),
-        ),
+        out_shape=(part, part),
         scratch_shapes=[
             pltpu.VMEM((count, rows, width), BF16),
             pltpu.VMEM((count, rows, heads), F32),
             pltpu.VMEM((count, depth, width), BF16),
             pltpu.SemaphoreType.DMA((count,)),
         ],
-        compiler_params=params(32),
+        compiler_params=params(60),
         name="embed",
     )(pixels, weight, shift, query)
 
 
 def pair_kernel(mine_ref, other_ref, out_ref):
     rows, padded = mine_ref.shape
-    width = padded - 128
+    width = padded - 256
     heads = width // HD
-    mine = mine_ref[:, width:]
-    peak_a, total_a = mine[:, :heads], mine[:, heads : 2 * heads]
+    peak_a, total_a = unpacked(mine_ref[:, width:])
     peak_b, total_b = unpacked(other_ref[:, width:])
     top = jnp.maximum(peak_a, peak_b)
     scale_a = jnp.exp(peak_a - top)
     scale_b = jnp.exp(peak_b - top)
     for h in range(heads):
         cols = slice(h * HD, (h + 1) * HD)
-        first = mine_ref[:, cols] * scale_a[:, h : h + 1]
+        first = mine_ref[:, cols].astype(F32) * scale_a[:, h : h + 1]
         second = other_ref[:, cols].astype(F32) * scale_b[:, h : h + 1]
         out_ref[:, cols] = (first + second).astype(BF16)
     out_ref[:, width:] = packed(top, total_a * scale_a + total_b * scale_b)
@@ -201,7 +197,7 @@
     )(parts, gain)
 
 
-def qkv_kernel(mine_ref, other_ref, weight_ref, tie_ref, kv_ref, keep_ref, send_ref, tokens, held, sems):
+def qkv_kernel(mine_ref, other_ref, weight_ref, kv_ref, keep_ref, send_ref, tokens, held, sems):
     core = lax.axis_index("c")
     z0 = lax.axis_index("z0")
     half, width = mine_ref.shape
@@ -241,7 +237,7 @@
                 kv_ref[to * rows : (to + 1) * rows, cols] = value.astype(BF16)
 
 
-def project(mine, other, weight, tie):
+def project(mine, other, weight):
     half, width = mine.shape
     cols = weight.shape[2]
     rows = 2 * half
@@ -251,16 +247,16 @@
     shapes = [(16 * rows, 2 * HD), (rows, HD), (rows, HD)]
     return pl.pallas_call(
         qkv_kernel,
-        in_specs=[vmem, vmem, hbm, hbm],
+        in_specs=[vmem, vmem, hbm],
         out_shape=[jax.ShapeDtypeStruct(shape, BF16) for shape in shapes],
         scratch_shapes=[
             pltpu.VMEM((rows, width), BF16),
             pltpu.VMEM((3, width, cols), BF16),
             pltpu.SemaphoreType.DMA((3, parts)),
         ],
-        compiler_params=params(24),
+        compiler_params=params(50),
         name="project",
-    )(mine, other, weight, tie)
+    )(mine, other, weight)
 
 
 def attend_kernel(keep_ref, got_ref, kv_ref, out_ref, scores):
@@ -353,7 +349,7 @@
             pltpu.VMEM((width, cols), BF16),
             pltpu.SemaphoreType.DMA((8,)),
         ],
-        compiler_params=params(16),
+        compiler_params=params(50),
         name="output",
     )(parts, weight)
 
@@ -367,25 +363,23 @@
 
 
 def body(patches, patch_weight, var_embed, agg_query, norm_gain, qkv_weight, out_weight, head_cot):
-    core, z0 = lax.axis_index("c"), lax.axis_index("z0")
+    core = lax.axis_index("c")
     width = out_weight.shape[1]
 
     keep, send = embed(patches.transpose(0, 2, 1), patch_weight, var_embed, agg_query.T)
-    send, cot, cols = lax.optimization_barrier((send, head_cot, out_weight))
     parts = pair(keep, swap(send, "c"))
-
-    other_cot = swap(cot, "z0")
-    cot = jnp.stack([jnp.where(z0 == 0, cot, other_cot), jnp.where(z0 == 0, other_cot, cot)])
-    cot = lax.all_gather(cot.reshape(256, 384), BANDS, axis=0, tiled=True)
+    parts, cols = lax.optimization_barrier((parts, out_weight))
+
+    cot = lax.all_gather(head_cot, SEQ, axis=0, tiled=True)
     cols = lax.dynamic_slice_in_dim(cols, lax.axis_index(BANDS) * 512, 512, 1)
     cols = lax.all_gather(cols, VAR, axis=0, tiled=True)
 
     parts = exchange(parts, CHIPS)
     normed, kept = merge(parts, norm_gain.reshape(1, width), 8)
     normed = exchange(normed, CHIPS)
-    kv, query, query_send = project(normed, swap(normed, "c"), qkv_weight.transpose(1, 0, 2), cot)
+    kv, query, query_send = project(normed, swap(normed, "c"), qkv_weight.transpose(1, 0, 2))
     query_got = swap(query_send, "z0")
-    kv = exchange(kv, SEQ)
+    kv, cot = lax.optimization_barrier((exchange(kv, SEQ), cot))
     attended = attend(query, query_got, kv)
     attended = exchange(attended, VAR + ("z0",))
     sent = jnp.concatenate(

time: 199 us -> 180 us (0.905)
  waiting for transfers between devices: 65.5 us -> 52.1 us
  local copies, waits for them, and re-layouts: 15.4 us -> 4.51 us
  Pallas kernels: 18 us -> 22.4 us
  blocking collectives: 60.6 us -> 62.6 us
    ppermute x5 -> x4, waiting for transfers between devices: 28.9 us -> 3.34 us  [swap(): return lax.ppermute(x, axis, [(0, 1), (1, 0)])]
    unnamed x24 -> x8, local copies, waits for them, and re-layouts: 12.9 us -> 2.04 us
    all_to_all x2, starting transfers between devices: 8.65 us -> 13.9 us  [exchange(): return lax.all_to_all(x, axes, 0, 0, tiled=True)]
    all_gather x1, waiting for transfers between devices: 0.01 us -> 5.2 us  [body(): cols = lax.all_gather(cols, VAR, axis=0, tiled=True)]
    ppermute x5 -> x4, starting transfers between devices: 13.9 us -> 8.92 us  [swap(): return lax.ppermute(x, axis, [(0, 1), (1, 0)])]
    all_gather x1, waiting for transfers between devices: 25.1 us -> 29.2 us  [body(): cot = lax.all_gather(head_cot, SEQ, axis=0, tiled=True)]
    pallas_call x1, Pallas kernels: 9.45 us -> 12.2 us  [embed(): pl.pallas_call(embed_kernel, in_specs=[vmem, pl.BlockSpec(memory_space=pl...]
    all_to_all x2, waiting for transfers between devices: 11.6 us -> 13.6 us  [exchange(): return lax.all_to_all(x, axes, 0, 0, tiled=True)]
  transfers between devices with their start and end apart: 9 -> 8, of which waited for: 7 -> 6; matrix products, arithmetic and copies ran while one was open for 2% -> 2% of each run, Pallas kernels for 4% -> 11%
where the time goes in v5:
time: 180 us
  blocking collectives  62.6 us (35%)
  waiting for transfers between devices  52.1 us (29%)
  starting transfers between devices  22.8 us (13%)
  Pallas kernels  22.4 us (12%)
  between operations  13.5 us (8%)
  local copies, waits for them, and re-layouts  4.51 us (3%)
    all_to_all x4, blocking collectives, exchange(): return lax.all_to_all(x, axes, 0, 0, tiled=True)  62.6 us
    all_gather x1, waiting for transfers between devices, body(): cot = lax.all_gather(head_cot, SEQ, axis=0, tiled=True)  29.2 us
    all_to_all x2, starting transfers between devices, exchange(): return lax.all_to_all(x, axes, 0, 0, tiled=True)  13.9 us
    all_to_all x2, waiting for transfers between devices, exchange(): return lax.all_to_all(x, axes, 0, 0, tiled=True)  13.6 us
    pallas_call x1, Pallas kernels, embed(): pl.pallas_call(embed_kernel, in_specs=[vmem, pl.BlockSpec(memory_space=pl...  12.2 us
    ppermute x4, starting transfers between devices, swap(): return lax.ppermute(x, axis, [(0, 1), (1, 0)])  8.92 us
    all_gather x1, waiting for transfers between devices, body(): cols = lax.all_gather(cols, VAR, axis=0, tiled=True)  5.2 us
    pallas_call x1, Pallas kernels, project(): pl.pallas_call(qkv_kernel, in_specs=[vmem, vmem, hbm], out_shape=[jax.Sha...  3.94 us
  transfers between devices with their start and end apart: 8, of which 6 were waited for; matrix products, arithmetic and copies ran while one was open for 2% of the time, Pallas kernels for 11%

profile of v5, /device:TPU:1, one launch (start us, length us, event | category | flops | bytes accessed | tf_op | source)
XLA Modules:
  0.0 179.6 jit_solution(12799797394211797133)
XLA Ops:
  6.5 0.0 copy-start
  6.5 0.0 all-gather.3.cloned.1.call-start
  6.5 0.7 all-gather.3.cloned.1.call-update
  7.3 0.0 all-gather.5.cloned.1.call-start
  7.3 12.2 %embed.1 = (bf16[64,4352]{1,0:T(8,128)(2,1)}, bf16[64,4352]{1,0:T(8,128)(2,1)}) custom-call(bf16[6,64,128]{2,1,0:T(8,128)(2,1)} %bitcast.43, bf16[6,64,4096]{2,1,0:T(8,128)(2,1)} %weight_ref.1, bf16[6,4096]{1,0:T(8,128)(2,1)} %shift_ref.1, bf16[32,4096]{1,0:T(8,128)(2,1)} %bitcast.41), custom_call_target="tpu_custom_call" | custom-call | tf_op jit(solution)/shard_map/embed/pallas_call | solution.py:101
  19.5 3.3 %collective-permute-start = (bf16[64,4352]{1,0:T(8,128)(2,1)}, bf16[64,4352]{1,0:T(8,128)(2,1)S(1)}, u32[]{:S(2)}, u32[]{:S(2)}) collective-permute-start(bf16[64,4352]{1,0:T(8,128)(2,1)} %get-tuple-element.17), channel_id=1, source_target_pairs={{0,16},{16,0},{1,17},{17,1},{2,18},{18,2},{3,19},{19,3},{4,20},{20... | collective-permute-start | bytes 1671176 | tf_op jit(solution)/shard_map/ppermute | solution.py:358
  22.8 1.8 collective-permute-done.other_ref
  24.6 0.0 copy-start.2
  24.6 1.1 copy-done.2
  25.7 0.0 copy-start.3
  25.7 1.7 pair.1
  27.3 0.0 copy-done
  27.3 0.7 constant_dynamic-slice_fusion
  28.1 0.0 all-gather.5.cloned.1.call-update
  28.1 3.5 %all-to-all-start = ((bf16[8,8,4352]{2,1,0:T(8,128)(2,1)}), bf16[8,8,4352]{2,1,0:T(8,128)(2,1)S(1)}, u32[]{:S(2)}, u32[]{:S(2)}) async-start(bf16[8,8,4352]{2,1,0:T(8,128)(2,1)} %bitcast.2), calls=%async_computation | async-start | bytes 1114112 | tf_op jit(solution)/shard_map/all_to_all | solution.py:362
  31.7 0.0 copy-done.3
  31.7 9.6 %all-to-all-done = bf16[8,8,4352]{2,1,0:T(8,128)(2,1)S(1)} async-done(((bf16[8,8,4352]{2,1,0:T(8,128)(2,1)}), bf16[8,8,4352]{2,1,0:T(8,128)(2,1)S(1)}, u32[]{:S(2)}, u32[]{:S(2)}) %all-to-all-start) | async-done | bytes 557088 | tf_op jit(solution)/shard_map/all_to_all | solution.py:362
  41.3 0.8 merge.1
  42.1 12.4 %all_to_all.60 = bf16[8,8,4096]{2,1,0:T(8,128)(2,1)S(1)} all-to-all(bf16[8,8,4096]{2,1,0:T(8,128)(2,1)S(1)} %bitcast.32), channel_id=1, replica_groups=mesh['y'=4,'xl'=2,'c'=2,'xh'=2,'zq'=4,'z0'=2] {'y','xl'}, dimensions={0} | all-to-all | bytes 1048576 | tf_op jit(solution)/shard_map/all_to_all | solution.py:362
  54.5 1.9 %collective-permute-start.1 = (bf16[64,4096]{1,0:T(8,128)(2,1)S(1)}, bf16[64,4096]{1,0:T(8,128)(2,1)S(1)}, u32[]{:S(2)}, u32[]{:S(2)}) collective-permute-start(bf16[64,4096]{1,0:T(8,128)(2,1)S(1)} %bitcast.28), channel_id=1, source_target_pairs={{0,16},{16,0},{1,17},{17,1},{2,18},{18,2},{3,19},{19,3},{4,20},{20... | collective-permute-start | bytes 1572872 | tf_op jit(solution)/shard_map/ppermute | solution.py:358
  56.4 1.5 collective-permute-done.1.other_ref
  58.0 3.9 %project.1 = (bf16[2048,256]{1,0:T(8,128)(2,1)S(1)}, bf16[128,128]{1,0:T(8,128)(2,1)S(1)}, bf16[128,128]{1,0:T(8,128)(2,1)S(1)}) custom-call(bf16[64,4096]{1,0:T(8,128)(2,1)S(1)} %bitcast.29, bf16[64,4096]{1,0:T(8,128)(2,1)S(1)} %collective-permute-done.1.other_ref, bf16[3,4096,256]{2,1,0:T(8,128)(2,1)} %bitcast.35), custom_call_target="tpu_custom_call" | custom-call | tf_op jit(solution)/shard_map/project/pallas_call | solution.py:248
  61.9 0.0 copy-start.1
  61.9 1.0 copy-done.1
  62.9 10.3 %all-to-all-start.2 = ((bf16[16,128,256]{2,1,0:T(8,128)(2,1)}), bf16[16,128,256]{2,1,0:T(8,128)(2,1)S(1)}, u32[]{:S(2)}, u32[]{:S(2)}) async-start(bf16[16,128,256]{2,1,0:T(8,128)(2,1)} %bitcast.31), calls=%async_computation.2 | async-start | bytes 2097152 | tf_op jit(solution)/shard_map/all_to_all | solution.py:362
  73.2 1.4 collective-permute-start.2
  74.6 29.2 %all-gather.3.cloned.1.call-done = bf16[2048,384]{1,0:T(8,128)(2,1)} async-done(((bf16[128,384]{1,0:T(8,128)(2,1)}), bf16[2048,384]{1,0:T(8,128)(2,1)}) %all-gather.3.cloned.1.call-update) | async-done | bytes 1572880 | tf_op jit(solution)/shard_map/all_gather | solution.py:373
  103.8 4.0 %all-to-all-done.2 = bf16[16,128,256]{2,1,0:T(8,128)(2,1)S(1)} async-done(((bf16[16,128,256]{2,1,0:T(8,128)(2,1)}), bf16[16,128,256]{2,1,0:T(8,128)(2,1)S(1)}, u32[]{:S(2)}, u32[]{:S(2)}) %all-to-all-start.2) | async-done | bytes 1048608 | tf_op jit(solution)/shard_map/all_to_all | solution.py:362
  107.8 0.0 collective-permute-done.2.got_ref
  107.8 1.3 attend.1
  109.1 10.4 %all_to_all.61 = bf16[32,8,128]{2,1,0:T(8,128)(2,1)S(1)} all-to-all(bf16[32,8,128]{2,1,0:T(8,128)(2,1)S(1)} %bitcast.33), channel_id=1, replica_groups=mesh['y'=4,'xl'=2,'c'=2,'xh'=2,'zq'=4,'z0'=2] {'y','xl','c','z0'}, dimensions={0} | all-to-all | bytes 131072 | tf_op jit(solution)/shard_map/all_to_all | solution.py:362
  119.5 0.1 broadcast_in_dim.9
  119.7 26.8 %all_to_all.62.parts_ref = bf16[8,288,128]{2,1,0:T(8,128)(2,1)S(1)} all-to-all(bf16[8,288,128]{2,1,0:T(8,128)(2,1)S(1)} %pad_maximum_fusion), channel_id=1, replica_groups=mesh['y'=4,'xl'=2,'c'=2,'xh'=2,'zq'=4,'z0'=2] {'xh','zq'}, dimensions={0} | all-to-all | bytes 1179648 | tf_op jit(solution)/shard_map/all_to_all | solution.py:362
  146.4 5.2 %all-gather.5.cloned.1.call-done.weight_ref = bf16[4096,512]{1,0:T(8,128)(2,1)} async-done(((bf16[256,512]{1,0:T(8,128)(2,1)}), bf16[4096,512]{1,0:T(8,128)(2,1)}) %all-gather.5.cloned.1.call-update) | async-done | bytes 4194320 | tf_op jit(solution)/shard_map/all_gather | solution.py:375
  151.6 2.5 %output.1 = bf16[1024,256]{1,0:T(8,128)(2,1)S(1)} custom-call(bf16[8,288,128]{2,1,0:T(8,128)(2,1)S(1)} %all_to_all.62.parts_ref, bf16[4096,512]{1,0:T(8,128)(2,1)} %all-gather.5.cloned.1.call-done.weight_ref), custom_call_target="tpu_custom_call" | custom-call | tf_op jit(solution)/shard_map/output/pallas_call | solution.py:343
  154.1 13.0 %all_to_all.63 = bf16[16,64,256]{2,1,0:T(8,128)(2,1)S(1)} all-to-all(bf16[16,64,256]{2,1,0:T(8,128)(2,1)S(1)} %bitcast.30), channel_id=1, replica_groups=mesh['y'=4,'xl'=2,'c'=2,'xh'=2,'zq'=4,'z0'=2] {'y','xl','z0'}, dimensions={0} | all-to-all | bytes 1048576 | tf_op jit(solution)/shard_map/all_to_all | solution.py:362
  167.1 2.3 %collective-permute-start.3 = (bf16[1024,256]{1,0:T(8,128)(2,1)S(1)}, bf16[1024,256]{1,0:T(8,128)(2,1)S(1)}, u32[]{:S(2)}, u32[]{:S(2)}) collective-permute-start(bf16[1024,256]{1,0:T(8,128)(2,1)S(1)} %bitcast.38), channel_id=1, source_target_pairs={{0,16},{16,0},{1,17},{17,1},{2,18},{18,2},{3,19},{19,3},{4,20},{20... | collective-permute-start | bytes 1572872 | tf_op jit(solution)/shard_map/ppermute | solution.py:358
  169.4 1.7 copy.9
  171.1 0.5 fusion.1
  171.6 0.0 collective-permute-done.3
  171.6 1.2 convolution_add_fusion
  (2 shorter events, 0.1 us)
Async XLA Ops:
  6.5 20.8 %copy-start = (bf16[256,4096]{1,0:T(8,128)(2,1)S(1)}, bf16[256,4096]{1,0:T(8,128)(2,1)}, u32[]{:S(2)}) copy-start(bf16[256,4096]{1,0:T(8,128)(2,1)} %param.14) | copy-start | bytes 6291460
  6.5 97.3 %all-gather.3.cloned.1.call-start = ((), (), s32[]{:S(2)}) async-start(), calls=%async_computation.6 | async-start | bytes 1671168 | tf_op jit(solution)/shard_map/all_gather | solution.py:373
  7.3 144.4 %all-gather.5.cloned.1.call-start = ((), (), s32[]{:S(2)}) async-start(), calls=%async_computation.7 | async-start | bytes 4456448 | tf_op jit(solution)/shard_map/all_gather | solution.py:375
  19.5 5.1 %collective-permute-start = (bf16[64,4352]{1,0:T(8,128)(2,1)}, bf16[64,4352]{1,0:T(8,128)(2,1)S(1)}, u32[]{:S(2)}, u32[]{:S(2)}) collective-permute-start(bf16[64,4352]{1,0:T(8,128)(2,1)} %get-tuple-element.17), channel_id=1, source_target_pairs={{0,16},{16,0},{1,17},{17,1},{2,18},{18,2},{3,19},{19,3},{4,20},{20... | collective-permute-start | bytes 1671176 | tf_op jit(solution)/shard_map/ppermute | solution.py:358
  24.6 1.1 copy-start.2
  25.7 6.0 %copy-start.3 = (bf16[4096]{0:T(1024)(128)(2,1)S(1)}, bf16[4096]{0:T(1024)(128)(2,1)}, u32[]{:S(2)}) copy-start(bf16[4096]{0:T(1024)(128)(2,1)} %param.12) | copy-start | bytes 24580
  28.1 13.2 %all-to-all-start = ((bf16[8,8,4352]{2,1,0:T(8,128)(2,1)}), bf16[8,8,4352]{2,1,0:T(8,128)(2,1)S(1)}, u32[]{:S(2)}, u32[]{:S(2)}) async-start(bf16[8,8,4352]{2,1,0:T(8,128)(2,1)} %bitcast.2), calls=%async_computation | async-start | bytes 1114112 | tf_op jit(solution)/shard_map/all_to_all | solution.py:362
  54.5 3.4 %collective-permute-start.1 = (bf16[64,4096]{1,0:T(8,128)(2,1)S(1)}, bf16[64,4096]{1,0:T(8,128)(2,1)S(1)}, u32[]{:S(2)}, u32[]{:S(2)}) collective-permute-start(bf16[64,4096]{1,0:T(8,128)(2,1)S(1)} %bitcast.28), channel_id=1, source_target_pairs={{0,16},{16,0},{1,17},{17,1},{2,18},{18,2},{3,19},{19,3},{4,20},{20... | collective-permute-start | bytes 1572872 | tf_op jit(solution)/shard_map/ppermute | solution.py:358
  61.9 1.0 copy-start.1
  62.9 44.9 %all-to-all-start.2 = ((bf16[16,128,256]{2,1,0:T(8,128)(2,1)}), bf16[16,128,256]{2,1,0:T(8,128)(2,1)S(1)}, u32[]{:S(2)}, u32[]{:S(2)}) async-start(bf16[16,128,256]{2,1,0:T(8,128)(2,1)} %bitcast.31), calls=%async_computation.2 | async-start | bytes 2097152 | tf_op jit(solution)/shard_map/all_to_all | solution.py:362
  73.2 34.6 %collective-permute-start.2 = (bf16[128,128]{1,0:T(8,128)(2,1)S(1)}, bf16[128,128]{1,0:T(8,128)(2,1)S(1)}, u32[]{:S(2)}, u32[]{:S(2)}) collective-permute-start(bf16[128,128]{1,0:T(8,128)(2,1)S(1)} %get-tuple-element.21), channel_id=1, source_target_pairs={{0,1},{1,0},{2,3},{3,2},{4,5},{5,4},{6,7},{7,6},{8,9},{9,8},{10,11... | collective-permute-start | bytes 98312 | tf_op jit(solution)/shard_map/ppermute | solution.py:358
  167.1 4.5 %collective-permute-start.3 = (bf16[1024,256]{1,0:T(8,128)(2,1)S(1)}, bf16[1024,256]{1,0:T(8,128)(2,1)S(1)}, u32[]{:S(2)}, u32[]{:S(2)}) collective-permute-start(bf16[1024,256]{1,0:T(8,128)(2,1)S(1)} %bitcast.38), channel_id=1, source_target_pairs={{0,16},{16,0},{1,17},{17,1},{2,18},{18,2},{3,19},{19,3},{4,20},{20... | collective-permute-start | bytes 1572872 | tf_op jit(solution)/shard_map/ppermute | solution.py:358
Sparse Core Ops, SparseCore 0:
  9.9 93.8 all-gather.2
  105.7 45.9 all-gather.4

commit v6 on v5

--- a/solution.py
+++ b/solution.py
@@ -51,14 +51,23 @@
     return peak, total
 
 
-def embed_kernel(pixels_ref, weight_ref, shift_ref, query_ref, keep_ref, send_ref, embedded, scores, held, sems):
+def embed_kernel(
+    pixels_ref, weight_ref, shift_ref, query_ref, rows_ref, keep_ref, send_ref, cols_ref, embedded, scores, held, sems
+):
     core = lax.axis_index("c")
+    part = lax.axis_index("xh") * 4 + lax.axis_index("zq")
     count, rows, width = embedded.shape
     heads = query_ref.shape[0]
     half = rows // 2
     copies = [
         pltpu.make_async_copy(weight_ref.at[v], held.at[v], sems.at[v]) for v in range(count)
     ]
+    cut = cols_ref.shape[1]
+    copies.append(
+        pltpu.make_async_copy(
+            rows_ref.at[:, pl.ds(pl.multiple_of(part * cut, cut), cut)], cols_ref, sems.at[count]
+        )
+    )
     for copy in copies:
         copy.start()
     new = lax.broadcasted_iota(jnp.int32, (rows, rows), 0)
@@ -90,27 +99,30 @@
         send_ref[:, cols] = numer[half:].astype(BF16)
     keep_ref[:, width:] = packed(peak[:half], total[:half])
     send_ref[:, width:] = packed(peak[half:], total[half:])
-
-
-def embed(pixels, weight, shift, query):
+    copies[count].wait()
+
+
+def embed(pixels, weight, shift, query, out_weight):
     count, depth, rows = pixels.shape
     width = weight.shape[2]
     heads = query.shape[0]
     vmem = pl.BlockSpec(memory_space=pltpu.VMEM)
+    hbm = pl.BlockSpec(memory_space=pltpu.HBM)
     part = jax.ShapeDtypeStruct((rows // 2, width + 256), BF16)
     return pl.pallas_call(
         embed_kernel,
-        in_specs=[vmem, pl.BlockSpec(memory_space=pltpu.HBM), vmem, vmem],
-        out_shape=(part, part),
+        in_specs=[vmem, hbm, vmem, vmem, hbm],
+        out_specs=[vmem, vmem, hbm],
+        out_shape=(part, part, jax.ShapeDtypeStruct((out_weight.shape[0], width // 8), BF16)),
         scratch_shapes=[
             pltpu.VMEM((count, rows, width), BF16),
             pltpu.VMEM((count, rows, heads), F32),
             pltpu.VMEM((count, depth, width), BF16),
-            pltpu.SemaphoreType.DMA((count,)),
+            pltpu.SemaphoreType.DMA((count + 1,)),
         ],
         compiler_params=params(60),
         name="embed",
-    )(pixels, weight, shift, query)
+    )(pixels, weight, shift, query, out_weight)
 
 
 def pair_kernel(mine_ref, other_ref, out_ref):
@@ -139,7 +151,13 @@
     )(mine, other)
 
 
-def merge_kernel(parts_ref, gain_ref, normed_ref, kept_ref, whole):
+def merge_kernel(
+    parts_ref, gain_ref, cot_ref, cot_got_ref, normed_ref, kept_ref, cot_out_ref, whole
+):
+    x_hi = lax.axis_index("xh")
+    tokens = cot_ref.shape[0]
+    cot_out_ref[pl.ds(pl.multiple_of(x_hi * tokens, tokens), tokens), :] = cot_ref[...]
+    cot_out_ref[pl.ds(pl.multiple_of((1 - x_hi) * tokens, tokens), tokens), :] = cot_got_ref[...]
     rows, padded = parts_ref.shape
     width = padded - 256
     heads = width // HD
@@ -182,22 +200,24 @@
             normed_ref[at : at + 16, cols] = twice
 
 
-def merge(parts, gain, copies):
+def merge(parts, gain, copies, cot, cot_got):
     rows, padded = parts.shape
+    tokens, cols = cot.shape
     width = padded - 256
     return pl.pallas_call(
         merge_kernel,
         out_shape=(
             jax.ShapeDtypeStruct((copies * 8, width), BF16),
             jax.ShapeDtypeStruct((width // 16, HD), BF16),
+            jax.ShapeDtypeStruct((2 * tokens, cols), BF16),
         ),
         scratch_shapes=[pltpu.VMEM((8, width), F32)],
         compiler_params=params(12),
         name="merge",
-    )(parts, gain)
-
-
-def qkv_kernel(mine_ref, other_ref, weight_ref, kv_ref, keep_ref, send_ref, tokens, held, sems):
+    )(parts, gain, cot, cot_got)
+
+
+def qkv_kernel(mine_ref, other_ref, weight_ref, kv_ref, query_ref, tokens, held, sems):
     core = lax.axis_index("c")
     z0 = lax.axis_index("z0")
     half, width = mine_ref.shape
@@ -207,51 +227,47 @@
     copies = [
         [
             pltpu.make_async_copy(
-                weight_ref.at[k, pl.ds(part * depth, depth), :],
-                held.at[k, pl.ds(part * depth, depth), :],
+                weight_ref.at[k, pl.ds(part * depth, depth), pl.ds(pl.multiple_of(z0 * HD, HD), HD)],
+                held.at[pl.ds(part * depth, depth), pl.ds(k * HD, HD)],
                 sems.at[k, part],
             )
-            for part in range(parts)
+            for k in range(3)
         ]
-        for k in range(3)
+        for part in range(parts)
     ]
-    for k in range(3):
-        for copy in copies[k]:
+    for part in range(parts):
+        for copy in copies[part]:
             copy.start()
     tokens[pl.ds(pl.multiple_of(core * half, half), half), :] = mine_ref[...]
     tokens[pl.ds(pl.multiple_of((1 - core) * half, half), half), :] = other_ref[...]
-    for k in range(3):
-        made = jnp.zeros((rows, 2 * HD), F32)
-        for part in range(parts):
-            copies[k][part].wait()
-            at = slice(part * depth, (part + 1) * depth)
-            made = made + dot(tokens[:, at], held[k, at, :], NN)
-        first, second = made[:, :HD], made[:, HD:]
-        if k == 0:
-            keep_ref[...] = jnp.where(z0 == 0, first, second).astype(BF16)
-            send_ref[...] = jnp.where(z0 == 0, second, first).astype(BF16)
-        else:
-            cols = slice((k - 1) * HD, k * HD)
-            for to in range(16):
-                value = first if to % 2 == 0 else second
-                kv_ref[to * rows : (to + 1) * rows, cols] = value.astype(BF16)
-
-
-def project(mine, other, weight):
+    made = jnp.zeros((rows, 3 * HD), F32)
+    for part in range(parts):
+        for copy in copies[part]:
+            copy.wait()
+        at = slice(part * depth, (part + 1) * depth)
+        made = made + dot(tokens[:, at], held[at, :], NN)
+    made = made.astype(BF16)
+    query_ref[...] = made[:, :HD]
+    for to in range(kv_ref.shape[0] // rows):
+        kv_ref[to * rows : (to + 1) * rows, :] = made[:, HD:]
+
+
+def project(mine, other, weight, copies):
     half, width = mine.shape
-    cols = weight.shape[2]
     rows = 2 * half
     parts = 4
     vmem = pl.BlockSpec(memory_space=pltpu.VMEM)
     hbm = pl.BlockSpec(memory_space=pltpu.HBM)
-    shapes = [(16 * rows, 2 * HD), (rows, HD), (rows, HD)]
     return pl.pallas_call(
         qkv_kernel,
         in_specs=[vmem, vmem, hbm],
-        out_shape=[jax.ShapeDtypeStruct(shape, BF16) for shape in shapes],
+        out_shape=(
+            jax.ShapeDtypeStruct((copies * rows, 2 * HD), BF16),
+            jax.ShapeDtypeStruct((rows, HD), BF16),
+        ),
         scratch_shapes=[
             pltpu.VMEM((rows, width), BF16),
-            pltpu.VMEM((3, width, cols), BF16),
+            pltpu.VMEM((width, 3 * HD), BF16),
             pltpu.SemaphoreType.DMA((3, parts)),
         ],
         compiler_params=params(50),
@@ -259,37 +275,33 @@
     )(mine, other, weight)
 
 
-def attend_kernel(keep_ref, got_ref, kv_ref, out_ref, scores):
-    z0 = lax.axis_index("z0")
+def attend_kernel(query_ref, kv_ref, out_ref, scores):
     count = kv_ref.shape[0]
+    rows = scores.shape[0]
     step = 256
-    mixed = []
-    for side in range(2):
-        query = jnp.where(z0 == side, keep_ref[...], got_ref[...])
+    for core in range(2):
+        query = query_ref[core * rows : (core + 1) * rows, :]
         for at in range(0, count, step):
             scores[:, at : at + step] = dot(query, kv_ref[at : at + step, :HD], NT) / math.sqrt(HD)
         every = scores[...]
         peak = jnp.max(every, axis=1, keepdims=True)
         weights = jnp.exp(every - peak)
         total = jnp.sum(weights, axis=1, keepdims=True)
-        mixed.append(dot(weights.astype(BF16), kv_ref[:, HD:], NN) / total)
-    for chip in range(8):
-        for core in range(2):
-            at = core * 64 + chip * 8
+        mixed = (dot(weights.astype(BF16), kv_ref[:, HD:], NN) / total).astype(BF16)
+        for chip in range(8):
             to = (chip * 2 + core) * 16
-            out_ref[to : to + 16, :] = jnp.concatenate(
-                [mixed[0][at : at + 8], mixed[1][at : at + 8]], axis=0
-            ).astype(BF16)
-
-
-def attend(keep, got, kv):
+            out_ref[to : to + 16, :] = mixed[chip * 16 : chip * 16 + 16]
+
+
+def attend(query, kv):
+    rows = query.shape[0]
     return pl.pallas_call(
         attend_kernel,
-        out_shape=jax.ShapeDtypeStruct((256, HD), BF16),
-        scratch_shapes=[pltpu.VMEM((128, 2048), F32)],
+        out_shape=jax.ShapeDtypeStruct((rows, HD), BF16),
+        scratch_shapes=[pltpu.VMEM((rows // 2, kv.shape[0]), F32)],
         compiler_params=params(16),
         name="attend",
-    )(keep, got, kv)
+    )(query, kv)
 
 
 def output_kernel(parts_ref, weight_ref, out_ref, attended, held, sems):
@@ -366,29 +378,27 @@
     core = lax.axis_index("c")
     width = out_weight.shape[1]
 
-    keep, send = embed(patches.transpose(0, 2, 1), patch_weight, var_embed, agg_query.T)
+    cot_got = swap(head_cot, "xh")
+    keep, send, cols = embed(
+        patches.transpose(0, 2, 1), patch_weight, var_embed, agg_query.T, out_weight
+    )
+    cols = lax.all_gather(cols, VAR, axis=0, tiled=True)
     parts = pair(keep, swap(send, "c"))
-    parts, cols = lax.optimization_barrier((parts, out_weight))
-
-    cot = lax.all_gather(head_cot, SEQ, axis=0, tiled=True)
-    cols = lax.dynamic_slice_in_dim(cols, lax.axis_index(BANDS) * 512, 512, 1)
-    cols = lax.all_gather(cols, VAR, axis=0, tiled=True)
-
     parts = exchange(parts, CHIPS)
-    normed, kept = merge(parts, norm_gain.reshape(1, width), 8)
-    normed = exchange(normed, CHIPS)
-    kv, query, query_send = project(normed, swap(normed, "c"), qkv_weight.transpose(1, 0, 2))
-    query_got = swap(query_send, "z0")
-    kv, cot = lax.optimization_barrier((exchange(kv, SEQ), cot))
-    attended = attend(query, query_got, kv)
+    normed, kept, cot = merge(parts, norm_gain.reshape(1, width), 16, head_cot, cot_got)
+    cot = lax.all_gather(cot, ("zq", "z0"), axis=0, tiled=True)
+    normed = exchange(normed, CHIPS + ("z0",))
+    kv, query = project(normed, swap(normed, "c"), qkv_weight.transpose(1, 0, 2), 8)
+    kv, cols = lax.optimization_barrier((exchange(kv, BANDS), cols))
+    attended = attend(query, kv)
     attended = exchange(attended, VAR + ("z0",))
     sent = jnp.concatenate(
         [jnp.broadcast_to(attended[None], (8, 256, HD)), kept.reshape(8, 32, HD)], axis=1
     )
-    got = exchange(sent, BANDS)
+    got, cot = lax.optimization_barrier((exchange(sent, BANDS), cot))
     layer = output(got, cols)
     layer = exchange(layer, CHIPS + ("z0",))
-    cot = cot.reshape(8, 2, 8, 2, 8, 384).transpose(3, 2, 1, 0, 4, 5).reshape(2, 1024, 384)
+    cot = cot.reshape(4, 2, 2, 8, 2, 8, 384).transpose(4, 3, 1, 2, 0, 5, 6).reshape(2, 1024, 384)
     first = lax.dynamic_index_in_dim(cot, core, 0, keepdims=False)
     second = lax.dynamic_index_in_dim(cot, 1 - core, 0, keepdims=False)
     return dot(layer, first, TN) + dot(swap(layer, "c"), second, TN)

time: 180 us -> 187 us (1.039)
  waiting for transfers between devices: 52.1 us -> 68.7 us
  blocking collectives: 62.6 us -> 47.4 us
  starting transfers between devices: 22.8 us -> 30 us
  local copies, waits for them, and re-layouts: 4.51 us -> 1.42 us
    all_to_all x2 -> x3, waiting for transfers between devices: 13.6 us -> 51.6 us  [exchange(): return lax.all_to_all(x, axes, 0, 0, tiled=True)]
    all_gather x1, waiting for transfers between devices: 29.2 us -> 0.01 us  [body(): cot = lax.all_gather(cot, ('zq', 'z0'), axis=0, tiled=True)]
    all_to_all x4 -> x3, blocking collectives: 62.6 us -> 47.4 us  [exchange(): return lax.all_to_all(x, axes, 0, 0, tiled=True)]
    ppermute x4, waiting for transfers between devices: 3.34 us -> 16.4 us  [swap(): return lax.ppermute(x, axis, [(0, 1), (1, 0)])]
    all_gather x1, waiting for transfers between devices: 5.2 us -> 0.01 us  [body(): cols = lax.all_gather(cols, VAR, axis=0, tiled=True)]
    ppermute x4, starting transfers between devices: 8.92 us -> 12.6 us  [swap(): return lax.ppermute(x, axis, [(0, 1), (1, 0)])]
    all_to_all x2 -> x3, starting transfers between devices: 13.9 us -> 17.4 us  [exchange(): return lax.all_to_all(x, axes, 0, 0, tiled=True)]
  transfers between devices with their start and end apart: 8 -> 9, of which waited for: 6 -> 6; matrix products, arithmetic and copies ran while one was open for 2% -> 1% of each run, Pallas kernels for 11% -> 4%
where the time goes in v6:
time: 187 us
  waiting for transfers between devices  68.7 us (37%)
  blocking collectives  47.4 us (25%)
  starting transfers between devices  30 us (16%)
  Pallas kernels  23.2 us (12%)
  between operations  13.5 us (7%)
    all_to_all x3, waiting for transfers between devices, exchange(): return lax.all_to_all(x, axes, 0, 0, tiled=True)  51.6 us
    all_to_all x3, blocking collectives, exchange(): return lax.all_to_all(x, axes, 0, 0, tiled=True)  47.4 us
    all_to_all x3, starting transfers between devices, exchange(): return lax.all_to_all(x, axes, 0, 0, tiled=True)  17.4 us
    ppermute x4, waiting for transfers between devices, swap(): return lax.ppermute(x, axis, [(0, 1), (1, 0)])  16.4 us
    ppermute x4, starting transfers between devices, swap(): return lax.ppermute(x, axis, [(0, 1), (1, 0)])  12.6 us
    pallas_call x1, Pallas kernels, embed(): pl.pallas_call(embed_kernel, in_specs=[vmem, hbm, vmem, vmem, hbm], out_s...  12.2 us
    pallas_call x1, Pallas kernels, project(): pl.pallas_call(qkv_kernel, in_specs=[vmem, vmem, hbm], out_shape=(jax.Sha...  4.02 us
  transfers between devices with their start and end apart: 9, of which 6 were waited for; matrix products, arithmetic and copies ran while one was open for 1% of the time, Pallas kernels for 4%

profile of v6, /device:TPU:1, one launch (start us, length us, event | category | flops | bytes accessed | tf_op | source)
XLA Modules:
  0.0 186.8 jit_solution(10239297901712101222)
XLA Ops:
  6.5 0.0 all-gather.3.cloned.1.call-start
  6.5 12.2 %embed.1 = (bf16[64,4352]{1,0:T(8,128)(2,1)}, bf16[64,4352]{1,0:T(8,128)(2,1)}, bf16[256,512]{1,0:T(8,128)(2,1)}) custom-call(bf16[6,64,128]{2,1,0:T(8,128)(2,1)} %bitcast.42, bf16[6,64,4096]{2,1,0:T(8,128)(2,1)} %weight_ref.1, bf16[6,4096]{1,0:T(8,128)(2,1)} %shift_ref.1, bf16[32,4096]{1,0:T(8,128)(2,1)} %bitcast.40, bf16[256,4096]{1,0:T(8,128)(2,1)} %rows_ref.1), custom_call_target="tpu_custom_call" | custom-call | tf_op jit(solution)/shard_map/embed/pallas_call | solution.py:112
  18.8 0.0 copy-start.1
  18.8 0.0 copy-start.3
  18.8 0.0 all-gather.3.cloned.1.call-update
  18.8 3.3 %collective-permute-start = (bf16[64,4352]{1,0:T(8,128)(2,1)}, bf16[64,4352]{1,0:T(8,128)(2,1)S(1)}, u32[]{:S(2)}, u32[]{:S(2)}) collective-permute-start(bf16[64,4352]{1,0:T(8,128)(2,1)} %get-tuple-element.18), channel_id=1, source_target_pairs={{0,16},{16,0},{1,17},{17,1},{2,18},{18,2},{3,19},{19,3},{4,20},{20... | collective-permute-start | bytes 1671176 | tf_op jit(solution)/shard_map/ppermute | solution.py:370
  22.1 1.8 collective-permute-done.other_ref
  23.9 0.0 copy-start
  23.9 1.1 copy-done
  25.0 1.7 pair.1
  26.7 3.5 %all-to-all-start = ((bf16[8,8,4352]{2,1,0:T(8,128)(2,1)}), bf16[8,8,4352]{2,1,0:T(8,128)(2,1)S(1)}, u32[]{:S(2)}, u32[]{:S(2)}) async-start(bf16[8,8,4352]{2,1,0:T(8,128)(2,1)} %bitcast.2), calls=%async_computation | async-start | bytes 1114112 | tf_op jit(solution)/shard_map/all_to_all | solution.py:374
  30.2 0.0 copy-done.1
  30.2 2.4 %collective-permute-start.1 = (bf16[128,384]{1,0:T(8,128)(2,1)S(1)}, bf16[128,384]{1,0:T(8,128)(2,1)S(1)}, u32[]{:S(2)}, u32[]{:S(2)}) collective-permute-start(bf16[128,384]{1,0:T(8,128)(2,1)S(1)} %copy-done.1), channel_id=1, source_target_pairs={{0,8},{8,0},{1,9},{9,1},{2,10},{10,2},{3,11},{11,3},{4,12},{12,4},... | collective-permute-start | bytes 294920 | tf_op jit(solution)/shard_map/ppermute | solution.py:370
  32.6 0.0 copy-done.3
  32.6 11.5 %collective-permute-done.1.cot_got_ref = bf16[128,384]{1,0:T(8,128)(2,1)S(1)} collective-permute-done((bf16[128,384]{1,0:T(8,128)(2,1)S(1)}, bf16[128,384]{1,0:T(8,128)(2,1)S(1)}, u32[]{:S(2)}, u32[]{:S(2)}) %collective-permute-start.1) | collective-permute-done | bytes 98336 | tf_op jit(solution)/shard_map/ppermute | solution.py:370
  44.1 0.0 all-to-all-done
  44.1 1.4 merge.1
  45.5 25.0 %all_to_all.60 = bf16[16,8,4096]{2,1,0:T(8,128)(2,1)S(1)} all-to-all(bf16[16,8,4096]{2,1,0:T(8,128)(2,1)S(1)} %bitcast.31), channel_id=1, replica_groups=mesh['y'=4,'xl'=2,'c'=2,'xh'=2,'zq'=4,'z0'=2] {'y','xl','z0'}, dimensions={0} | all-to-all | bytes 2097152 | tf_op jit(solution)/shard_map/all_to_all | solution.py:374
  70.5 3.5 %collective-permute-start.2 = (bf16[128,4096]{1,0:T(8,128)(2,1)S(1)}, bf16[128,4096]{1,0:T(8,128)(2,1)S(1)}, u32[]{:S(2)}, u32[]{:S(2)}) collective-permute-start(bf16[128,4096]{1,0:T(8,128)(2,1)S(1)} %bitcast.27), channel_id=1, source_target_pairs={{0,16},{16,0},{1,17},{17,1},{2,18},{18,2},{3,19},{19,3},{4,20},{20... | collective-permute-start | bytes 3145736 | tf_op jit(solution)/shard_map/ppermute | solution.py:370
  74.1 2.3 %collective-permute-done.2.other_ref = bf16[128,4096]{1,0:T(8,128)(2,1)S(1)} collective-permute-done((bf16[128,4096]{1,0:T(8,128)(2,1)S(1)}, bf16[128,4096]{1,0:T(8,128)(2,1)S(1)}, u32[]{:S(2)}, u32[]{:S(2)}) %collective-permute-start.2) | collective-permute-done | bytes 1048608 | tf_op jit(solution)/shard_map/ppermute | solution.py:370
  76.3 4.0 %project.1 = (bf16[2048,256]{1,0:T(8,128)(2,1)}, bf16[256,128]{1,0:T(8,128)(2,1)S(1)}) custom-call(bf16[128,4096]{1,0:T(8,128)(2,1)S(1)} %bitcast.28, bf16[128,4096]{1,0:T(8,128)(2,1)S(1)} %collective-permute-done.2.other_ref, bf16[3,4096,256]{2,1,0:T(8,128)(2,1)} %bitcast.36), custom_call_target="tpu_custom_call" | custom-call | tf_op jit(solution)/shard_map/project/pallas_call | solution.py:261
  80.4 10.0 %all-to-all-start.2 = ((bf16[8,256,256]{2,1,0:T(8,128)(2,1)}), bf16[8,256,256]{2,1,0:T(8,128)(2,1)S(1)}, u32[]{:S(2)}, u32[]{:S(2)}) async-start(bf16[8,256,256]{2,1,0:T(8,128)(2,1)} %bitcast.7), calls=%async_computation.2 | async-start | bytes 2097152 | tf_op jit(solution)/shard_map/all_to_all | solution.py:374
  90.4 0.0 all-gather.5.cloned.1.call-start
  90.4 0.7 all-gather.5.cloned.1.call-update
  91.1 32.3 %all-to-all-done.2 = bf16[8,256,256]{2,1,0:T(8,128)(2,1)S(1)} async-done(((bf16[8,256,256]{2,1,0:T(8,128)(2,1)}), bf16[8,256,256]{2,1,0:T(8,128)(2,1)S(1)}, u32[]{:S(2)}, u32[]{:S(2)}) %all-to-all-start.2) | async-done | bytes 1048608 | tf_op jit(solution)/shard_map/all_to_all | solution.py:374
  123.4 0.0 all-gather.3.cloned.1.call-done.weight_ref
  123.4 1.3 attend.1
  124.7 12.6 %all_to_all.61 = bf16[32,8,128]{2,1,0:T(8,128)(2,1)S(1)} all-to-all(bf16[32,8,128]{2,1,0:T(8,128)(2,1)S(1)} %bitcast.32), channel_id=1, replica_groups=mesh['y'=4,'xl'=2,'c'=2,'xh'=2,'zq'=4,'z0'=2] {'y','xl','c','z0'}, dimensions={0} | all-to-all | bytes 131072 | tf_op jit(solution)/shard_map/all_to_all | solution.py:374
  137.3 0.1 broadcast_in_dim.9
  137.4 0.9 pad_maximum_fusion
  138.3 3.8 %all-to-all-start.4 = ((bf16[8,288,128]{2,1,0:T(8,128)(2,1)}), bf16[8,288,128]{2,1,0:T(8,128)(2,1)S(1)}, u32[]{:S(2)}, u32[]{:S(2)}) async-start(bf16[8,288,128]{2,1,0:T(8,128)(2,1)} %pad_maximum_fusion), calls=%async_computation.4 | async-start | bytes 1179648 | tf_op jit(solution)/shard_map/all_to_all | solution.py:374
  142.1 0.0 all-gather.5.cloned.1.call-done
  142.1 19.3 %all-to-all-done.4.parts_ref = bf16[8,288,128]{2,1,0:T(8,128)(2,1)S(1)} async-done(((bf16[8,288,128]{2,1,0:T(8,128)(2,1)}), bf16[8,288,128]{2,1,0:T(8,128)(2,1)S(1)}, u32[]{:S(2)}, u32[]{:S(2)}) %all-to-all-start.4) | async-done | bytes 589856 | tf_op jit(solution)/shard_map/all_to_all | solution.py:374
  161.5 0.0 copy-start.2
  161.5 2.6 %output.1 = bf16[1024,256]{1,0:T(8,128)(2,1)S(1)} custom-call(bf16[8,288,128]{2,1,0:T(8,128)(2,1)S(1)} %all-to-all-done.4.parts_ref, bf16[4096,512]{1,0:T(8,128)(2,1)} %all-gather.3.cloned.1.call-done.weight_ref), custom_call_target="tpu_custom_call" | custom-call | tf_op jit(solution)/shard_map/output/pallas_call | solution.py:355
  164.0 9.8 %all_to_all.62 = bf16[16,64,256]{2,1,0:T(8,128)(2,1)S(1)} all-to-all(bf16[16,64,256]{2,1,0:T(8,128)(2,1)S(1)} %bitcast.30), channel_id=1, replica_groups=mesh['y'=4,'xl'=2,'c'=2,'xh'=2,'zq'=4,'z0'=2] {'y','xl','z0'}, dimensions={0} | all-to-all | bytes 1048576 | tf_op jit(solution)/shard_map/all_to_all | solution.py:374
  173.9 3.3 %collective-permute-start.3 = (bf16[1024,256]{1,0:T(8,128)(2,1)S(1)}, bf16[1024,256]{1,0:T(8,128)(2,1)S(1)}, u32[]{:S(2)}, u32[]{:S(2)}) collective-permute-start(bf16[1024,256]{1,0:T(8,128)(2,1)S(1)} %bitcast.37), channel_id=1, source_target_pairs={{0,16},{16,0},{1,17},{17,1},{2,18},{18,2},{3,19},{19,3},{4,20},{20... | collective-permute-start | bytes 1572872 | tf_op jit(solution)/shard_map/ppermute | solution.py:370
  177.2 0.0 copy-done.2
  177.2 0.3 copy.9
  177.5 0.5 fusion.1
  178.0 0.8 collective-permute-done.3
  178.7 1.2 convolution_add_fusion
  (1 shorter events, 0.0 us)
Async XLA Ops:
  6.5 116.9 %all-gather.3.cloned.1.call-start = ((), (), s32[]{:S(2)}) async-start(), calls=%async_computation.6 | async-start | bytes 4456448 | tf_op jit(solution)/shard_map/all_gather | solution.py:385
  18.8 11.4 %copy-start.1 = (bf16[128,384]{1,0:T(8,128)(2,1)S(1)}, bf16[128,384]{1,0:T(8,128)(2,1)}, u32[]{:S(2)}) copy-start(bf16[128,384]{1,0:T(8,128)(2,1)} %cot_ref.1) | copy-start | bytes 294916
  18.8 13.8 %copy-start.3 = (bf16[4096]{0:T(1024)(128)(2,1)S(1)}, bf16[4096]{0:T(1024)(128)(2,1)}, u32[]{:S(2)}) copy-start(bf16[4096]{0:T(1024)(128)(2,1)} %param.12) | copy-start | bytes 24580
  18.8 5.1 %collective-permute-start = (bf16[64,4352]{1,0:T(8,128)(2,1)}, bf16[64,4352]{1,0:T(8,128)(2,1)S(1)}, u32[]{:S(2)}, u32[]{:S(2)}) collective-permute-start(bf16[64,4352]{1,0:T(8,128)(2,1)} %get-tuple-element.18), channel_id=1, source_target_pairs={{0,16},{16,0},{1,17},{17,1},{2,18},{18,2},{3,19},{19,3},{4,20},{20... | collective-permute-start | bytes 1671176 | tf_op jit(solution)/shard_map/ppermute | solution.py:370
  23.9 1.1 copy-start
  26.7 17.5 %all-to-all-start = ((bf16[8,8,4352]{2,1,0:T(8,128)(2,1)}), bf16[8,8,4352]{2,1,0:T(8,128)(2,1)S(1)}, u32[]{:S(2)}, u32[]{:S(2)}) async-start(bf16[8,8,4352]{2,1,0:T(8,128)(2,1)} %bitcast.2), calls=%async_computation | async-start | bytes 1114112 | tf_op jit(solution)/shard_map/all_to_all | solution.py:374
  30.2 13.9 %collective-permute-start.1 = (bf16[128,384]{1,0:T(8,128)(2,1)S(1)}, bf16[128,384]{1,0:T(8,128)(2,1)S(1)}, u32[]{:S(2)}, u32[]{:S(2)}) collective-permute-start(bf16[128,384]{1,0:T(8,128)(2,1)S(1)} %copy-done.1), channel_id=1, source_target_pairs={{0,8},{8,0},{1,9},{9,1},{2,10},{10,2},{3,11},{11,3},{4,12},{12,4},... | collective-permute-start | bytes 294920 | tf_op jit(solution)/shard_map/ppermute | solution.py:370
  70.5 5.8 %collective-permute-start.2 = (bf16[128,4096]{1,0:T(8,128)(2,1)S(1)}, bf16[128,4096]{1,0:T(8,128)(2,1)S(1)}, u32[]{:S(2)}, u32[]{:S(2)}) collective-permute-start(bf16[128,4096]{1,0:T(8,128)(2,1)S(1)} %bitcast.27), channel_id=1, source_target_pairs={{0,16},{16,0},{1,17},{17,1},{2,18},{18,2},{3,19},{19,3},{4,20},{20... | collective-permute-start | bytes 3145736 | tf_op jit(solution)/shard_map/ppermute | solution.py:370
  80.4 43.0 %all-to-all-start.2 = ((bf16[8,256,256]{2,1,0:T(8,128)(2,1)}), bf16[8,256,256]{2,1,0:T(8,128)(2,1)S(1)}, u32[]{:S(2)}, u32[]{:S(2)}) async-start(bf16[8,256,256]{2,1,0:T(8,128)(2,1)} %bitcast.7), calls=%async_computation.2 | async-start | bytes 2097152 | tf_op jit(solution)/shard_map/all_to_all | solution.py:374
  90.4 51.7 %all-gather.5.cloned.1.call-start = ((), (), s32[]{:S(2)}) async-start(), calls=%async_computation.7 | async-start | bytes 1769472 | tf_op jit(solution)/shard_map/all_gather | solution.py:389
  138.3 23.2 %all-to-all-start.4 = ((bf16[8,288,128]{2,1,0:T(8,128)(2,1)}), bf16[8,288,128]{2,1,0:T(8,128)(2,1)S(1)}, u32[]{:S(2)}, u32[]{:S(2)}) async-start(bf16[8,288,128]{2,1,0:T(8,128)(2,1)} %pad_maximum_fusion), calls=%async_computation.4 | async-start | bytes 1179648 | tf_op jit(solution)/shard_map/all_to_all | solution.py:374
  161.5 15.8 %copy-start.2 = (bf16[2048,384]{1,0:T(8,128)(2,1)S(1)}, bf16[2048,384]{1,0:T(8,128)(2,1)}, u32[]{:S(2)}) copy-start(bf16[2048,384]{1,0:T(8,128)(2,1)} %all-gather.5.cloned.1.call-done) | copy-start | bytes 4718596
  173.9 4.9 %collective-permute-start.3 = (bf16[1024,256]{1,0:T(8,128)(2,1)S(1)}, bf16[1024,256]{1,0:T(8,128)(2,1)S(1)}, u32[]{:S(2)}, u32[]{:S(2)}) collective-permute-start(bf16[1024,256]{1,0:T(8,128)(2,1)S(1)} %bitcast.37), channel_id=1, source_target_pairs={{0,16},{16,0},{1,17},{17,1},{2,18},{18,2},{3,19},{19,3},{4,20},{20... | collective-permute-start | bytes 1572872 | tf_op jit(solution)/shard_map/ppermute | solution.py:370
Sparse Core Ops, SparseCore 0:
  18.9 57.8 all-gather.2
  93.0 43.3 all-gather.4

commit v7 on v6

--- a/solution.py
+++ b/solution.py
@@ -125,7 +125,11 @@
     )(pixels, weight, shift, query, out_weight)
 
 
-def pair_kernel(mine_ref, other_ref, out_ref):
+def pair_kernel(mine_ref, other_ref, cot_ref, cot_got_ref, out_ref, cot_out_ref):
+    x_hi = lax.axis_index("xh")
+    tokens = cot_ref.shape[0]
+    cot_out_ref[pl.ds(pl.multiple_of(x_hi * tokens, tokens), tokens), :] = cot_ref[...]
+    cot_out_ref[pl.ds(pl.multiple_of((1 - x_hi) * tokens, tokens), tokens), :] = cot_got_ref[...]
     rows, padded = mine_ref.shape
     width = padded - 256
     heads = width // HD
@@ -142,22 +146,20 @@
     out_ref[:, width:] = packed(top, total_a * scale_a + total_b * scale_b)
 
 
-def pair(mine, other):
+def pair(mine, other, cot, cot_got):
+    tokens, cols = cot.shape
     return pl.pallas_call(
         pair_kernel,
-        out_shape=jax.ShapeDtypeStruct(other.shape, BF16),
+        out_shape=(
+            jax.ShapeDtypeStruct(other.shape, BF16),
+            jax.ShapeDtypeStruct((2 * tokens, cols), BF16),
+        ),
         compiler_params=params(12),
         name="pair",
-    )(mine, other)
-
-
-def merge_kernel(
-    parts_ref, gain_ref, cot_ref, cot_got_ref, normed_ref, kept_ref, cot_out_ref, whole
-):
-    x_hi = lax.axis_index("xh")
-    tokens = cot_ref.shape[0]
-    cot_out_ref[pl.ds(pl.multiple_of(x_hi * tokens, tokens), tokens), :] = cot_ref[...]
-    cot_out_ref[pl.ds(pl.multiple_of((1 - x_hi) * tokens, tokens), tokens), :] = cot_got_ref[...]
+    )(mine, other, cot, cot_got)
+
+
+def merge_kernel(parts_ref, gain_ref, normed_ref, kept_ref, whole):
     rows, padded = parts_ref.shape
     width = padded - 256
     heads = width // HD
@@ -200,21 +202,19 @@
             normed_ref[at : at + 16, cols] = twice
 
 
-def merge(parts, gain, copies, cot, cot_got):
+def merge(parts, gain, copies):
     rows, padded = parts.shape
-    tokens, cols = cot.shape
     width = padded - 256
     return pl.pallas_call(
         merge_kernel,
         out_shape=(
             jax.ShapeDtypeStruct((copies * 8, width), BF16),
             jax.ShapeDtypeStruct((width // 16, HD), BF16),
-            jax.ShapeDtypeStruct((2 * tokens, cols), BF16),
         ),
         scratch_shapes=[pltpu.VMEM((8, width), F32)],
         compiler_params=params(12),
         name="merge",
-    )(parts, gain, cot, cot_got)
+    )(parts, gain)
 
 
 def qkv_kernel(mine_ref, other_ref, weight_ref, kv_ref, query_ref, tokens, held, sems):
@@ -382,20 +382,20 @@
     keep, send, cols = embed(
         patches.transpose(0, 2, 1), patch_weight, var_embed, agg_query.T, out_weight
     )
+    parts, cot = pair(keep, swap(send, "c"), head_cot, cot_got)
+    cot = lax.all_gather(cot, ("zq", "z0"), axis=0, tiled=True)
+    parts, cols = lax.optimization_barrier((exchange(parts, CHIPS), cols))
     cols = lax.all_gather(cols, VAR, axis=0, tiled=True)
-    parts = pair(keep, swap(send, "c"))
-    parts = exchange(parts, CHIPS)
-    normed, kept, cot = merge(parts, norm_gain.reshape(1, width), 16, head_cot, cot_got)
-    cot = lax.all_gather(cot, ("zq", "z0"), axis=0, tiled=True)
+    normed, kept = merge(parts, norm_gain.reshape(1, width), 16)
     normed = exchange(normed, CHIPS + ("z0",))
     kv, query = project(normed, swap(normed, "c"), qkv_weight.transpose(1, 0, 2), 8)
-    kv, cols = lax.optimization_barrier((exchange(kv, BANDS), cols))
+    kv, cot = lax.optimization_barrier((exchange(kv, BANDS), cot))
     attended = attend(query, kv)
     attended = exchange(attended, VAR + ("z0",))
     sent = jnp.concatenate(
         [jnp.broadcast_to(attended[None], (8, 256, HD)), kept.reshape(8, 32, HD)], axis=1
     )
-    got, cot = lax.optimization_barrier((exchange(sent, BANDS), cot))
+    got = exchange(sent, BANDS)
     layer = output(got, cols)
     layer = exchange(layer, CHIPS + ("z0",))
     cot = cot.reshape(4, 2, 2, 8, 2, 8, 384).transpose(4, 3, 1, 2, 0, 5, 6).reshape(2, 1024, 384)

time: 187 us -> 182 us (0.973)
  blocking collectives: 47.4 us -> 88.7 us
  waiting for transfers between devices: 68.7 us -> 33.3 us
  starting transfers between devices: 30 us -> 20 us
    all_to_all x3 -> x5, blocking collectives: 47.4 us -> 88.7 us  [exchange(): return lax.all_to_all(x, axes, 0, 0, tiled=True)]
    all_to_all x3 -> x1, waiting for transfers between devices: 51.6 us -> 25.4 us  [exchange(): return lax.all_to_all(x, axes, 0, 0, tiled=True)]
    ppermute x4, waiting for transfers between devices: 16.4 us -> 7.89 us  [swap(): return lax.ppermute(x, axis, [(0, 1), (1, 0)])]
    all_to_all x3 -> x1, starting transfers between devices: 17.4 us -> 9.46 us  [exchange(): return lax.all_to_all(x, axes, 0, 0, tiled=True)]
    ppermute x4, starting transfers between devices: 12.6 us -> 10.5 us  [swap(): return lax.ppermute(x, axis, [(0, 1), (1, 0)])]
  transfers between devices with their start and end apart: 9 -> 7, of which waited for: 6 -> 4; matrix products, arithmetic and copies ran while one was open for 1% -> 0% of each run, Pallas kernels for 4% -> 3%
where the time goes in v7:
time: 182 us; the launch traced here: 181 us
  blocking collectives  88.7 us (49%)
  waiting for transfers between devices  33.3 us (18%)
  Pallas kernels  22.6 us (12%)
  starting transfers between devices  20 us (11%)
  between operations  13.5 us (7%)
    all_to_all x5, blocking collectives, exchange(): return lax.all_to_all(x, axes, 0, 0, tiled=True)  88.7 us
    all_to_all x1, waiting for transfers between devices, exchange(): return lax.all_to_all(x, axes, 0, 0, tiled=True)  25.4 us
    pallas_call x1, Pallas kernels, embed(): pl.pallas_call(embed_kernel, in_specs=[vmem, hbm, vmem, vmem, hbm], out_s...  12.3 us
    ppermute x4, starting transfers between devices, swap(): return lax.ppermute(x, axis, [(0, 1), (1, 0)])  10.5 us
    all_to_all x1, starting transfers between devices, exchange(): return lax.all_to_all(x, axes, 0, 0, tiled=True)  9.46 us
    ppermute x4, waiting for transfers between devices, swap(): return lax.ppermute(x, axis, [(0, 1), (1, 0)])  7.89 us
    pallas_call x1, Pallas kernels, project(): pl.pallas_call(qkv_kernel, in_specs=[vmem, vmem, hbm], out_shape=(jax.Sha...  4.01 us
  transfers between devices with their start and end apart: 7, of which 4 were waited for; matrix products, arithmetic and copies ran while one was open for 0% of the time, Pallas kernels for 3%

profile of v7, /device:TPU:1, one launch (start us, length us, event | category | flops | bytes accessed | tf_op | source)
XLA Modules:
  0.0 181.3 jit_solution(5183049484570595323)
XLA Ops:
  6.5 0.0 all-gather.3.cloned.1.call-start
  6.5 0.0 copy-start.1
  6.5 0.0 copy-start.3
  6.5 12.3 %embed.1 = (bf16[64,4352]{1,0:T(8,128)(2,1)}, bf16[64,4352]{1,0:T(8,128)(2,1)}, bf16[256,512]{1,0:T(8,128)(2,1)}) custom-call(bf16[6,64,128]{2,1,0:T(8,128)(2,1)} %bitcast.43, bf16[6,64,4096]{2,1,0:T(8,128)(2,1)} %weight_ref.1, bf16[6,4096]{1,0:T(8,128)(2,1)} %shift_ref.1, bf16[32,4096]{1,0:T(8,128)(2,1)} %bitcast.41, bf16[256,4096]{1,0:T(8,128)(2,1)} %rows_ref.1), custom_call_target="tpu_custom_call" | custom-call | tf_op jit(solution)/shard_map/embed/pallas_call | solution.py:112
  18.8 3.3 %collective-permute-start = (bf16[64,4352]{1,0:T(8,128)(2,1)}, bf16[64,4352]{1,0:T(8,128)(2,1)S(1)}, u32[]{:S(2)}, u32[]{:S(2)}) collective-permute-start(bf16[64,4352]{1,0:T(8,128)(2,1)} %get-tuple-element.19), channel_id=1, source_target_pairs={{0,16},{16,0},{1,17},{17,1},{2,18},{18,2},{3,19},{19,3},{4,20},{20... | collective-permute-start | bytes 1671176 | tf_op jit(solution)/shard_map/ppermute | solution.py:370
  22.1 0.0 copy-done.1
  22.1 1.0 collective-permute-start.1
  23.2 4.8 %collective-permute-done.1.cot_got_ref = bf16[128,384]{1,0:T(8,128)(2,1)S(1)} collective-permute-done((bf16[128,384]{1,0:T(8,128)(2,1)S(1)}, bf16[128,384]{1,0:T(8,128)(2,1)S(1)}, u32[]{:S(2)}, u32[]{:S(2)}) %collective-permute-start.1) | collective-permute-done | bytes 98336 | tf_op jit(solution)/shard_map/ppermute | solution.py:370
  28.0 0.0 collective-permute-done.other_ref
  28.0 0.0 copy-start
  28.0 1.1 copy-done
  29.1 1.5 pair.1
  30.5 0.0 all-gather.3.cloned.1.call-update
  30.6 0.0 all-gather.5.cloned.1.call-start
  30.6 12.5 %all_to_all.61 = bf16[8,8,4352]{2,1,0:T(8,128)(2,1)S(1)} all-to-all(bf16[8,8,4352]{2,1,0:T(8,128)(2,1)S(1)} %bitcast.32), channel_id=1, replica_groups=mesh['y'=4,'xl'=2,'c'=2,'xh'=2,'zq'=4,'z0'=2] {'y','xl'}, dimensions={0} | all-to-all | bytes 1114112 | tf_op jit(solution)/shard_map/all_to_all | solution.py:374
  43.1 0.0 all-gather.5.cloned.1.call-update
  43.1 0.0 copy-done.3
  43.2 1.0 merge.1
  44.1 26.3 %all_to_all.62 = bf16[16,8,4096]{2,1,0:T(8,128)(2,1)S(1)} all-to-all(bf16[16,8,4096]{2,1,0:T(8,128)(2,1)S(1)} %bitcast.31), channel_id=1, replica_groups=mesh['y'=4,'xl'=2,'c'=2,'xh'=2,'zq'=4,'z0'=2] {'y','xl','z0'}, dimensions={0} | all-to-all | bytes 2097152 | tf_op jit(solution)/shard_map/all_to_all | solution.py:374
  70.4 2.6 %collective-permute-start.2 = (bf16[128,4096]{1,0:T(8,128)(2,1)S(1)}, bf16[128,4096]{1,0:T(8,128)(2,1)S(1)}, u32[]{:S(2)}, u32[]{:S(2)}) collective-permute-start(bf16[128,4096]{1,0:T(8,128)(2,1)S(1)} %bitcast.27), channel_id=1, source_target_pairs={{0,16},{16,0},{1,17},{17,1},{2,18},{18,2},{3,19},{19,3},{4,20},{20... | collective-permute-start | bytes 3145736 | tf_op jit(solution)/shard_map/ppermute | solution.py:370
  73.0 2.3 %collective-permute-done.2.other_ref = bf16[128,4096]{1,0:T(8,128)(2,1)S(1)} collective-permute-done((bf16[128,4096]{1,0:T(8,128)(2,1)S(1)}, bf16[128,4096]{1,0:T(8,128)(2,1)S(1)}, u32[]{:S(2)}, u32[]{:S(2)}) %collective-permute-start.2) | collective-permute-done | bytes 1048608 | tf_op jit(solution)/shard_map/ppermute | solution.py:370
  75.3 4.0 %project.1 = (bf16[2048,256]{1,0:T(8,128)(2,1)}, bf16[256,128]{1,0:T(8,128)(2,1)S(1)}) custom-call(bf16[128,4096]{1,0:T(8,128)(2,1)S(1)} %bitcast.28, bf16[128,4096]{1,0:T(8,128)(2,1)S(1)} %collective-permute-done.2.other_ref, bf16[3,4096,256]{2,1,0:T(8,128)(2,1)} %bitcast.37), custom_call_target="tpu_custom_call" | custom-call | tf_op jit(solution)/shard_map/project/pallas_call | solution.py:261
  79.3 9.5 %all-to-all-start.2 = ((bf16[8,256,256]{2,1,0:T(8,128)(2,1)}), bf16[8,256,256]{2,1,0:T(8,128)(2,1)S(1)}, u32[]{:S(2)}, u32[]{:S(2)}) async-start(bf16[8,256,256]{2,1,0:T(8,128)(2,1)} %bitcast.7), calls=%async_computation.2 | async-start | bytes 2097152 | tf_op jit(solution)/shard_map/all_to_all | solution.py:374
  88.8 0.0 all-gather.3.cloned.1.call-done
  88.8 25.4 %all-to-all-done.2 = bf16[8,256,256]{2,1,0:T(8,128)(2,1)S(1)} async-done(((bf16[8,256,256]{2,1,0:T(8,128)(2,1)}), bf16[8,256,256]{2,1,0:T(8,128)(2,1)S(1)}, u32[]{:S(2)}, u32[]{:S(2)}) %all-to-all-start.2) | async-done | bytes 1048608 | tf_op jit(solution)/shard_map/all_to_all | solution.py:374
  114.1 1.3 attend.1
  115.5 18.3 %all_to_all.63 = bf16[32,8,128]{2,1,0:T(8,128)(2,1)S(1)} all-to-all(bf16[32,8,128]{2,1,0:T(8,128)(2,1)S(1)} %bitcast.33), channel_id=1, replica_groups=mesh['y'=4,'xl'=2,'c'=2,'xh'=2,'zq'=4,'z0'=2] {'y','xl','c','z0'}, dimensions={0} | all-to-all | bytes 131072 | tf_op jit(solution)/shard_map/all_to_all | solution.py:374
  133.8 0.1 broadcast_in_dim.9
  133.9 21.8 %all_to_all.64.parts_ref = bf16[8,288,128]{2,1,0:T(8,128)(2,1)S(1)} all-to-all(bf16[8,288,128]{2,1,0:T(8,128)(2,1)S(1)} %pad_maximum_fusion), channel_id=1, replica_groups=mesh['y'=4,'xl'=2,'c'=2,'xh'=2,'zq'=4,'z0'=2] {'xh','zq'}, dimensions={0} | all-to-all | bytes 1179648 | tf_op jit(solution)/shard_map/all_to_all | solution.py:374
  155.7 0.0 all-gather.5.cloned.1.call-done.weight_ref
  155.7 0.0 copy-start.2
  155.7 2.6 %output.1 = bf16[1024,256]{1,0:T(8,128)(2,1)S(1)} custom-call(bf16[8,288,128]{2,1,0:T(8,128)(2,1)S(1)} %all_to_all.64.parts_ref, bf16[4096,512]{1,0:T(8,128)(2,1)} %all-gather.5.cloned.1.call-done.weight_ref), custom_call_target="tpu_custom_call" | custom-call | tf_op jit(solution)/shard_map/output/pallas_call | solution.py:355
  158.3 9.9 %all_to_all.65 = bf16[16,64,256]{2,1,0:T(8,128)(2,1)S(1)} all-to-all(bf16[16,64,256]{2,1,0:T(8,128)(2,1)S(1)} %bitcast.30), channel_id=1, replica_groups=mesh['y'=4,'xl'=2,'c'=2,'xh'=2,'zq'=4,'z0'=2] {'y','xl','z0'}, dimensions={0} | all-to-all | bytes 1048576 | tf_op jit(solution)/shard_map/all_to_all | solution.py:374
  168.1 3.6 %collective-permute-start.3 = (bf16[1024,256]{1,0:T(8,128)(2,1)S(1)}, bf16[1024,256]{1,0:T(8,128)(2,1)S(1)}, u32[]{:S(2)}, u32[]{:S(2)}) collective-permute-start(bf16[1024,256]{1,0:T(8,128)(2,1)S(1)} %bitcast.38), channel_id=1, source_target_pairs={{0,16},{16,0},{1,17},{17,1},{2,18},{18,2},{3,19},{19,3},{4,20},{20... | collective-permute-start | bytes 1572872 | tf_op jit(solution)/shard_map/ppermute | solution.py:370
  171.7 0.0 copy-done.2
  171.7 0.3 copy.9
  172.0 0.5 fusion.1
  172.5 0.8 collective-permute-done.3
  173.2 1.2 convolution_add_fusion
  (2 shorter events, 0.1 us)
Async XLA Ops:
  6.5 82.2 %all-gather.3.cloned.1.call-start = ((), (), s32[]{:S(2)}) async-start(), calls=%async_computation.6 | async-start | bytes 1769472 | tf_op jit(solution)/shard_map/all_gather | solution.py:386
  6.5 15.6 %copy-start.1 = (bf16[128,384]{1,0:T(8,128)(2,1)S(1)}, bf16[128,384]{1,0:T(8,128)(2,1)}, u32[]{:S(2)}) copy-start(bf16[128,384]{1,0:T(8,128)(2,1)} %cot_ref.1) | copy-start | bytes 294916
  6.5 36.6 %copy-start.3 = (bf16[4096]{0:T(1024)(128)(2,1)S(1)}, bf16[4096]{0:T(1024)(128)(2,1)}, u32[]{:S(2)}) copy-start(bf16[4096]{0:T(1024)(128)(2,1)} %param.12) | copy-start | bytes 24580
  18.8 9.2 %collective-permute-start = (bf16[64,4352]{1,0:T(8,128)(2,1)}, bf16[64,4352]{1,0:T(8,128)(2,1)S(1)}, u32[]{:S(2)}, u32[]{:S(2)}) collective-permute-start(bf16[64,4352]{1,0:T(8,128)(2,1)} %get-tuple-element.19), channel_id=1, source_target_pairs={{0,16},{16,0},{1,17},{17,1},{2,18},{18,2},{3,19},{19,3},{4,20},{20... | collective-permute-start | bytes 1671176 | tf_op jit(solution)/shard_map/ppermute | solution.py:370
  22.1 5.9 %collective-permute-start.1 = (bf16[128,384]{1,0:T(8,128)(2,1)S(1)}, bf16[128,384]{1,0:T(8,128)(2,1)S(1)}, u32[]{:S(2)}, u32[]{:S(2)}) collective-permute-start(bf16[128,384]{1,0:T(8,128)(2,1)S(1)} %copy-done.1), channel_id=1, source_target_pairs={{0,8},{8,0},{1,9},{9,1},{2,10},{10,2},{3,11},{11,3},{4,12},{12,4},... | collective-permute-start | bytes 294920 | tf_op jit(solution)/shard_map/ppermute | solution.py:370
  28.0 1.1 copy-start
  30.6 125.1 %all-gather.5.cloned.1.call-start = ((), (), s32[]{:S(2)}) async-start(), calls=%async_computation.7 | async-start | bytes 4456448 | tf_op jit(solution)/shard_map/all_gather | solution.py:388
  70.4 4.9 %collective-permute-start.2 = (bf16[128,4096]{1,0:T(8,128)(2,1)S(1)}, bf16[128,4096]{1,0:T(8,128)(2,1)S(1)}, u32[]{:S(2)}, u32[]{:S(2)}) collective-permute-start(bf16[128,4096]{1,0:T(8,128)(2,1)S(1)} %bitcast.27), channel_id=1, source_target_pairs={{0,16},{16,0},{1,17},{17,1},{2,18},{18,2},{3,19},{19,3},{4,20},{20... | collective-permute-start | bytes 3145736 | tf_op jit(solution)/shard_map/ppermute | solution.py:370
  79.3 34.9 %all-to-all-start.2 = ((bf16[8,256,256]{2,1,0:T(8,128)(2,1)}), bf16[8,256,256]{2,1,0:T(8,128)(2,1)S(1)}, u32[]{:S(2)}, u32[]{:S(2)}) async-start(bf16[8,256,256]{2,1,0:T(8,128)(2,1)} %bitcast.7), calls=%async_computation.2 | async-start | bytes 2097152 | tf_op jit(solution)/shard_map/all_to_all | solution.py:374
  155.7 16.0 %copy-start.2 = (bf16[2048,384]{1,0:T(8,128)(2,1)S(1)}, bf16[2048,384]{1,0:T(8,128)(2,1)}, u32[]{:S(2)}) copy-start(bf16[2048,384]{1,0:T(8,128)(2,1)} %all-gather.3.cloned.1.call-done) | copy-start | bytes 4718596
  168.1 5.1 %collective-permute-start.3 = (bf16[1024,256]{1,0:T(8,128)(2,1)S(1)}, bf16[1024,256]{1,0:T(8,128)(2,1)S(1)}, u32[]{:S(2)}, u32[]{:S(2)}) collective-permute-start(bf16[1024,256]{1,0:T(8,128)(2,1)S(1)} %bitcast.38), channel_id=1, source_target_pairs={{0,16},{16,0},{1,17},{17,1},{2,18},{18,2},{3,19},{19,3},{4,20},{20... | collective-permute-start | bytes 1572872 | tf_op jit(solution)/shard_map/ppermute | solution.py:370
Sparse Core Ops, SparseCore 0:
  30.7 42.4 all-gather.2
  75.1 48.2 all-gather.4

commit v8 on v5

--- a/solution.py
+++ b/solution.py
@@ -51,14 +51,23 @@
     return peak, total
 
 
-def embed_kernel(pixels_ref, weight_ref, shift_ref, query_ref, keep_ref, send_ref, embedded, scores, held, sems):
+def embed_kernel(
+    pixels_ref, weight_ref, shift_ref, query_ref, rows_ref, keep_ref, send_ref, cols_ref, embedded, scores, held, sems
+):
     core = lax.axis_index("c")
+    part = lax.axis_index("xh") * 4 + lax.axis_index("zq")
     count, rows, width = embedded.shape
     heads = query_ref.shape[0]
     half = rows // 2
     copies = [
         pltpu.make_async_copy(weight_ref.at[v], held.at[v], sems.at[v]) for v in range(count)
     ]
+    cut = cols_ref.shape[1]
+    copies.append(
+        pltpu.make_async_copy(
+            rows_ref.at[:, pl.ds(pl.multiple_of(part * cut, cut), cut)], cols_ref, sems.at[count]
+        )
+    )
     for copy in copies:
         copy.start()
     new = lax.broadcasted_iota(jnp.int32, (rows, rows), 0)
@@ -90,30 +99,37 @@
         send_ref[:, cols] = numer[half:].astype(BF16)
     keep_ref[:, width:] = packed(peak[:half], total[:half])
     send_ref[:, width:] = packed(peak[half:], total[half:])
-
-
-def embed(pixels, weight, shift, query):
+    copies[count].wait()
+
+
+def embed(pixels, weight, shift, query, out_weight):
     count, depth, rows = pixels.shape
     width = weight.shape[2]
     heads = query.shape[0]
     vmem = pl.BlockSpec(memory_space=pltpu.VMEM)
+    hbm = pl.BlockSpec(memory_space=pltpu.HBM)
     part = jax.ShapeDtypeStruct((rows // 2, width + 256), BF16)
     return pl.pallas_call(
         embed_kernel,
-        in_specs=[vmem, pl.BlockSpec(memory_space=pltpu.HBM), vmem, vmem],
-        out_shape=(part, part),
+        in_specs=[vmem, hbm, vmem, vmem, hbm],
+        out_specs=[vmem, vmem, hbm],
+        out_shape=(part, part, jax.ShapeDtypeStruct((out_weight.shape[0], width // 8), BF16)),
         scratch_shapes=[
             pltpu.VMEM((count, rows, width), BF16),
             pltpu.VMEM((count, rows, heads), F32),
             pltpu.VMEM((count, depth, width), BF16),
-            pltpu.SemaphoreType.DMA((count,)),
+            pltpu.SemaphoreType.DMA((count + 1,)),
         ],
         compiler_params=params(60),
         name="embed",
-    )(pixels, weight, shift, query)
-
-
-def pair_kernel(mine_ref, other_ref, out_ref):
+    )(pixels, weight, shift, query, out_weight)
+
+
+def pair_kernel(mine_ref, other_ref, cot_ref, cot_got_ref, out_ref, cot_out_ref):
+    x_hi = lax.axis_index("xh")
+    tokens = cot_ref.shape[0]
+    cot_out_ref[pl.ds(pl.multiple_of(x_hi * tokens, tokens), tokens), :] = cot_ref[...]
+    cot_out_ref[pl.ds(pl.multiple_of((1 - x_hi) * tokens, tokens), tokens), :] = cot_got_ref[...]
     rows, padded = mine_ref.shape
     width = padded - 256
     heads = width // HD
@@ -130,13 +146,17 @@
     out_ref[:, width:] = packed(top, total_a * scale_a + total_b * scale_b)
 
 
-def pair(mine, other):
+def pair(mine, other, cot, cot_got):
+    tokens, cols = cot.shape
     return pl.pallas_call(
         pair_kernel,
-        out_shape=jax.ShapeDtypeStruct(other.shape, BF16),
+        out_shape=(
+            jax.ShapeDtypeStruct(other.shape, BF16),
+            jax.ShapeDtypeStruct((2 * tokens, cols), BF16),
+        ),
         compiler_params=params(12),
         name="pair",
-    )(mine, other)
+    )(mine, other, cot, cot_got)
 
 
 def merge_kernel(parts_ref, gain_ref, normed_ref, kept_ref, whole):
@@ -366,15 +386,14 @@
     core = lax.axis_index("c")
     width = out_weight.shape[1]
 
-    keep, send = embed(patches.transpose(0, 2, 1), patch_weight, var_embed, agg_query.T)
-    parts = pair(keep, swap(send, "c"))
-    parts, cols = lax.optimization_barrier((parts, out_weight))
-
-    cot = lax.all_gather(head_cot, SEQ, axis=0, tiled=True)
-    cols = lax.dynamic_slice_in_dim(cols, lax.axis_index(BANDS) * 512, 512, 1)
+    cot_got = swap(head_cot, "xh")
+    keep, send, cols = embed(
+        patches.transpose(0, 2, 1), patch_weight, var_embed, agg_query.T, out_weight
+    )
+    parts, cot = pair(keep, swap(send, "c"), head_cot, cot_got)
+    cot = lax.all_gather(cot, ("zq", "z0"), axis=0, tiled=True)
+    parts, cols = lax.optimization_barrier((exchange(parts, CHIPS), cols))
     cols = lax.all_gather(cols, VAR, axis=0, tiled=True)
-
-    parts = exchange(parts, CHIPS)
     normed, kept = merge(parts, norm_gain.reshape(1, width), 8)
     normed = exchange(normed, CHIPS)
     kv, query, query_send = project(normed, swap(normed, "c"), qkv_weight.transpose(1, 0, 2))
@@ -388,7 +407,7 @@
     got = exchange(sent, BANDS)
     layer = output(got, cols)
     layer = exchange(layer, CHIPS + ("z0",))
-    cot = cot.reshape(8, 2, 8, 2, 8, 384).transpose(3, 2, 1, 0, 4, 5).reshape(2, 1024, 384)
+    cot = cot.reshape(4, 2, 2, 8, 2, 8, 384).transpose(4, 3, 1, 2, 0, 5, 6).reshape(2, 1024, 384)
     first = lax.dynamic_index_in_dim(cot, core, 0, keepdims=False)
     second = lax.dynamic_index_in_dim(cot, 1 - core, 0, keepdims=False)
     return dot(layer, first, TN) + dot(swap(layer, "c"), second, TN)

time: 180 us -> 166 us (0.922)
  waiting for transfers between devices: 52.1 us -> 32.8 us
  blocking collectives: 62.6 us -> 69.6 us
  local copies, waits for them, and re-layouts: 4.51 us -> 1.42 us
    all_gather x1, waiting for transfers between devices: 29.2 us -> 0.01 us  [body(): cot = lax.all_gather(cot, ('zq', 'z0'), axis=0, tiled=True)]
    all_to_all x2 -> x1, waiting for transfers between devices: 13.6 us -> 25.6 us  [exchange(): return lax.all_to_all(x, axes, 0, 0, tiled=True)]
    all_to_all x4 -> x5, blocking collectives: 62.6 us -> 69.6 us  [exchange(): return lax.all_to_all(x, axes, 0, 0, tiled=True)]
    all_gather x1, waiting for transfers between devices: 5.2 us -> 0.01 us  [body(): cols = lax.all_gather(cols, VAR, axis=0, tiled=True)]
    ppermute x4 -> x5, waiting for transfers between devices: 3.34 us -> 7.14 us  [swap(): return lax.ppermute(x, axis, [(0, 1), (1, 0)])]
    all_to_all x2 -> x1, starting transfers between devices: 13.9 us -> 10.5 us  [exchange(): return lax.all_to_all(x, axes, 0, 0, tiled=True)]
    ppermute x4 -> x5, starting transfers between devices: 8.92 us -> 12.2 us  [swap(): return lax.ppermute(x, axis, [(0, 1), (1, 0)])]
  transfers between devices with their start and end apart: 8 -> 8, of which waited for: 6 -> 4; matrix products, arithmetic and copies ran while one was open for 2% -> 1% of each run, Pallas kernels for 11% -> 4%
where the time goes in v8:
time: 166 us; the launch traced here: 165 us
  blocking collectives  69.6 us (42%)
  waiting for transfers between devices  32.8 us (20%)
  Pallas kernels  23.4 us (14%)
  starting transfers between devices  22.8 us (14%)
  between operations  13.5 us (8%)
  matrix products  1.7 us (1%)
    all_to_all x5, blocking collectives, exchange(): return lax.all_to_all(x, axes, 0, 0, tiled=True)  69.6 us
    all_to_all x1, waiting for transfers between devices, exchange(): return lax.all_to_all(x, axes, 0, 0, tiled=True)  25.6 us
    pallas_call x1, Pallas kernels, embed(): pl.pallas_call(embed_kernel, in_specs=[vmem, hbm, vmem, vmem, hbm], out_s...  12.3 us
    ppermute x5, starting transfers between devices, swap(): return lax.ppermute(x, axis, [(0, 1), (1, 0)])  12.2 us
    all_to_all x1, starting transfers between devices, exchange(): return lax.all_to_all(x, axes, 0, 0, tiled=True)  10.5 us
    ppermute x5, waiting for transfers between devices, swap(): return lax.ppermute(x, axis, [(0, 1), (1, 0)])  7.14 us
    pallas_call x1, Pallas kernels, project(): pl.pallas_call(qkv_kernel, in_specs=[vmem, vmem, hbm], out_shape=[jax.Sha...  4.93 us
  transfers between devices with their start and end apart: 8, of which 4 were waited for; matrix products, arithmetic and copies ran while one was open for 1% of the time, Pallas kernels for 4%

profile of v8, /device:TPU:1, one launch (start us, length us, event | category | flops | bytes accessed | tf_op | source)
XLA Modules:
  0.0 165.3 jit_solution(10419559009180462173)
XLA Ops:
  6.5 0.0 all-gather.3.cloned.1.call-start
  6.5 0.0 copy-start.1
  6.5 0.0 copy-start.3
  6.5 12.3 %embed.1 = (bf16[64,4352]{1,0:T(8,128)(2,1)}, bf16[64,4352]{1,0:T(8,128)(2,1)}, bf16[256,512]{1,0:T(8,128)(2,1)}) custom-call(bf16[6,64,128]{2,1,0:T(8,128)(2,1)} %bitcast.43, bf16[6,64,4096]{2,1,0:T(8,128)(2,1)} %weight_ref.1, bf16[6,4096]{1,0:T(8,128)(2,1)} %shift_ref.1, bf16[32,4096]{1,0:T(8,128)(2,1)} %bitcast.41, bf16[256,4096]{1,0:T(8,128)(2,1)} %rows_ref.1), custom_call_target="tpu_custom_call" | custom-call | tf_op jit(solution)/shard_map/embed/pallas_call | solution.py:112
  18.8 3.3 %collective-permute-start = (bf16[64,4352]{1,0:T(8,128)(2,1)}, bf16[64,4352]{1,0:T(8,128)(2,1)S(1)}, u32[]{:S(2)}, u32[]{:S(2)}) collective-permute-start(bf16[64,4352]{1,0:T(8,128)(2,1)} %get-tuple-element.20), channel_id=1, source_target_pairs={{0,16},{16,0},{1,17},{17,1},{2,18},{18,2},{3,19},{19,3},{4,20},{20... | collective-permute-start | bytes 1671176 | tf_op jit(solution)/shard_map/ppermute | solution.py:378
  22.1 0.0 copy-done.1
  22.1 1.0 collective-permute-start.1
  23.2 4.8 %collective-permute-done.1.cot_got_ref = bf16[128,384]{1,0:T(8,128)(2,1)S(1)} collective-permute-done((bf16[128,384]{1,0:T(8,128)(2,1)S(1)}, bf16[128,384]{1,0:T(8,128)(2,1)S(1)}, u32[]{:S(2)}, u32[]{:S(2)}) %collective-permute-start.1) | collective-permute-done | bytes 98336 | tf_op jit(solution)/shard_map/ppermute | solution.py:378
  28.0 0.0 collective-permute-done.other_ref
  28.0 0.0 copy-start
  28.0 1.1 copy-done
  29.1 1.5 pair.1
  30.5 0.0 all-gather.3.cloned.1.call-update
  30.6 0.0 all-gather.5.cloned.1.call-start
  30.6 12.5 %all_to_all.61 = bf16[8,8,4352]{2,1,0:T(8,128)(2,1)S(1)} all-to-all(bf16[8,8,4352]{2,1,0:T(8,128)(2,1)S(1)} %bitcast.31), channel_id=1, replica_groups=mesh['y'=4,'xl'=2,'c'=2,'xh'=2,'zq'=4,'z0'=2] {'y','xl'}, dimensions={0} | all-to-all | bytes 1114112 | tf_op jit(solution)/shard_map/all_to_all | solution.py:382
  43.1 0.0 all-gather.5.cloned.1.call-update
  43.1 0.0 copy-done.3
  43.1 0.8 merge.1
  44.0 10.8 %all_to_all.62 = bf16[8,8,4096]{2,1,0:T(8,128)(2,1)S(1)} all-to-all(bf16[8,8,4096]{2,1,0:T(8,128)(2,1)S(1)} %bitcast.32), channel_id=1, replica_groups=mesh['y'=4,'xl'=2,'c'=2,'xh'=2,'zq'=4,'z0'=2] {'y','xl'}, dimensions={0} | all-to-all | bytes 1048576 | tf_op jit(solution)/shard_map/all_to_all | solution.py:382
  54.7 3.0 %collective-permute-start.2 = (bf16[64,4096]{1,0:T(8,128)(2,1)S(1)}, bf16[64,4096]{1,0:T(8,128)(2,1)S(1)}, u32[]{:S(2)}, u32[]{:S(2)}) collective-permute-start(bf16[64,4096]{1,0:T(8,128)(2,1)S(1)} %bitcast.28), channel_id=1, source_target_pairs={{0,16},{16,0},{1,17},{17,1},{2,18},{18,2},{3,19},{19,3},{4,20},{20... | collective-permute-start | bytes 1572872 | tf_op jit(solution)/shard_map/ppermute | solution.py:378
  57.7 1.5 collective-permute-done.2.other_ref
  59.2 4.9 %project.1 = (bf16[2048,256]{1,0:T(8,128)(2,1)}, bf16[128,128]{1,0:T(8,128)(2,1)S(1)}, bf16[128,128]{1,0:T(8,128)(2,1)S(1)}) custom-call(bf16[64,4096]{1,0:T(8,128)(2,1)S(1)} %bitcast.29, bf16[64,4096]{1,0:T(8,128)(2,1)S(1)} %collective-permute-done.2.other_ref, bf16[3,4096,256]{2,1,0:T(8,128)(2,1)} %bitcast.35), custom_call_target="tpu_custom_call" | custom-call | tf_op jit(solution)/shard_map/project/pallas_call | solution.py:268
  64.2 10.5 %all-to-all-start.2 = ((bf16[16,128,256]{2,1,0:T(8,128)(2,1)}), bf16[16,128,256]{2,1,0:T(8,128)(2,1)S(1)}, u32[]{:S(2)}, u32[]{:S(2)}) async-start(bf16[16,128,256]{2,1,0:T(8,128)(2,1)} %bitcast.7), calls=%async_computation.2 | async-start | bytes 2097152 | tf_op jit(solution)/shard_map/all_to_all | solution.py:382
  74.7 1.4 collective-permute-start.3
  76.0 0.0 all-gather.3.cloned.1.call-done
  76.0 25.6 %all-to-all-done.2 = bf16[16,128,256]{2,1,0:T(8,128)(2,1)S(1)} async-done(((bf16[16,128,256]{2,1,0:T(8,128)(2,1)}), bf16[16,128,256]{2,1,0:T(8,128)(2,1)S(1)}, u32[]{:S(2)}, u32[]{:S(2)}) %all-to-all-start.2) | async-done | bytes 1048608 | tf_op jit(solution)/shard_map/all_to_all | solution.py:382
  101.7 0.0 collective-permute-done.3.got_ref
  101.7 1.3 attend.1
  103.0 12.8 %all_to_all.63 = bf16[32,8,128]{2,1,0:T(8,128)(2,1)S(1)} all-to-all(bf16[32,8,128]{2,1,0:T(8,128)(2,1)S(1)} %bitcast.33), channel_id=1, replica_groups=mesh['y'=4,'xl'=2,'c'=2,'xh'=2,'zq'=4,'z0'=2] {'y','xl','c','z0'}, dimensions={0} | all-to-all | bytes 131072 | tf_op jit(solution)/shard_map/all_to_all | solution.py:382
  115.8 0.1 broadcast_in_dim.9
  115.9 23.7 %all_to_all.64.parts_ref = bf16[8,288,128]{2,1,0:T(8,128)(2,1)S(1)} all-to-all(bf16[8,288,128]{2,1,0:T(8,128)(2,1)S(1)} %pad_maximum_fusion), channel_id=1, replica_groups=mesh['y'=4,'xl'=2,'c'=2,'xh'=2,'zq'=4,'z0'=2] {'xh','zq'}, dimensions={0} | all-to-all | bytes 1179648 | tf_op jit(solution)/shard_map/all_to_all | solution.py:382
  139.6 0.0 all-gather.5.cloned.1.call-done.weight_ref
  139.6 0.0 copy-start.2
  139.6 2.6 %output.1 = bf16[1024,256]{1,0:T(8,128)(2,1)S(1)} custom-call(bf16[8,288,128]{2,1,0:T(8,128)(2,1)S(1)} %all_to_all.64.parts_ref, bf16[4096,512]{1,0:T(8,128)(2,1)} %all-gather.5.cloned.1.call-done.weight_ref), custom_call_target="tpu_custom_call" | custom-call | tf_op jit(solution)/shard_map/output/pallas_call | solution.py:363
  142.2 9.9 %all_to_all.65 = bf16[16,64,256]{2,1,0:T(8,128)(2,1)S(1)} all-to-all(bf16[16,64,256]{2,1,0:T(8,128)(2,1)S(1)} %bitcast.30), channel_id=1, replica_groups=mesh['y'=4,'xl'=2,'c'=2,'xh'=2,'zq'=4,'z0'=2] {'y','xl','z0'}, dimensions={0} | all-to-all | bytes 1048576 | tf_op jit(solution)/shard_map/all_to_all | solution.py:382
  152.1 3.6 %collective-permute-start.4 = (bf16[1024,256]{1,0:T(8,128)(2,1)S(1)}, bf16[1024,256]{1,0:T(8,128)(2,1)S(1)}, u32[]{:S(2)}, u32[]{:S(2)}) collective-permute-start(bf16[1024,256]{1,0:T(8,128)(2,1)S(1)} %bitcast.38), channel_id=1, source_target_pairs={{0,16},{16,0},{1,17},{17,1},{2,18},{18,2},{3,19},{19,3},{4,20},{20... | collective-permute-start | bytes 1572872 | tf_op jit(solution)/shard_map/ppermute | solution.py:378
  155.7 0.0 copy-done.2
  155.7 0.3 copy.9
  155.9 0.5 fusion.1
  156.4 0.8 collective-permute-done.4
  157.2 1.2 convolution_add_fusion
  (2 shorter events, 0.1 us)
Async XLA Ops:
  6.5 69.5 %all-gather.3.cloned.1.call-start = ((), (), s32[]{:S(2)}) async-start(), calls=%async_computation.6 | async-start | bytes 1769472 | tf_op jit(solution)/shard_map/all_gather | solution.py:394
  6.5 15.6 %copy-start.1 = (bf16[128,384]{1,0:T(8,128)(2,1)S(1)}, bf16[128,384]{1,0:T(8,128)(2,1)}, u32[]{:S(2)}) copy-start(bf16[128,384]{1,0:T(8,128)(2,1)} %cot_ref.1) | copy-start | bytes 294916
  6.5 36.6 %copy-start.3 = (bf16[4096]{0:T(1024)(128)(2,1)S(1)}, bf16[4096]{0:T(1024)(128)(2,1)}, u32[]{:S(2)}) copy-start(bf16[4096]{0:T(1024)(128)(2,1)} %param.12) | copy-start | bytes 24580
  18.8 9.2 %collective-permute-start = (bf16[64,4352]{1,0:T(8,128)(2,1)}, bf16[64,4352]{1,0:T(8,128)(2,1)S(1)}, u32[]{:S(2)}, u32[]{:S(2)}) collective-permute-start(bf16[64,4352]{1,0:T(8,128)(2,1)} %get-tuple-element.20), channel_id=1, source_target_pairs={{0,16},{16,0},{1,17},{17,1},{2,18},{18,2},{3,19},{19,3},{4,20},{20... | collective-permute-start | bytes 1671176 | tf_op jit(solution)/shard_map/ppermute | solution.py:378
  22.1 5.9 %collective-permute-start.1 = (bf16[128,384]{1,0:T(8,128)(2,1)S(1)}, bf16[128,384]{1,0:T(8,128)(2,1)S(1)}, u32[]{:S(2)}, u32[]{:S(2)}) collective-permute-start(bf16[128,384]{1,0:T(8,128)(2,1)S(1)} %copy-done.1), channel_id=1, source_target_pairs={{0,8},{8,0},{1,9},{9,1},{2,10},{10,2},{3,11},{11,3},{4,12},{12,4},... | collective-permute-start | bytes 294920 | tf_op jit(solution)/shard_map/ppermute | solution.py:378
  28.0 1.1 copy-start
  30.6 109.1 %all-gather.5.cloned.1.call-start = ((), (), s32[]{:S(2)}) async-start(), calls=%async_computation.7 | async-start | bytes 4456448 | tf_op jit(solution)/shard_map/all_gather | solution.py:396
  54.7 4.5 %collective-permute-start.2 = (bf16[64,4096]{1,0:T(8,128)(2,1)S(1)}, bf16[64,4096]{1,0:T(8,128)(2,1)S(1)}, u32[]{:S(2)}, u32[]{:S(2)}) collective-permute-start(bf16[64,4096]{1,0:T(8,128)(2,1)S(1)} %bitcast.28), channel_id=1, source_target_pairs={{0,16},{16,0},{1,17},{17,1},{2,18},{18,2},{3,19},{19,3},{4,20},{20... | collective-permute-start | bytes 1572872 | tf_op jit(solution)/shard_map/ppermute | solution.py:378
  64.2 37.5 %all-to-all-start.2 = ((bf16[16,128,256]{2,1,0:T(8,128)(2,1)}), bf16[16,128,256]{2,1,0:T(8,128)(2,1)S(1)}, u32[]{:S(2)}, u32[]{:S(2)}) async-start(bf16[16,128,256]{2,1,0:T(8,128)(2,1)} %bitcast.7), calls=%async_computation.2 | async-start | bytes 2097152 | tf_op jit(solution)/shard_map/all_to_all | solution.py:382
  74.7 27.0 %collective-permute-start.3 = (bf16[128,128]{1,0:T(8,128)(2,1)S(1)}, bf16[128,128]{1,0:T(8,128)(2,1)S(1)}, u32[]{:S(2)}, u32[]{:S(2)}) collective-permute-start(bf16[128,128]{1,0:T(8,128)(2,1)S(1)} %get-tuple-element.26), channel_id=1, source_target_pairs={{0,1},{1,0},{2,3},{3,2},{4,5},{5,4},{6,7},{7,6},{8,9},{9,8},{10,11... | collective-permute-start | bytes 98312 | tf_op jit(solution)/shard_map/ppermute | solution.py:378
  139.6 16.0 %copy-start.2 = (bf16[2048,384]{1,0:T(8,128)(2,1)S(1)}, bf16[2048,384]{1,0:T(8,128)(2,1)}, u32[]{:S(2)}) copy-start(bf16[2048,384]{1,0:T(8,128)(2,1)} %all-gather.3.cloned.1.call-done) | copy-start | bytes 4718596
  152.1 5.1 %collective-permute-start.4 = (bf16[1024,256]{1,0:T(8,128)(2,1)S(1)}, bf16[1024,256]{1,0:T(8,128)(2,1)S(1)}, u32[]{:S(2)}, u32[]{:S(2)}) collective-permute-start(bf16[1024,256]{1,0:T(8,128)(2,1)S(1)} %bitcast.38), channel_id=1, source_target_pairs={{0,16},{16,0},{1,17},{17,1},{2,18},{18,2},{3,19},{19,3},{4,20},{20... | collective-permute-start | bytes 1572872 | tf_op jit(solution)/shard_map/ppermute | solution.py:378
Sparse Core Ops, SparseCore 0:
  30.7 37.3 all-gather.2
  69.9 48.4 all-gather.4

commit v9 on v8

--- a/solution.py
+++ b/solution.py
@@ -13,8 +13,7 @@
 BF16 = jnp.bfloat16
 VAR = ("y", "xl", "c")
 CHIPS = ("y", "xl")
-SEQ = ("xh", "zq", "z0")
-BANDS = ("xh", "zq")
+SEQ = ("xh", "z")
 NT = (((1,), (1,)), ((), ()))
 TN = (((0,), (0,)), ((), ()))
 NN = (((1,), (0,)), ((), ()))
@@ -52,32 +51,50 @@
 
 
 def embed_kernel(
-    pixels_ref, weight_ref, shift_ref, query_ref, rows_ref, keep_ref, send_ref, cols_ref, embedded, scores, held, sems
+    pixels_hbm, weight_ref, shift_hbm, query_hbm, rows_ref, keep_ref, send_ref, cols_ref,
+    pixels_ref, shift_ref, query_ref, embedded, scores, held, keep, send, sems, small_sems, out_sems,
 ):
     core = lax.axis_index("c")
-    part = lax.axis_index("xh") * 4 + lax.axis_index("zq")
+    z = lax.axis_index("z")
     count, rows, width = embedded.shape
     heads = query_ref.shape[0]
     half = rows // 2
+    small = [
+        pltpu.make_async_copy(pixels_hbm, pixels_ref, small_sems.at[0]),
+        pltpu.make_async_copy(shift_hbm, shift_ref, small_sems.at[1]),
+        pltpu.make_async_copy(query_hbm, query_ref, small_sems.at[2]),
+    ]
     copies = [
         pltpu.make_async_copy(weight_ref.at[v], held.at[v], sems.at[v]) for v in range(count)
     ]
-    cut = cols_ref.shape[1]
-    copies.append(
-        pltpu.make_async_copy(
-            rows_ref.at[:, pl.ds(pl.multiple_of(part * cut, cut), cut)], cols_ref, sems.at[count]
+    for copy in [small[0], copies[0], small[1], small[2]] + copies[1:]:
+        copy.start()
+    cut = cols_ref.shape[1] // 2
+    slices = []
+    for side in range(2):
+        place = pl.multiple_of(side * (width // 2) + z * cut, cut)
+        slices.append(
+            pltpu.make_async_copy(
+                rows_ref.at[:, pl.ds(place, cut)],
+                cols_ref.at[:, pl.ds(side * cut, cut)],
+                small_sems.at[3 + side],
+            )
         )
-    )
-    for copy in copies:
-        copy.start()
+        slices[side].start()
     new = lax.broadcasted_iota(jnp.int32, (rows, rows), 0)
     old = lax.broadcasted_iota(jnp.int32, (rows, rows), 1)
     group = (new % half) // 8 * 2 + jnp.where(new < half, core, 1 - core)
     order = jnp.where(old == group * 8 + new % 8, 1.0, 0.0).astype(BF16)
     step = 1024
+    small[0].wait()
     for v in range(count):
         tokens = dot(order, pixels_ref[v], NT).astype(BF16)
-        copies[v].wait()
+        if v == 0:
+            small[1].wait()
+            small[2].wait()
+        if v % 2 == 0:
+            for copy in copies[v : v + 2]:
+                copy.wait()
         total = jnp.zeros((rows, heads), F32)
         for at in range(0, width, step):
             block = dot(tokens, held[v, :, at : at + step], NN)
@@ -90,37 +107,64 @@
     peak = jnp.max(every, axis=0)
     weights = jnp.exp(every - peak[None])
     total = jnp.sum(weights, axis=0)
+    keep[:, width:] = packed(peak[:half], total[:half])
+    send[:, width:] = packed(peak[half:], total[half:])
+    leaving = []
+
+    def leave(place, size):
+        at = len(leaving) // 2
+        for side, (source, target) in enumerate(((keep, keep_ref), (send, send_ref))):
+            copy = pltpu.make_async_copy(
+                source.at[:, pl.ds(place, size)], target.at[:, pl.ds(place, size)], out_sems.at[side, at]
+            )
+            copy.start()
+            leaving.append(copy)
+
+    leave(width, 256)
     for h in range(heads):
         cols = slice(h * HD, (h + 1) * HD)
         numer = weights[0][:, h : h + 1] * embedded[0, :, cols].astype(F32)
         for v in range(1, count):
             numer = numer + weights[v][:, h : h + 1] * embedded[v, :, cols].astype(F32)
-        keep_ref[:, cols] = numer[:half].astype(BF16)
-        send_ref[:, cols] = numer[half:].astype(BF16)
-    keep_ref[:, width:] = packed(peak[:half], total[:half])
-    send_ref[:, width:] = packed(peak[half:], total[half:])
-    copies[count].wait()
+        keep[:, cols] = numer[:half].astype(BF16)
+        send[:, cols] = numer[half:].astype(BF16)
+        if h % 8 == 7:
+            leave((h - 7) * HD, 8 * HD)
+    for copy in slices + leaving:
+        copy.wait()
 
 
 def embed(pixels, weight, shift, query, out_weight):
     count, depth, rows = pixels.shape
     width = weight.shape[2]
     heads = query.shape[0]
-    vmem = pl.BlockSpec(memory_space=pltpu.VMEM)
+    half = rows // 2
     hbm = pl.BlockSpec(memory_space=pltpu.HBM)
-    part = jax.ShapeDtypeStruct((rows // 2, width + 256), BF16)
+    part = jax.ShapeDtypeStruct((half, width + 256), BF16)
     return pl.pallas_call(
         embed_kernel,
-        in_specs=[vmem, hbm, vmem, vmem, hbm],
-        out_specs=[vmem, vmem, hbm],
+        in_specs=[hbm] * 5,
+        out_specs=[hbm] * 3,
         out_shape=(part, part, jax.ShapeDtypeStruct((out_weight.shape[0], width // 8), BF16)),
         scratch_shapes=[
+            pltpu.VMEM((count, depth, rows), BF16),
+            pltpu.VMEM((count, width), BF16),
+            pltpu.VMEM((heads, width), BF16),
             pltpu.VMEM((count, rows, width), BF16),
             pltpu.VMEM((count, rows, heads), F32),
             pltpu.VMEM((count, depth, width), BF16),
-            pltpu.SemaphoreType.DMA((count + 1,)),
+            pltpu.VMEM((half, width + 256), BF16),
+            pltpu.VMEM((half, width + 256), BF16),
+            pltpu.SemaphoreType.DMA((count,)),
+            pltpu.SemaphoreType.DMA((5,)),
+            pltpu.SemaphoreType.DMA((2, 5)),
         ],
         compiler_params=params(60),
+        cost_estimate=pl.CostEstimate(
+            flops=2 * count * rows * width * (depth + heads),
+            bytes_accessed=4 * count * depth * width,
+            transcendentals=count * rows * heads,
+        ),
         name="embed",
     )(pixels, weight, shift, query, out_weight)
 
@@ -186,7 +230,8 @@
         if h % 2 == 0:
             last = value
         else:
-            to = h // 2 * 16
+            block = h // 2
+            to = (block % 8 * 2 + block // 8) * 16
             kept_ref[to : to + 16, :] = jnp.concatenate([last, value], axis=0).astype(BF16)
     center = jnp.sum(sums, axis=1, keepdims=True) / width
     squares = jnp.zeros((share, HD), F32)
@@ -219,7 +264,7 @@
 
 def qkv_kernel(mine_ref, other_ref, weight_ref, kv_ref, keep_ref, send_ref, tokens, held, sems):
     core = lax.axis_index("c")
-    z0 = lax.axis_index("z0")
+    x_hi = lax.axis_index("xh")
     half, width = mine_ref.shape
     rows = 2 * half
     parts = sems.shape[1]
@@ -241,19 +286,17 @@
     tokens[pl.ds(pl.multiple_of(core * half, half), half), :] = mine_ref[...]
     tokens[pl.ds(pl.multiple_of((1 - core) * half, half), half), :] = other_ref[...]
     for k in range(3):
-        made = jnp.zeros((rows, 2 * HD), F32)
-        for part in range(parts):
-            copies[k][part].wait()
-            at = slice(part * depth, (part + 1) * depth)
-            made = made + dot(tokens[:, at], held[k, at, :], NN)
+        for copy in copies[k]:
+            copy.wait()
+        made = dot(tokens[...], held[k], NN)
         first, second = made[:, :HD], made[:, HD:]
         if k == 0:
-            keep_ref[...] = jnp.where(z0 == 0, first, second).astype(BF16)
-            send_ref[...] = jnp.where(z0 == 0, second, first).astype(BF16)
+            keep_ref[...] = jnp.where(x_hi == 0, first, second).astype(BF16)
+            send_ref[...] = jnp.where(x_hi == 0, second, first).astype(BF16)
         else:
             cols = slice((k - 1) * HD, k * HD)
             for to in range(16):
-                value = first if to % 2 == 0 else second
+                value = first if to < 8 else second
                 kv_ref[to * rows : (to + 1) * rows, cols] = value.astype(BF16)
 
 
@@ -261,7 +304,7 @@
     half, width = mine.shape
     cols = weight.shape[2]
     rows = 2 * half
-    parts = 4
+    parts = 1
     vmem = pl.BlockSpec(memory_space=pltpu.VMEM)
     hbm = pl.BlockSpec(memory_space=pltpu.HBM)
     shapes = [(16 * rows, 2 * HD), (rows, HD), (rows, HD)]
@@ -280,12 +323,12 @@
 
 
 def attend_kernel(keep_ref, got_ref, kv_ref, out_ref, scores):
-    z0 = lax.axis_index("z0")
+    x_hi = lax.axis_index("xh")
     count = kv_ref.shape[0]
     step = 256
     mixed = []
     for side in range(2):
-        query = jnp.where(z0 == side, keep_ref[...], got_ref[...])
+        query = jnp.where(x_hi == side, keep_ref[...], got_ref[...])
         for at in range(0, count, step):
             scores[:, at : at + step] = dot(query, kv_ref[at : at + step, :HD], NT) / math.sqrt(HD)
         every = scores[...]
@@ -390,31 +433,32 @@
     keep, send, cols = embed(
         patches.transpose(0, 2, 1), patch_weight, var_embed, agg_query.T, out_weight
     )
+    send, cot_got = lax.optimization_barrier((send, cot_got))
     parts, cot = pair(keep, swap(send, "c"), head_cot, cot_got)
-    cot = lax.all_gather(cot, ("zq", "z0"), axis=0, tiled=True)
+    cot = lax.all_gather(cot, "z", axis=0, tiled=True)
     parts, cols = lax.optimization_barrier((exchange(parts, CHIPS), cols))
     cols = lax.all_gather(cols, VAR, axis=0, tiled=True)
     normed, kept = merge(parts, norm_gain.reshape(1, width), 8)
     normed = exchange(normed, CHIPS)
     kv, query, query_send = project(normed, swap(normed, "c"), qkv_weight.transpose(1, 0, 2))
-    query_got = swap(query_send, "z0")
+    query_got = swap(query_send, "xh")
     kv, cot = lax.optimization_barrier((exchange(kv, SEQ), cot))
     attended = attend(query, query_got, kv)
-    attended = exchange(attended, VAR + ("z0",))
+    attended = exchange(attended, VAR + ("xh",))
     sent = jnp.concatenate(
         [jnp.broadcast_to(attended[None], (8, 256, HD)), kept.reshape(8, 32, HD)], axis=1
     )
-    got = exchange(sent, BANDS)
+    got = exchange(sent, "z")
     layer = output(got, cols)
-    layer = exchange(layer, CHIPS + ("z0",))
-    cot = cot.reshape(4, 2, 2, 8, 2, 8, 384).transpose(4, 3, 1, 2, 0, 5, 6).reshape(2, 1024, 384)
+    layer = exchange(layer, CHIPS + ("xh",))
+    cot = cot.reshape(8, 2, 8, 2, 8, 384).transpose(3, 2, 1, 0, 4, 5).reshape(2, 1024, 384)
     first = lax.dynamic_index_in_dim(cot, core, 0, keepdims=False)
     second = lax.dynamic_index_in_dim(cot, 1 - core, 0, keepdims=False)
     return dot(layer, first, TN) + dot(swap(layer, "c"), second, TN)
 
 
 def solution(mesh):
-    whole = Mesh(mesh.devices.reshape(4, 2, 2, 2, 4, 2), ("y", "xl", "c", "xh", "zq", "z0"))
+    whole = Mesh(mesh.devices.reshape(4, 2, 2, 2, 8), ("y", "xl", "c", "xh", "z"))
     return jax.shard_map(
         body,
         mesh=whole,

time: 166 us -> 161 us (0.970)
  waiting for transfers between devices: 32.8 us -> 28.3 us
    ppermute x5, waiting for transfers between devices: 7.14 us -> 4.11 us  [swap(): return lax.ppermute(x, axis, [(0, 1), (1, 0)])]
  transfers between devices with their start and end apart: 8 -> 8, of which waited for: 4 -> 4; matrix products, arithmetic and copies ran while one was open for 1% -> 1% of each run, Pallas kernels for 4% -> 11%
where the time goes in v9:
time: 161 us; the launch traced here: 160 us
  blocking collectives  71.1 us (44%)
  waiting for transfers between devices  28.3 us (18%)
  starting transfers between devices  22.5 us (14%)
  Pallas kernels  21.9 us (14%)
  between operations  13.5 us (8%)
  matrix products  1.7 us (1%)
    all_to_all x5, blocking collectives, exchange(): return lax.all_to_all(x, axes, 0, 0, tiled=True)  71.1 us
    all_to_all x1, waiting for transfers between devices, exchange(): return lax.all_to_all(x, axes, 0, 0, tiled=True)  24.2 us
    ppermute x5, starting transfers between devices, swap(): return lax.ppermute(x, axis, [(0, 1), (1, 0)])  12.7 us
    pallas_call x1, Pallas kernels, embed(): pl.pallas_call(embed_kernel, in_specs=[hbm] * 5, out_specs=[hbm] * 3, out...  10.9 us
    all_to_all x1, starting transfers between devices, exchange(): return lax.all_to_all(x, axes, 0, 0, tiled=True)  9.75 us
    pallas_call x1, Pallas kernels, project(): pl.pallas_call(qkv_kernel, in_specs=[vmem, vmem, hbm], out_shape=[jax.Sha...  4.77 us
    ppermute x5, waiting for transfers between devices, swap(): return lax.ppermute(x, axis, [(0, 1), (1, 0)])  4.11 us
  transfers between devices with their start and end apart: 8, of which 4 were waited for; matrix products, arithmetic and copies ran while one was open for 1% of the time, Pallas kernels for 11%

profile of v9, /device:TPU:1, one launch (start us, length us, event | category | flops | bytes accessed | tf_op | source)
XLA Modules:
  0.0 160.5 jit_solution(15324516765280308277)
XLA Ops:
  6.5 0.0 all-gather.3.cloned.1.call-start
  6.5 3.6 %collective-permute-start = (bf16[128,384]{1,0:T(8,128)(2,1)}, bf16[128,384]{1,0:T(8,128)(2,1)S(1)}, u32[]{:S(2)}, u32[]{:S(2)}) collective-permute-start(bf16[128,384]{1,0:T(8,128)(2,1)} %cot_ref.1), channel_id=1, source_target_pairs={{0,8},{8,0},{1,9},{9,1},{2,10},{10,2},{3,11},{11,3},{4,12},{12,4},... | collective-permute-start | bytes 294920 | tf_op jit(solution)/shard_map/ppermute | solution.py:421
  10.1 0.0 copy-start.1
  10.1 0.0 copy-start.3
  10.1 10.9 %embed.1 = (bf16[64,4352]{1,0:T(8,128)(2,1)}, bf16[64,4352]{1,0:T(8,128)(2,1)}, bf16[256,512]{1,0:T(8,128)(2,1)}) custom-call(bf16[6,64,128]{2,1,0:T(8,128)(2,1)} %bitcast.43, bf16[6,64,4096]{2,1,0:T(8,128)(2,1)} %weight_ref.1, bf16[6,4096]{1,0:T(8,128)(2,1)} %shift_hbm.1, bf16[32,4096]{1,0:T(8,128)(2,1)} %bitcast.41, bf16[256,4096]{1,0:T(8,128)(2,1)} %rows_ref.1), custom_call_target="tpu_custom_call" | custom-call | flops 603979776 | bytes 6291456 | tf_op jit(solution)/shard_map/embed/pallas_call | solution.py:144
  21.1 0.0 collective-permute-done.cot_got_ref
  21.1 1.0 collective-permute-start.1
  22.1 1.8 %collective-permute-done.1.other_ref = bf16[64,4352]{1,0:T(8,128)(2,1)S(1)} collective-permute-done((bf16[64,4352]{1,0:T(8,128)(2,1)}, bf16[64,4352]{1,0:T(8,128)(2,1)S(1)}, u32[]{:S(2)}, u32[]{:S(2)}) %collective-permute-start.1) | collective-permute-done | bytes 557088 | tf_op jit(solution)/shard_map/ppermute | solution.py:421
  23.9 0.0 copy-done.1
  23.9 0.0 copy-start
  23.9 1.1 copy-done
  25.0 1.5 pair.1
  26.4 0.0 all-gather.3.cloned.1.call-update
  26.5 0.0 all-gather.5.cloned.1.call-start
  26.5 14.0 %all_to_all.61 = bf16[8,8,4352]{2,1,0:T(8,128)(2,1)S(1)} all-to-all(bf16[8,8,4352]{2,1,0:T(8,128)(2,1)S(1)} %bitcast.31), channel_id=1, replica_groups=mesh['y'=4,'xl'=2,'c'=2,'xh'=2,'z'=8] {'y','xl'}, dimensions={0} | all-to-all | bytes 1114112 | tf_op jit(solution)/shard_map/all_to_all | solution.py:425
  40.5 0.0 all-gather.5.cloned.1.call-update
  40.5 0.0 copy-done.3
  40.6 0.8 merge.1
  41.4 11.6 %all_to_all.62 = bf16[8,8,4096]{2,1,0:T(8,128)(2,1)S(1)} all-to-all(bf16[8,8,4096]{2,1,0:T(8,128)(2,1)S(1)} %bitcast.32), channel_id=1, replica_groups=mesh['y'=4,'xl'=2,'c'=2,'xh'=2,'z'=8] {'y','xl'}, dimensions={0} | all-to-all | bytes 1048576 | tf_op jit(solution)/shard_map/all_to_all | solution.py:425
  53.0 2.2 %collective-permute-start.2 = (bf16[64,4096]{1,0:T(8,128)(2,1)S(1)}, bf16[64,4096]{1,0:T(8,128)(2,1)S(1)}, u32[]{:S(2)}, u32[]{:S(2)}) collective-permute-start(bf16[64,4096]{1,0:T(8,128)(2,1)S(1)} %bitcast.28), channel_id=1, source_target_pairs={{0,16},{16,0},{1,17},{17,1},{2,18},{18,2},{3,19},{19,3},{4,20},{20... | collective-permute-start | bytes 1572872 | tf_op jit(solution)/shard_map/ppermute | solution.py:421
  55.2 1.5 collective-permute-done.2.other_ref
  56.7 4.8 %project.1 = (bf16[2048,256]{1,0:T(8,128)(2,1)}, bf16[128,128]{1,0:T(8,128)(2,1)S(1)}, bf16[128,128]{1,0:T(8,128)(2,1)S(1)}) custom-call(bf16[64,4096]{1,0:T(8,128)(2,1)S(1)} %bitcast.29, bf16[64,4096]{1,0:T(8,128)(2,1)S(1)} %collective-permute-done.2.other_ref, bf16[3,4096,256]{2,1,0:T(8,128)(2,1)} %bitcast.35), custom_call_target="tpu_custom_call" | custom-call | tf_op jit(solution)/shard_map/project/pallas_call | solution.py:311
  61.5 9.8 %all-to-all-start.2 = ((bf16[16,128,256]{2,1,0:T(8,128)(2,1)}), bf16[16,128,256]{2,1,0:T(8,128)(2,1)S(1)}, u32[]{:S(2)}, u32[]{:S(2)}) async-start(bf16[16,128,256]{2,1,0:T(8,128)(2,1)} %bitcast.7), calls=%async_computation.2 | async-start | bytes 2097152 | tf_op jit(solution)/shard_map/all_to_all | solution.py:425
  71.3 2.9 %collective-permute-start.3 = (bf16[128,128]{1,0:T(8,128)(2,1)S(1)}, bf16[128,128]{1,0:T(8,128)(2,1)S(1)}, u32[]{:S(2)}, u32[]{:S(2)}) collective-permute-start(bf16[128,128]{1,0:T(8,128)(2,1)S(1)} %get-tuple-element.30), channel_id=1, source_target_pairs={{0,8},{8,0},{1,9},{9,1},{2,10},{10,2},{3,11},{11,3},{4,12},{12,4},... | collective-permute-start | bytes 98312 | tf_op jit(solution)/shard_map/ppermute | solution.py:421
  74.2 0.0 all-gather.3.cloned.1.call-done
  74.2 24.2 %all-to-all-done.2 = bf16[16,128,256]{2,1,0:T(8,128)(2,1)S(1)} async-done(((bf16[16,128,256]{2,1,0:T(8,128)(2,1)}), bf16[16,128,256]{2,1,0:T(8,128)(2,1)S(1)}, u32[]{:S(2)}, u32[]{:S(2)}) %all-to-all-start.2) | async-done | bytes 1048608 | tf_op jit(solution)/shard_map/all_to_all | solution.py:425
  98.3 0.0 collective-permute-done.3.got_ref
  98.3 1.3 attend.1
  99.6 12.4 %all_to_all.63 = bf16[32,8,128]{2,1,0:T(8,128)(2,1)S(1)} all-to-all(bf16[32,8,128]{2,1,0:T(8,128)(2,1)S(1)} %bitcast.33), channel_id=1, replica_groups=mesh['y'=4,'xl'=2,'c'=2,'xh'=2,'z'=8] {'y','xl','c','xh'}, dimensions={0} | all-to-all | bytes 131072 | tf_op jit(solution)/shard_map/all_to_all | solution.py:425
  112.0 0.1 broadcast_in_dim.9
  112.1 20.7 %all_to_all.64.parts_ref = bf16[8,288,128]{2,1,0:T(8,128)(2,1)S(1)} all-to-all(bf16[8,288,128]{2,1,0:T(8,128)(2,1)S(1)} %pad_maximum_fusion), channel_id=1, replica_groups=mesh['y'=4,'xl'=2,'c'=2,'xh'=2,'z'=8] {'z'}, dimensions={0} | all-to-all | bytes 1179648 | tf_op jit(solution)/shard_map/all_to_all | solution.py:425
  132.8 0.0 all-gather.5.cloned.1.call-done.weight_ref
  132.8 0.0 copy-start.2
  132.8 2.6 %output.1 = bf16[1024,256]{1,0:T(8,128)(2,1)S(1)} custom-call(bf16[8,288,128]{2,1,0:T(8,128)(2,1)S(1)} %all_to_all.64.parts_ref, bf16[4096,512]{1,0:T(8,128)(2,1)} %all-gather.5.cloned.1.call-done.weight_ref), custom_call_target="tpu_custom_call" | custom-call | tf_op jit(solution)/shard_map/output/pallas_call | solution.py:406
  135.4 12.5 %all_to_all.65 = bf16[16,64,256]{2,1,0:T(8,128)(2,1)S(1)} all-to-all(bf16[16,64,256]{2,1,0:T(8,128)(2,1)S(1)} %bitcast.30), channel_id=1, replica_groups=mesh['y'=4,'xl'=2,'c'=2,'xh'=2,'z'=8] {'y','xl','xh'}, dimensions={0} | all-to-all | bytes 1048576 | tf_op jit(solution)/shard_map/all_to_all | solution.py:425
  147.9 3.0 %collective-permute-start.4 = (bf16[1024,256]{1,0:T(8,128)(2,1)S(1)}, bf16[1024,256]{1,0:T(8,128)(2,1)S(1)}, u32[]{:S(2)}, u32[]{:S(2)}) collective-permute-start(bf16[1024,256]{1,0:T(8,128)(2,1)S(1)} %bitcast.38), channel_id=1, source_target_pairs={{0,16},{16,0},{1,17},{17,1},{2,18},{18,2},{3,19},{19,3},{4,20},{20... | collective-permute-start | bytes 1572872 | tf_op jit(solution)/shard_map/ppermute | solution.py:421
  150.9 0.0 copy-done.2
  150.9 0.3 copy.9
  151.2 0.5 fusion.1
  151.7 0.8 collective-permute-done.4
  152.4 1.2 convolution_add_fusion
  (2 shorter events, 0.1 us)
Async XLA Ops:
  6.5 67.6 %all-gather.3.cloned.1.call-start = ((), (), s32[]{:S(2)}) async-start(), calls=%async_computation.6 | async-start | bytes 1769472 | tf_op jit(solution)/shard_map/all_gather | solution.py:438
  6.5 14.5 %collective-permute-start = (bf16[128,384]{1,0:T(8,128)(2,1)}, bf16[128,384]{1,0:T(8,128)(2,1)S(1)}, u32[]{:S(2)}, u32[]{:S(2)}) collective-permute-start(bf16[128,384]{1,0:T(8,128)(2,1)} %cot_ref.1), channel_id=1, source_target_pairs={{0,8},{8,0},{1,9},{9,1},{2,10},{10,2},{3,11},{11,3},{4,12},{12,4},... | collective-permute-start | bytes 294920 | tf_op jit(solution)/shard_map/ppermute | solution.py:421
  10.1 13.8 %copy-start.1 = (bf16[128,384]{1,0:T(8,128)(2,1)S(1)}, bf16[128,384]{1,0:T(8,128)(2,1)}, u32[]{:S(2)}) copy-start(bf16[128,384]{1,0:T(8,128)(2,1)} %cot_ref.1) | copy-start | bytes 294916
  10.1 30.4 %copy-start.3 = (bf16[4096]{0:T(1024)(128)(2,1)S(1)}, bf16[4096]{0:T(1024)(128)(2,1)}, u32[]{:S(2)}) copy-start(bf16[4096]{0:T(1024)(128)(2,1)} %param.12) | copy-start | bytes 24580
  21.1 2.8 %collective-permute-start.1 = (bf16[64,4352]{1,0:T(8,128)(2,1)}, bf16[64,4352]{1,0:T(8,128)(2,1)S(1)}, u32[]{:S(2)}, u32[]{:S(2)}) collective-permute-start(bf16[64,4352]{1,0:T(8,128)(2,1)} %get-tuple-element.23), channel_id=1, source_target_pairs={{0,16},{16,0},{1,17},{17,1},{2,18},{18,2},{3,19},{19,3},{4,20},{20... | collective-permute-start | bytes 1671176 | tf_op jit(solution)/shard_map/ppermute | solution.py:421
  23.9 1.1 copy-start
  26.5 106.4 %all-gather.5.cloned.1.call-start = ((), (), s32[]{:S(2)}) async-start(), calls=%async_computation.7 | async-start | bytes 4456448 | tf_op jit(solution)/shard_map/all_gather | solution.py:440
  53.0 3.8 %collective-permute-start.2 = (bf16[64,4096]{1,0:T(8,128)(2,1)S(1)}, bf16[64,4096]{1,0:T(8,128)(2,1)S(1)}, u32[]{:S(2)}, u32[]{:S(2)}) collective-permute-start(bf16[64,4096]{1,0:T(8,128)(2,1)S(1)} %bitcast.28), channel_id=1, source_target_pairs={{0,16},{16,0},{1,17},{17,1},{2,18},{18,2},{3,19},{19,3},{4,20},{20... | collective-permute-start | bytes 1572872 | tf_op jit(solution)/shard_map/ppermute | solution.py:421
  61.5 36.8 %all-to-all-start.2 = ((bf16[16,128,256]{2,1,0:T(8,128)(2,1)}), bf16[16,128,256]{2,1,0:T(8,128)(2,1)S(1)}, u32[]{:S(2)}, u32[]{:S(2)}) async-start(bf16[16,128,256]{2,1,0:T(8,128)(2,1)} %bitcast.7), calls=%async_computation.2 | async-start | bytes 2097152 | tf_op jit(solution)/shard_map/all_to_all | solution.py:425
  71.3 27.0 %collective-permute-start.3 = (bf16[128,128]{1,0:T(8,128)(2,1)S(1)}, bf16[128,128]{1,0:T(8,128)(2,1)S(1)}, u32[]{:S(2)}, u32[]{:S(2)}) collective-permute-start(bf16[128,128]{1,0:T(8,128)(2,1)S(1)} %get-tuple-element.30), channel_id=1, source_target_pairs={{0,8},{8,0},{1,9},{9,1},{2,10},{10,2},{3,11},{11,3},{4,12},{12,4},... | collective-permute-start | bytes 98312 | tf_op jit(solution)/shard_map/ppermute | solution.py:421
  132.8 18.1 %copy-start.2 = (bf16[2048,384]{1,0:T(8,128)(2,1)S(1)}, bf16[2048,384]{1,0:T(8,128)(2,1)}, u32[]{:S(2)}) copy-start(bf16[2048,384]{1,0:T(8,128)(2,1)} %all-gather.3.cloned.1.call-done) | copy-start | bytes 4718596
  147.9 4.6 %collective-permute-start.4 = (bf16[1024,256]{1,0:T(8,128)(2,1)S(1)}, bf16[1024,256]{1,0:T(8,128)(2,1)S(1)}, u32[]{:S(2)}, u32[]{:S(2)}) collective-permute-start(bf16[1024,256]{1,0:T(8,128)(2,1)S(1)} %bitcast.38), channel_id=1, source_target_pairs={{0,16},{16,0},{1,17},{17,1},{2,18},{18,2},{3,19},{19,3},{4,20},{20... | collective-permute-start | bytes 1572872 | tf_op jit(solution)/shard_map/ppermute | solution.py:421
Sparse Core Ops, SparseCore 0:
  26.6 36.6 all-gather.2
  65.1 48.9 all-gather.4

commit v10 on v9

--- a/solution.py
+++ b/solution.py
@@ -28,26 +28,13 @@
     return pltpu.CompilerParams(vmem_limit_bytes=megabytes * MB)
 
 
-def in_three(x):
-    high = x.astype(BF16).astype(F32)
-    rest = x - high
-    middle = rest.astype(BF16).astype(F32)
-    return high, middle, rest - middle
-
-
 def packed(peak, total):
-    p0, p1, p2 = in_three(peak)
-    t0, t1, t2 = in_three(total)
     blank = jnp.zeros_like(peak)
-    parts = [p0, p1, p2, t0, t1, t2, blank, blank]
-    return jnp.concatenate(parts, axis=1).astype(BF16)
+    return jnp.concatenate([peak, total, blank, blank], axis=1)
 
 
 def unpacked(stats):
-    stats = stats.astype(F32)
-    peak = stats[:, 0:32] + stats[:, 32:64] + stats[:, 64:96]
-    total = stats[:, 96:128] + stats[:, 128:160] + stats[:, 160:192]
-    return peak, total
+    return stats[:, 0:32], stats[:, 32:64]
 
 
 def embed_kernel(
@@ -120,14 +107,14 @@
             copy.start()
             leaving.append(copy)
 
-    leave(width, 256)
+    leave(width, 128)
     for h in range(heads):
         cols = slice(h * HD, (h + 1) * HD)
         numer = weights[0][:, h : h + 1] * embedded[0, :, cols].astype(F32)
         for v in range(1, count):
             numer = numer + weights[v][:, h : h + 1] * embedded[v, :, cols].astype(F32)
-        keep[:, cols] = numer[:half].astype(BF16)
-        send[:, cols] = numer[half:].astype(BF16)
+        keep[:, cols] = numer[:half]
+        send[:, cols] = numer[half:]
         if h % 8 == 7:
             leave((h - 7) * HD, 8 * HD)
     for copy in slices + leaving:
@@ -140,7 +127,7 @@
     heads = query.shape[0]
     half = rows // 2
     hbm = pl.BlockSpec(memory_space=pltpu.HBM)
-    part = jax.ShapeDtypeStruct((half, width + 256), BF16)
+    part = jax.ShapeDtypeStruct((half, width + 128), F32)
     return pl.pallas_call(
         embed_kernel,
         in_specs=[hbm] * 5,
@@ -153,8 +140,8 @@
             pltpu.VMEM((count, rows, width), BF16),
             pltpu.VMEM((count, rows, heads), F32),
             pltpu.VMEM((count, depth, width), BF16),
-            pltpu.VMEM((half, width + 256), BF16),
-            pltpu.VMEM((half, width + 256), BF16),
+            pltpu.VMEM((half, width + 128), F32),
+            pltpu.VMEM((half, width + 128), F32),
             pltpu.SemaphoreType.DMA((count,)),
             pltpu.SemaphoreType.DMA((5,)),
             pltpu.SemaphoreType.DMA((2, 5)),
@@ -175,7 +162,7 @@
     cot_out_ref[pl.ds(pl.multiple_of(x_hi * tokens, tokens), tokens), :] = cot_ref[...]
     cot_out_ref[pl.ds(pl.multiple_of((1 - x_hi) * tokens, tokens), tokens), :] = cot_got_ref[...]
     rows, padded = mine_ref.shape
-    width = padded - 256
+    width = padded - 128
     heads = width // HD
     peak_a, total_a = unpacked(mine_ref[:, width:])
     peak_b, total_b = unpacked(other_ref[:, width:])
@@ -184,9 +171,9 @@
     scale_b = jnp.exp(peak_b - top)
     for h in range(heads):
         cols = slice(h * HD, (h + 1) * HD)
-        first = mine_ref[:, cols].astype(F32) * scale_a[:, h : h + 1]
-        second = other_ref[:, cols].astype(F32) * scale_b[:, h : h + 1]
-        out_ref[:, cols] = (first + second).astype(BF16)
+        first = mine_ref[:, cols] * scale_a[:, h : h + 1]
+        second = other_ref[:, cols] * scale_b[:, h : h + 1]
+        out_ref[:, cols] = first + second
     out_ref[:, width:] = packed(top, total_a * scale_a + total_b * scale_b)
 
 
@@ -195,7 +182,7 @@
     return pl.pallas_call(
         pair_kernel,
         out_shape=(
-            jax.ShapeDtypeStruct(other.shape, BF16),
+            jax.ShapeDtypeStruct(other.shape, F32),
             jax.ShapeDtypeStruct((2 * tokens, cols), BF16),
         ),
         compiler_params=params(12),
@@ -205,7 +192,7 @@
 
 def merge_kernel(parts_ref, gain_ref, normed_ref, kept_ref, whole):
     rows, padded = parts_ref.shape
-    width = padded - 256
+    width = padded - 128
     heads = width // HD
     share = 8
     sources = rows // share
@@ -221,9 +208,8 @@
     for h in range(heads):
         cols = slice(h * HD, (h + 1) * HD)
         numer = jnp.zeros((share, HD), F32)
-        for at in range(0, rows, 16):
-            block = parts_ref[at : at + 16, cols].astype(F32) * scale[at : at + 16, h : h + 1]
-            numer = numer + block[:8] + block[8:]
+        for at in range(0, rows, share):
+            numer = numer + parts_ref[at : at + share, cols] * scale[at : at + share, h : h + 1]
         value = (numer / total[:, h : h + 1]).astype(BF16).astype(F32)
         whole[:, cols] = value
         sums = sums + value
@@ -249,7 +235,7 @@
 
 def merge(parts, gain, copies):
     rows, padded = parts.shape
-    width = padded - 256
+    width = padded - 128
     return pl.pallas_call(
         merge_kernel,
         out_shape=(

time: 161 us -> 167 us (1.037)
  blocking collectives: 71.1 us -> 75.5 us
    all_to_all x5, blocking collectives: 71.1 us -> 75.5 us  [exchange(): return lax.all_to_all(x, axes, 0, 0, tiled=True)]
where the time goes in v10:
time: 167 us
  blocking collectives  75.5 us (45%)
  waiting for transfers between devices  29 us (17%)
  starting transfers between devices  23.6 us (14%)
  Pallas kernels  21.7 us (13%)
  between operations  13.5 us (8%)
  matrix products  1.7 us (1%)
    all_to_all x5, blocking collectives, exchange(): return lax.all_to_all(x, axes, 0, 0, tiled=True)  75.5 us
    all_to_all x1, waiting for transfers between devices, exchange(): return lax.all_to_all(x, axes, 0, 0, tiled=True)  24.1 us
    ppermute x5, starting transfers between devices, swap(): return lax.ppermute(x, axis, [(0, 1), (1, 0)])  13.6 us
    pallas_call x1, Pallas kernels, embed(): pl.pallas_call(embed_kernel, in_specs=[hbm] * 5, out_specs=[hbm] * 3, out...  11 us
    all_to_all x1, starting transfers between devices, exchange(): return lax.all_to_all(x, axes, 0, 0, tiled=True)  9.94 us
    ppermute x5, waiting for transfers between devices, swap(): return lax.ppermute(x, axis, [(0, 1), (1, 0)])  4.86 us
    pallas_call x1, Pallas kernels, project(): pl.pallas_call(qkv_kernel, in_specs=[vmem, vmem, hbm], out_shape=[jax.Sha...  4.75 us
  transfers between devices with their start and end apart: 8, of which 4 were waited for; matrix products, arithmetic and copies ran while one was open for 1% of the time, Pallas kernels for 11%

profile of v10, /device:TPU:1, one launch (start us, length us, event | category | flops | bytes accessed | tf_op | source)
XLA Modules:
  0.0 166.7 jit_solution(208678528232021707)
XLA Ops:
  6.5 0.0 all-gather.3.cloned.1.call-start
  6.5 3.6 %collective-permute-start = (bf16[128,384]{1,0:T(8,128)(2,1)}, bf16[128,384]{1,0:T(8,128)(2,1)S(1)}, u32[]{:S(2)}, u32[]{:S(2)}) collective-permute-start(bf16[128,384]{1,0:T(8,128)(2,1)} %cot_ref.1), channel_id=1, source_target_pairs={{0,8},{8,0},{1,9},{9,1},{2,10},{10,2},{3,11},{11,3},{4,12},{12,4},... | collective-permute-start | bytes 294920 | tf_op jit(solution)/shard_map/ppermute | solution.py:407
  10.1 0.0 copy-start.1
  10.1 11.0 %embed.1 = (f32[64,4224]{1,0:T(8,128)}, f32[64,4224]{1,0:T(8,128)}, bf16[256,512]{1,0:T(8,128)(2,1)}) custom-call(bf16[6,64,128]{2,1,0:T(8,128)(2,1)} %bitcast.43, bf16[6,64,4096]{2,1,0:T(8,128)(2,1)} %weight_ref.1, bf16[6,4096]{1,0:T(8,128)(2,1)} %shift_hbm.1, bf16[32,4096]{1,0:T(8,128)(2,1)} %bitcast.41, bf16[256,4096]{1,0:T(8,128)(2,1)} %rows_ref.1), custom_call_target="tpu_custom_call" | custom-call | flops 603979776 | bytes 6291456 | tf_op jit(solution)/shard_map/embed/pallas_call | solution.py:131
  21.1 0.0 collective-permute-done.cot_got_ref
  21.1 1.1 collective-permute-start.1
  22.2 2.5 %collective-permute-done.1.other_ref = f32[64,4224]{1,0:T(8,128)S(1)} collective-permute-done((f32[64,4224]{1,0:T(8,128)}, f32[64,4224]{1,0:T(8,128)S(1)}, u32[]{:S(2)}, u32[]{:S(2)}) %collective-permute-start.1) | collective-permute-done | bytes 1081376 | tf_op jit(solution)/shard_map/ppermute | solution.py:407
  24.7 0.0 copy-done.1
  24.7 0.0 copy-start
  24.7 1.2 copy-done
  26.0 1.3 pair.1
  27.3 0.0 copy-start.3
  27.3 0.0 all-gather.3.cloned.1.call-update
  27.3 0.0 all-gather.5.cloned.1.call-start
  27.4 19.6 %all_to_all.61 = f32[8,8,4224]{2,1,0:T(8,128)S(1)} all-to-all(f32[8,8,4224]{2,1,0:T(8,128)S(1)} %bitcast.31), channel_id=1, replica_groups=mesh['y'=4,'xl'=2,'c'=2,'xh'=2,'z'=8] {'y','xl'}, dimensions={0} | all-to-all | bytes 2162688 | tf_op jit(solution)/shard_map/all_to_all | solution.py:411
  47.0 0.0 all-gather.5.cloned.1.call-update
  47.0 0.0 copy-done.3
  47.0 0.8 merge.1
  47.8 11.6 %all_to_all.62 = bf16[8,8,4096]{2,1,0:T(8,128)(2,1)S(1)} all-to-all(bf16[8,8,4096]{2,1,0:T(8,128)(2,1)S(1)} %bitcast.32), channel_id=1, replica_groups=mesh['y'=4,'xl'=2,'c'=2,'xh'=2,'z'=8] {'y','xl'}, dimensions={0} | all-to-all | bytes 1048576 | tf_op jit(solution)/shard_map/all_to_all | solution.py:411
  59.4 2.2 %collective-permute-start.2 = (bf16[64,4096]{1,0:T(8,128)(2,1)S(1)}, bf16[64,4096]{1,0:T(8,128)(2,1)S(1)}, u32[]{:S(2)}, u32[]{:S(2)}) collective-permute-start(bf16[64,4096]{1,0:T(8,128)(2,1)S(1)} %bitcast.28), channel_id=1, source_target_pairs={{0,16},{16,0},{1,17},{17,1},{2,18},{18,2},{3,19},{19,3},{4,20},{20... | collective-permute-start | bytes 1572872 | tf_op jit(solution)/shard_map/ppermute | solution.py:407
  61.6 1.5 collective-permute-done.2.other_ref
  63.1 4.7 %project.1 = (bf16[2048,256]{1,0:T(8,128)(2,1)}, bf16[128,128]{1,0:T(8,128)(2,1)S(1)}, bf16[128,128]{1,0:T(8,128)(2,1)S(1)}) custom-call(bf16[64,4096]{1,0:T(8,128)(2,1)S(1)} %bitcast.29, bf16[64,4096]{1,0:T(8,128)(2,1)S(1)} %collective-permute-done.2.other_ref, bf16[3,4096,256]{2,1,0:T(8,128)(2,1)} %bitcast.35), custom_call_target="tpu_custom_call" | custom-call | tf_op jit(solution)/shard_map/project/pallas_call | solution.py:297
  67.9 9.9 %all-to-all-start.2 = ((bf16[16,128,256]{2,1,0:T(8,128)(2,1)}), bf16[16,128,256]{2,1,0:T(8,128)(2,1)S(1)}, u32[]{:S(2)}, u32[]{:S(2)}) async-start(bf16[16,128,256]{2,1,0:T(8,128)(2,1)} %bitcast.7), calls=%async_computation.2 | async-start | bytes 2097152 | tf_op jit(solution)/shard_map/all_to_all | solution.py:411
  77.8 2.9 %collective-permute-start.3 = (bf16[128,128]{1,0:T(8,128)(2,1)S(1)}, bf16[128,128]{1,0:T(8,128)(2,1)S(1)}, u32[]{:S(2)}, u32[]{:S(2)}) collective-permute-start(bf16[128,128]{1,0:T(8,128)(2,1)S(1)} %get-tuple-element.30), channel_id=1, source_target_pairs={{0,8},{8,0},{1,9},{9,1},{2,10},{10,2},{3,11},{11,3},{4,12},{12,4},... | collective-permute-start | bytes 98312 | tf_op jit(solution)/shard_map/ppermute | solution.py:407
  80.7 0.0 all-gather.3.cloned.1.call-done
  80.7 24.1 %all-to-all-done.2 = bf16[16,128,256]{2,1,0:T(8,128)(2,1)S(1)} async-done(((bf16[16,128,256]{2,1,0:T(8,128)(2,1)}), bf16[16,128,256]{2,1,0:T(8,128)(2,1)S(1)}, u32[]{:S(2)}, u32[]{:S(2)}) %all-to-all-start.2) | async-done | bytes 1048608 | tf_op jit(solution)/shard_map/all_to_all | solution.py:411
  104.8 0.0 collective-permute-done.3.got_ref
  104.8 1.3 attend.1
  106.2 12.4 %all_to_all.63 = bf16[32,8,128]{2,1,0:T(8,128)(2,1)S(1)} all-to-all(bf16[32,8,128]{2,1,0:T(8,128)(2,1)S(1)} %bitcast.33), channel_id=1, replica_groups=mesh['y'=4,'xl'=2,'c'=2,'xh'=2,'z'=8] {'y','xl','c','xh'}, dimensions={0} | all-to-all | bytes 131072 | tf_op jit(solution)/shard_map/all_to_all | solution.py:411
  118.5 0.1 broadcast_in_dim.9
  118.6 20.7 %all_to_all.64.parts_ref = bf16[8,288,128]{2,1,0:T(8,128)(2,1)S(1)} all-to-all(bf16[8,288,128]{2,1,0:T(8,128)(2,1)S(1)} %pad_maximum_fusion), channel_id=1, replica_groups=mesh['y'=4,'xl'=2,'c'=2,'xh'=2,'z'=8] {'z'}, dimensions={0} | all-to-all | bytes 1179648 | tf_op jit(solution)/shard_map/all_to_all | solution.py:411
  139.4 0.0 all-gather.5.cloned.1.call-done.weight_ref
  139.4 0.0 copy-start.2
  139.4 2.6 %output.1 = bf16[1024,256]{1,0:T(8,128)(2,1)S(1)} custom-call(bf16[8,288,128]{2,1,0:T(8,128)(2,1)S(1)} %all_to_all.64.parts_ref, bf16[4096,512]{1,0:T(8,128)(2,1)} %all-gather.5.cloned.1.call-done.weight_ref), custom_call_target="tpu_custom_call" | custom-call | tf_op jit(solution)/shard_map/output/pallas_call | solution.py:392
  142.0 11.3 %all_to_all.65 = bf16[16,64,256]{2,1,0:T(8,128)(2,1)S(1)} all-to-all(bf16[16,64,256]{2,1,0:T(8,128)(2,1)S(1)} %bitcast.30), channel_id=1, replica_groups=mesh['y'=4,'xl'=2,'c'=2,'xh'=2,'z'=8] {'y','xl','xh'}, dimensions={0} | all-to-all | bytes 1048576 | tf_op jit(solution)/shard_map/all_to_all | solution.py:411
  153.2 3.9 %collective-permute-start.4 = (bf16[1024,256]{1,0:T(8,128)(2,1)S(1)}, bf16[1024,256]{1,0:T(8,128)(2,1)S(1)}, u32[]{:S(2)}, u32[]{:S(2)}) collective-permute-start(bf16[1024,256]{1,0:T(8,128)(2,1)S(1)} %bitcast.38), channel_id=1, source_target_pairs={{0,16},{16,0},{1,17},{17,1},{2,18},{18,2},{3,19},{19,3},{4,20},{20... | collective-permute-start | bytes 1572872 | tf_op jit(solution)/shard_map/ppermute | solution.py:407
  157.2 0.0 copy-done.2
  157.2 0.3 copy.9
  157.4 0.5 fusion.1
  157.9 0.8 collective-permute-done.4
  158.7 1.2 convolution_add_fusion
  (2 shorter events, 0.1 us)
Async XLA Ops:
  6.5 74.2 %all-gather.3.cloned.1.call-start = ((), (), s32[]{:S(2)}) async-start(), calls=%async_computation.6 | async-start | bytes 1769472 | tf_op jit(solution)/shard_map/all_gather | solution.py:424
  6.5 14.6 %collective-permute-start = (bf16[128,384]{1,0:T(8,128)(2,1)}, bf16[128,384]{1,0:T(8,128)(2,1)S(1)}, u32[]{:S(2)}, u32[]{:S(2)}) collective-permute-start(bf16[128,384]{1,0:T(8,128)(2,1)} %cot_ref.1), channel_id=1, source_target_pairs={{0,8},{8,0},{1,9},{9,1},{2,10},{10,2},{3,11},{11,3},{4,12},{12,4},... | collective-permute-start | bytes 294920 | tf_op jit(solution)/shard_map/ppermute | solution.py:407
  10.1 14.6 %copy-start.1 = (bf16[128,384]{1,0:T(8,128)(2,1)S(1)}, bf16[128,384]{1,0:T(8,128)(2,1)}, u32[]{:S(2)}) copy-start(bf16[128,384]{1,0:T(8,128)(2,1)} %cot_ref.1) | copy-start | bytes 294916
  21.1 3.6 %collective-permute-start.1 = (f32[64,4224]{1,0:T(8,128)}, f32[64,4224]{1,0:T(8,128)S(1)}, u32[]{:S(2)}, u32[]{:S(2)}) collective-permute-start(f32[64,4224]{1,0:T(8,128)} %get-tuple-element.23), channel_id=1, source_target_pairs={{0,16},{16,0},{1,17},{17,1},{2,18},{18,2},{3,19},{19,3},{4,20},{20... | collective-permute-start | bytes 3244040 | tf_op jit(solution)/shard_map/ppermute | solution.py:407
  24.7 1.2 copy-start
  27.3 19.7 %copy-start.3 = (bf16[4096]{0:T(1024)(128)(2,1)S(1)}, bf16[4096]{0:T(1024)(128)(2,1)}, u32[]{:S(2)}) copy-start(bf16[4096]{0:T(1024)(128)(2,1)} %param.12) | copy-start | bytes 24580
  27.3 112.1 %all-gather.5.cloned.1.call-start = ((), (), s32[]{:S(2)}) async-start(), calls=%async_computation.7 | async-start | bytes 4456448 | tf_op jit(solution)/shard_map/all_gather | solution.py:426
  59.4 3.7 %collective-permute-start.2 = (bf16[64,4096]{1,0:T(8,128)(2,1)S(1)}, bf16[64,4096]{1,0:T(8,128)(2,1)S(1)}, u32[]{:S(2)}, u32[]{:S(2)}) collective-permute-start(bf16[64,4096]{1,0:T(8,128)(2,1)S(1)} %bitcast.28), channel_id=1, source_target_pairs={{0,16},{16,0},{1,17},{17,1},{2,18},{18,2},{3,19},{19,3},{4,20},{20... | collective-permute-start | bytes 1572872 | tf_op jit(solution)/shard_map/ppermute | solution.py:407
  67.9 37.0 %all-to-all-start.2 = ((bf16[16,128,256]{2,1,0:T(8,128)(2,1)}), bf16[16,128,256]{2,1,0:T(8,128)(2,1)S(1)}, u32[]{:S(2)}, u32[]{:S(2)}) async-start(bf16[16,128,256]{2,1,0:T(8,128)(2,1)} %bitcast.7), calls=%async_computation.2 | async-start | bytes 2097152 | tf_op jit(solution)/shard_map/all_to_all | solution.py:411
  77.8 27.0 %collective-permute-start.3 = (bf16[128,128]{1,0:T(8,128)(2,1)S(1)}, bf16[128,128]{1,0:T(8,128)(2,1)S(1)}, u32[]{:S(2)}, u32[]{:S(2)}) collective-permute-start(bf16[128,128]{1,0:T(8,128)(2,1)S(1)} %get-tuple-element.30), channel_id=1, source_target_pairs={{0,8},{8,0},{1,9},{9,1},{2,10},{10,2},{3,11},{11,3},{4,12},{12,4},... | collective-permute-start | bytes 98312 | tf_op jit(solution)/shard_map/ppermute | solution.py:407
  139.4 17.8 %copy-start.2 = (bf16[2048,384]{1,0:T(8,128)(2,1)S(1)}, bf16[2048,384]{1,0:T(8,128)(2,1)}, u32[]{:S(2)}) copy-start(bf16[2048,384]{1,0:T(8,128)(2,1)} %all-gather.3.cloned.1.call-done) | copy-start | bytes 4718596
  153.2 5.5 %collective-permute-start.4 = (bf16[1024,256]{1,0:T(8,128)(2,1)S(1)}, bf16[1024,256]{1,0:T(8,128)(2,1)S(1)}, u32[]{:S(2)}, u32[]{:S(2)}) collective-permute-start(bf16[1024,256]{1,0:T(8,128)(2,1)S(1)} %bitcast.38), channel_id=1, source_target_pairs={{0,16},{16,0},{1,17},{17,1},{2,18},{18,2},{3,19},{19,3},{4,20},{20... | collective-permute-start | bytes 1572872 | tf_op jit(solution)/shard_map/ppermute | solution.py:407
Sparse Core Ops, SparseCore 0:
  27.4 36.6 all-gather.2
  66.0 48.8 all-gather.4

commit v11 on v10

--- a/solution.py
+++ b/solution.py
@@ -156,6 +156,20 @@
     )(pixels, weight, shift, query, out_weight)
 
 
+def stage_kernel(source_ref, target_ref):
+    target_ref[...] = source_ref[...]
+
+
+def stage(source):
+    return pl.pallas_call(
+        stage_kernel,
+        out_shape=jax.ShapeDtypeStruct(source.shape, F32),
+        compiler_params=params(12),
+        cost_estimate=pl.CostEstimate(flops=0, bytes_accessed=8 * MB, transcendentals=0),
+        name="stage",
+    )(source)
+
+
 def pair_kernel(mine_ref, other_ref, cot_ref, cot_got_ref, out_ref, cot_out_ref):
     x_hi = lax.axis_index("xh")
     tokens = cot_ref.shape[0]
@@ -420,7 +434,7 @@
         patches.transpose(0, 2, 1), patch_weight, var_embed, agg_query.T, out_weight
     )
     send, cot_got = lax.optimization_barrier((send, cot_got))
-    parts, cot = pair(keep, swap(send, "c"), head_cot, cot_got)
+    parts, cot = pair(stage(keep), swap(send, "c"), head_cot, cot_got)
     cot = lax.all_gather(cot, "z", axis=0, tiled=True)
     parts, cols = lax.optimization_barrier((exchange(parts, CHIPS), cols))
     cols = lax.all_gather(cols, VAR, axis=0, tiled=True)

time: 167 us -> 166 us (level)
  no operation moved by 1% of the time
where the time goes in v11:
time: 166 us; the launch traced here: 165 us
  blocking collectives  75.6 us (46%)
  waiting for transfers between devices  27.7 us (17%)
  starting transfers between devices  23.4 us (14%)
  Pallas kernels  21.8 us (13%)
  between operations  13.5 us (8%)
  matrix products  1.7 us (1%)
    all_to_all x5, blocking collectives, exchange(): return lax.all_to_all(x, axes, 0, 0, tiled=True)  75.6 us
    all_to_all x1, waiting for transfers between devices, exchange(): return lax.all_to_all(x, axes, 0, 0, tiled=True)  24.2 us
    ppermute x5, starting transfers between devices, swap(): return lax.ppermute(x, axis, [(0, 1), (1, 0)])  13.6 us
    pallas_call x1, Pallas kernels, embed(): pl.pallas_call(embed_kernel, in_specs=[hbm] * 5, out_specs=[hbm] * 3, out...  11 us
    all_to_all x1, starting transfers between devices, exchange(): return lax.all_to_all(x, axes, 0, 0, tiled=True)  9.76 us
    pallas_call x1, Pallas kernels, project(): pl.pallas_call(qkv_kernel, in_specs=[vmem, vmem, hbm], out_shape=[jax.Sha...  4.75 us
    ppermute x5, waiting for transfers between devices, swap(): return lax.ppermute(x, axis, [(0, 1), (1, 0)])  3.55 us
  transfers between devices with their start and end apart: 8, of which 4 were waited for; matrix products, arithmetic and copies ran while one was open for 1% of the time, Pallas kernels for 11%

profile of v11, /device:TPU:1, one launch (start us, length us, event | category | flops | bytes accessed | tf_op | source)
XLA Modules:
  0.0 165.3 jit_solution(14978556713016232877)
XLA Ops:
  6.5 0.0 all-gather.3.cloned.1.call-start
  6.5 3.6 %collective-permute-start = (bf16[128,384]{1,0:T(8,128)(2,1)}, bf16[128,384]{1,0:T(8,128)(2,1)S(1)}, u32[]{:S(2)}, u32[]{:S(2)}) collective-permute-start(bf16[128,384]{1,0:T(8,128)(2,1)} %cot_ref.1), channel_id=1, source_target_pairs={{0,8},{8,0},{1,9},{9,1},{2,10},{10,2},{3,11},{11,3},{4,12},{12,4},... | collective-permute-start | bytes 294920 | tf_op jit(solution)/shard_map/ppermute | solution.py:421
  10.1 0.0 copy-start.1
  10.1 11.0 %embed.1 = (f32[64,4224]{1,0:T(8,128)}, f32[64,4224]{1,0:T(8,128)}, bf16[256,512]{1,0:T(8,128)(2,1)}) custom-call(bf16[6,64,128]{2,1,0:T(8,128)(2,1)} %bitcast.43, bf16[6,64,4096]{2,1,0:T(8,128)(2,1)} %weight_ref.1, bf16[6,4096]{1,0:T(8,128)(2,1)} %shift_hbm.1, bf16[32,4096]{1,0:T(8,128)(2,1)} %bitcast.41, bf16[256,4096]{1,0:T(8,128)(2,1)} %rows_ref.1), custom_call_target="tpu_custom_call" | custom-call | flops 603979776 | bytes 6291456 | tf_op jit(solution)/shard_map/embed/pallas_call | solution.py:131
  21.1 0.0 collective-permute-done.cot_got_ref
  21.1 1.1 collective-permute-start.1
  22.2 0.0 copy-start
  22.2 1.2 copy-done
  23.4 0.1 stage.1.mine_ref
  23.5 1.2 collective-permute-done.1.other_ref
  24.7 0.0 copy-done.1
  24.7 1.3 pair.1
  26.1 0.0 copy-start.3
  26.1 0.0 all-gather.3.cloned.1.call-update
  26.1 0.0 all-gather.5.cloned.1.call-start
  26.1 19.6 %all_to_all.61 = f32[8,8,4224]{2,1,0:T(8,128)S(1)} all-to-all(f32[8,8,4224]{2,1,0:T(8,128)S(1)} %bitcast.31), channel_id=1, replica_groups=mesh['y'=4,'xl'=2,'c'=2,'xh'=2,'z'=8] {'y','xl'}, dimensions={0} | all-to-all | bytes 2162688 | tf_op jit(solution)/shard_map/all_to_all | solution.py:425
  45.7 0.0 all-gather.5.cloned.1.call-update
  45.8 0.0 copy-done.3
  45.8 0.8 merge.1
  46.5 11.6 %all_to_all.62 = bf16[8,8,4096]{2,1,0:T(8,128)(2,1)S(1)} all-to-all(bf16[8,8,4096]{2,1,0:T(8,128)(2,1)S(1)} %bitcast.32), channel_id=1, replica_groups=mesh['y'=4,'xl'=2,'c'=2,'xh'=2,'z'=8] {'y','xl'}, dimensions={0} | all-to-all | bytes 1048576 | tf_op jit(solution)/shard_map/all_to_all | solution.py:425
  58.1 2.2 %collective-permute-start.2 = (bf16[64,4096]{1,0:T(8,128)(2,1)S(1)}, bf16[64,4096]{1,0:T(8,128)(2,1)S(1)}, u32[]{:S(2)}, u32[]{:S(2)}) collective-permute-start(bf16[64,4096]{1,0:T(8,128)(2,1)S(1)} %bitcast.28), channel_id=1, source_target_pairs={{0,16},{16,0},{1,17},{17,1},{2,18},{18,2},{3,19},{19,3},{4,20},{20... | collective-permute-start | bytes 1572872 | tf_op jit(solution)/shard_map/ppermute | solution.py:421
  60.3 1.5 collective-permute-done.2.other_ref
  61.9 4.7 %project.1 = (bf16[2048,256]{1,0:T(8,128)(2,1)}, bf16[128,128]{1,0:T(8,128)(2,1)S(1)}, bf16[128,128]{1,0:T(8,128)(2,1)S(1)}) custom-call(bf16[64,4096]{1,0:T(8,128)(2,1)S(1)} %bitcast.29, bf16[64,4096]{1,0:T(8,128)(2,1)S(1)} %collective-permute-done.2.other_ref, bf16[3,4096,256]{2,1,0:T(8,128)(2,1)} %bitcast.35), custom_call_target="tpu_custom_call" | custom-call | tf_op jit(solution)/shard_map/project/pallas_call | solution.py:311
  66.6 9.8 %all-to-all-start.2 = ((bf16[16,128,256]{2,1,0:T(8,128)(2,1)}), bf16[16,128,256]{2,1,0:T(8,128)(2,1)S(1)}, u32[]{:S(2)}, u32[]{:S(2)}) async-start(bf16[16,128,256]{2,1,0:T(8,128)(2,1)} %bitcast.7), calls=%async_computation.2 | async-start | bytes 2097152 | tf_op jit(solution)/shard_map/all_to_all | solution.py:425
  76.4 2.9 %collective-permute-start.3 = (bf16[128,128]{1,0:T(8,128)(2,1)S(1)}, bf16[128,128]{1,0:T(8,128)(2,1)S(1)}, u32[]{:S(2)}, u32[]{:S(2)}) collective-permute-start(bf16[128,128]{1,0:T(8,128)(2,1)S(1)} %get-tuple-element.30), channel_id=1, source_target_pairs={{0,8},{8,0},{1,9},{9,1},{2,10},{10,2},{3,11},{11,3},{4,12},{12,4},... | collective-permute-start | bytes 98312 | tf_op jit(solution)/shard_map/ppermute | solution.py:421
  79.3 0.0 all-gather.3.cloned.1.call-done
  79.3 24.2 %all-to-all-done.2 = bf16[16,128,256]{2,1,0:T(8,128)(2,1)S(1)} async-done(((bf16[16,128,256]{2,1,0:T(8,128)(2,1)}), bf16[16,128,256]{2,1,0:T(8,128)(2,1)S(1)}, u32[]{:S(2)}, u32[]{:S(2)}) %all-to-all-start.2) | async-done | bytes 1048608 | tf_op jit(solution)/shard_map/all_to_all | solution.py:425
  103.4 0.0 collective-permute-done.3.got_ref
  103.4 1.3 attend.1
  104.8 12.4 %all_to_all.63 = bf16[32,8,128]{2,1,0:T(8,128)(2,1)S(1)} all-to-all(bf16[32,8,128]{2,1,0:T(8,128)(2,1)S(1)} %bitcast.33), channel_id=1, replica_groups=mesh['y'=4,'xl'=2,'c'=2,'xh'=2,'z'=8] {'y','xl','c','xh'}, dimensions={0} | all-to-all | bytes 131072 | tf_op jit(solution)/shard_map/all_to_all | solution.py:425
  117.1 0.1 broadcast_in_dim.9
  117.2 20.7 %all_to_all.64.parts_ref = bf16[8,288,128]{2,1,0:T(8,128)(2,1)S(1)} all-to-all(bf16[8,288,128]{2,1,0:T(8,128)(2,1)S(1)} %pad_maximum_fusion), channel_id=1, replica_groups=mesh['y'=4,'xl'=2,'c'=2,'xh'=2,'z'=8] {'z'}, dimensions={0} | all-to-all | bytes 1179648 | tf_op jit(solution)/shard_map/all_to_all | solution.py:425
  138.0 0.0 all-gather.5.cloned.1.call-done.weight_ref
  138.0 0.0 copy-start.2
  138.0 2.6 %output.1 = bf16[1024,256]{1,0:T(8,128)(2,1)S(1)} custom-call(bf16[8,288,128]{2,1,0:T(8,128)(2,1)S(1)} %all_to_all.64.parts_ref, bf16[4096,512]{1,0:T(8,128)(2,1)} %all-gather.5.cloned.1.call-done.weight_ref), custom_call_target="tpu_custom_call" | custom-call | tf_op jit(solution)/shard_map/output/pallas_call | solution.py:406
  140.5 11.3 %all_to_all.65 = bf16[16,64,256]{2,1,0:T(8,128)(2,1)S(1)} all-to-all(bf16[16,64,256]{2,1,0:T(8,128)(2,1)S(1)} %bitcast.30), channel_id=1, replica_groups=mesh['y'=4,'xl'=2,'c'=2,'xh'=2,'z'=8] {'y','xl','xh'}, dimensions={0} | all-to-all | bytes 1048576 | tf_op jit(solution)/shard_map/all_to_all | solution.py:425
  151.8 3.9 %collective-permute-start.4 = (bf16[1024,256]{1,0:T(8,128)(2,1)S(1)}, bf16[1024,256]{1,0:T(8,128)(2,1)S(1)}, u32[]{:S(2)}, u32[]{:S(2)}) collective-permute-start(bf16[1024,256]{1,0:T(8,128)(2,1)S(1)} %bitcast.38), channel_id=1, source_target_pairs={{0,16},{16,0},{1,17},{17,1},{2,18},{18,2},{3,19},{19,3},{4,20},{20... | collective-permute-start | bytes 1572872 | tf_op jit(solution)/shard_map/ppermute | solution.py:421
  155.7 0.0 copy-done.2
  155.7 0.3 copy.9
  156.0 0.5 fusion.1
  156.5 0.8 collective-permute-done.4
  157.3 1.2 convolution_add_fusion
  (2 shorter events, 0.1 us)
Async XLA Ops:
  6.5 72.7 %all-gather.3.cloned.1.call-start = ((), (), s32[]{:S(2)}) async-start(), calls=%async_computation.6 | async-start | bytes 1769472 | tf_op jit(solution)/shard_map/all_gather | solution.py:438
  6.5 14.6 %collective-permute-start = (bf16[128,384]{1,0:T(8,128)(2,1)}, bf16[128,384]{1,0:T(8,128)(2,1)S(1)}, u32[]{:S(2)}, u32[]{:S(2)}) collective-permute-start(bf16[128,384]{1,0:T(8,128)(2,1)} %cot_ref.1), channel_id=1, source_target_pairs={{0,8},{8,0},{1,9},{9,1},{2,10},{10,2},{3,11},{11,3},{4,12},{12,4},... | collective-permute-start | bytes 294920 | tf_op jit(solution)/shard_map/ppermute | solution.py:421
  10.1 14.6 %copy-start.1 = (bf16[128,384]{1,0:T(8,128)(2,1)S(1)}, bf16[128,384]{1,0:T(8,128)(2,1)}, u32[]{:S(2)}) copy-start(bf16[128,384]{1,0:T(8,128)(2,1)} %cot_ref.1) | copy-start | bytes 294916
  21.1 3.6 %collective-permute-start.1 = (f32[64,4224]{1,0:T(8,128)}, f32[64,4224]{1,0:T(8,128)S(1)}, u32[]{:S(2)}, u32[]{:S(2)}) collective-permute-start(f32[64,4224]{1,0:T(8,128)} %get-tuple-element.23), channel_id=1, source_target_pairs={{0,16},{16,0},{1,17},{17,1},{2,18},{18,2},{3,19},{19,3},{4,20},{20... | collective-permute-start | bytes 3244040 | tf_op jit(solution)/shard_map/ppermute | solution.py:421
  22.2 1.2 copy-start
  26.1 19.7 %copy-start.3 = (bf16[4096]{0:T(1024)(128)(2,1)S(1)}, bf16[4096]{0:T(1024)(128)(2,1)}, u32[]{:S(2)}) copy-start(bf16[4096]{0:T(1024)(128)(2,1)} %param.12) | copy-start | bytes 24580
  26.1 111.9 %all-gather.5.cloned.1.call-start = ((), (), s32[]{:S(2)}) async-start(), calls=%async_computation.7 | async-start | bytes 4456448 | tf_op jit(solution)/shard_map/all_gather | solution.py:440
  58.1 3.8 %collective-permute-start.2 = (bf16[64,4096]{1,0:T(8,128)(2,1)S(1)}, bf16[64,4096]{1,0:T(8,128)(2,1)S(1)}, u32[]{:S(2)}, u32[]{:S(2)}) collective-permute-start(bf16[64,4096]{1,0:T(8,128)(2,1)S(1)} %bitcast.28), channel_id=1, source_target_pairs={{0,16},{16,0},{1,17},{17,1},{2,18},{18,2},{3,19},{19,3},{4,20},{20... | collective-permute-start | bytes 1572872 | tf_op jit(solution)/shard_map/ppermute | solution.py:421
  66.6 36.8 %all-to-all-start.2 = ((bf16[16,128,256]{2,1,0:T(8,128)(2,1)}), bf16[16,128,256]{2,1,0:T(8,128)(2,1)S(1)}, u32[]{:S(2)}, u32[]{:S(2)}) async-start(bf16[16,128,256]{2,1,0:T(8,128)(2,1)} %bitcast.7), calls=%async_computation.2 | async-start | bytes 2097152 | tf_op jit(solution)/shard_map/all_to_all | solution.py:425
  76.4 27.0 %collective-permute-start.3 = (bf16[128,128]{1,0:T(8,128)(2,1)S(1)}, bf16[128,128]{1,0:T(8,128)(2,1)S(1)}, u32[]{:S(2)}, u32[]{:S(2)}) collective-permute-start(bf16[128,128]{1,0:T(8,128)(2,1)S(1)} %get-tuple-element.30), channel_id=1, source_target_pairs={{0,8},{8,0},{1,9},{9,1},{2,10},{10,2},{3,11},{11,3},{4,12},{12,4},... | collective-permute-start | bytes 98312 | tf_op jit(solution)/shard_map/ppermute | solution.py:421
  138.0 17.8 %copy-start.2 = (bf16[2048,384]{1,0:T(8,128)(2,1)S(1)}, bf16[2048,384]{1,0:T(8,128)(2,1)}, u32[]{:S(2)}) copy-start(bf16[2048,384]{1,0:T(8,128)(2,1)} %all-gather.3.cloned.1.call-done) | copy-start | bytes 4718596
  151.8 5.4 %collective-permute-start.4 = (bf16[1024,256]{1,0:T(8,128)(2,1)S(1)}, bf16[1024,256]{1,0:T(8,128)(2,1)S(1)}, u32[]{:S(2)}, u32[]{:S(2)}) collective-permute-start(bf16[1024,256]{1,0:T(8,128)(2,1)S(1)} %bitcast.38), channel_id=1, source_target_pairs={{0,16},{16,0},{1,17},{17,1},{2,18},{18,2},{3,19},{19,3},{4,20},{20... | collective-permute-start | bytes 1572872 | tf_op jit(solution)/shard_map/ppermute | solution.py:421
Sparse Core Ops, SparseCore 0:
  26.2 36.6 all-gather.2
  64.7 49.4 all-gather.4

commit v12 on v11

--- a/solution.py
+++ b/solution.py
@@ -38,8 +38,8 @@
 
 
 def embed_kernel(
-    pixels_hbm, weight_ref, shift_hbm, query_hbm, rows_ref, keep_ref, send_ref, cols_ref,
-    pixels_ref, shift_ref, query_ref, embedded, scores, held, keep, send, sems, small_sems, out_sems,
+    pixels_hbm, weight_ref, shift_ref, query_hbm, rows_ref, keep_ref, send_ref, cols_ref,
+    pixels_ref, query_ref, embedded, scores, held, keep, send, sems, small_sems, out_sems,
 ):
     core = lax.axis_index("c")
     z = lax.axis_index("z")
@@ -48,13 +48,12 @@
     half = rows // 2
     small = [
         pltpu.make_async_copy(pixels_hbm, pixels_ref, small_sems.at[0]),
-        pltpu.make_async_copy(shift_hbm, shift_ref, small_sems.at[1]),
-        pltpu.make_async_copy(query_hbm, query_ref, small_sems.at[2]),
+        pltpu.make_async_copy(query_hbm, query_ref, small_sems.at[1]),
     ]
     copies = [
         pltpu.make_async_copy(weight_ref.at[v], held.at[v], sems.at[v]) for v in range(count)
     ]
-    for copy in [small[0], copies[0], small[1], small[2]] + copies[1:]:
+    for copy in [small[0], copies[0], small[1]] + copies[1:]:
         copy.start()
     cut = cols_ref.shape[1] // 2
     slices = []
@@ -64,7 +63,7 @@
             pltpu.make_async_copy(
                 rows_ref.at[:, pl.ds(place, cut)],
                 cols_ref.at[:, pl.ds(side * cut, cut)],
-                small_sems.at[3 + side],
+                small_sems.at[2 + side],
             )
         )
         slices[side].start()
@@ -73,20 +72,21 @@
     group = (new % half) // 8 * 2 + jnp.where(new < half, core, 1 - core)
     order = jnp.where(old == group * 8 + new % 8, 1.0, 0.0).astype(BF16)
     step = 1024
+    shifts = shift_ref[...].astype(F32)
+    row = lax.broadcasted_iota(jnp.int32, shifts.shape, 0)
     small[0].wait()
     for v in range(count):
         tokens = dot(order, pixels_ref[v], NT).astype(BF16)
         if v == 0:
             small[1].wait()
-            small[2].wait()
         if v % 2 == 0:
             for copy in copies[v : v + 2]:
                 copy.wait()
         total = jnp.zeros((rows, heads), F32)
+        shift = jnp.sum(jnp.where(row == v, shifts, 0.0), axis=0, keepdims=True)
         for at in range(0, width, step):
             block = dot(tokens, held[v, :, at : at + step], NN)
-            shift = shift_ref[v : v + 1, at : at + step].astype(F32)
-            block = (block + shift).astype(BF16)
+            block = (block + shift[:, at : at + step]).astype(BF16)
             embedded[v, :, at : at + step] = block
             total = total + dot(block, query_ref[:, at : at + step], NT)
         scores[v] = total / math.sqrt(HD)
@@ -130,12 +130,11 @@
     part = jax.ShapeDtypeStruct((half, width + 128), F32)
     return pl.pallas_call(
         embed_kernel,
-        in_specs=[hbm] * 5,
+        in_specs=[hbm, hbm, pl.BlockSpec(memory_space=pltpu.VMEM), hbm, hbm],
         out_specs=[hbm] * 3,
         out_shape=(part, part, jax.ShapeDtypeStruct((out_weight.shape[0], width // 8), BF16)),
         scratch_shapes=[
             pltpu.VMEM((count, depth, rows), BF16),
-            pltpu.VMEM((count, width), BF16),
             pltpu.VMEM((heads, width), BF16),
             pltpu.VMEM((count, rows, width), BF16),
             pltpu.VMEM((count, rows, heads), F32),
@@ -143,7 +142,7 @@
             pltpu.VMEM((half, width + 128), F32),
             pltpu.VMEM((half, width + 128), F32),
             pltpu.SemaphoreType.DMA((count,)),
-            pltpu.SemaphoreType.DMA((5,)),
+            pltpu.SemaphoreType.DMA((4,)),
             pltpu.SemaphoreType.DMA((2, 5)),
         ],
         compiler_params=params(60),

time: 166 us -> 167 us (level)
  no operation moved by 1% of the time
where the time goes in v12:
time: 167 us; the launch traced here: 166 us
  blocking collectives  75.6 us (45%)
  waiting for transfers between devices  27.7 us (17%)
  starting transfers between devices  23.4 us (14%)
  Pallas kernels  22.7 us (14%)
  between operations  13.5 us (8%)
  matrix products  1.7 us (1%)
    all_to_all x5, blocking collectives, exchange(): return lax.all_to_all(x, axes, 0, 0, tiled=True)  75.6 us
    all_to_all x1, waiting for transfers between devices, exchange(): return lax.all_to_all(x, axes, 0, 0, tiled=True)  24.2 us
    ppermute x5, starting transfers between devices, swap(): return lax.ppermute(x, axis, [(0, 1), (1, 0)])  13.6 us
    pallas_call x1, Pallas kernels, embed(): pl.pallas_call(embed_kernel, in_specs=[hbm, hbm, pl.BlockSpec(memory_spac...  11.9 us
    all_to_all x1, starting transfers between devices, exchange(): return lax.all_to_all(x, axes, 0, 0, tiled=True)  9.75 us
    pallas_call x1, Pallas kernels, project(): pl.pallas_call(qkv_kernel, in_specs=[vmem, vmem, hbm], out_shape=[jax.Sha...  4.75 us
    ppermute x5, waiting for transfers between devices, swap(): return lax.ppermute(x, axis, [(0, 1), (1, 0)])  3.55 us
  transfers between devices with their start and end apart: 8, of which 4 were waited for; matrix products, arithmetic and copies ran while one was open for 1% of the time, Pallas kernels for 11%

profile of v12, /device:TPU:1, one launch (start us, length us, event | category | flops | bytes accessed | tf_op | source)
XLA Modules:
  0.0 166.2 jit_solution(1136222501525437672)
XLA Ops:
  6.5 0.0 all-gather.3.cloned.1.call-start
  6.5 3.6 %collective-permute-start = (bf16[128,384]{1,0:T(8,128)(2,1)}, bf16[128,384]{1,0:T(8,128)(2,1)S(1)}, u32[]{:S(2)}, u32[]{:S(2)}) collective-permute-start(bf16[128,384]{1,0:T(8,128)(2,1)} %cot_ref.1), channel_id=1, source_target_pairs={{0,8},{8,0},{1,9},{9,1},{2,10},{10,2},{3,11},{11,3},{4,12},{12,4},... | collective-permute-start | bytes 294920 | tf_op jit(solution)/shard_map/ppermute | solution.py:420
  10.1 0.0 copy-start.1
  10.1 11.9 %embed.1 = (f32[64,4224]{1,0:T(8,128)}, f32[64,4224]{1,0:T(8,128)}, bf16[256,512]{1,0:T(8,128)(2,1)}) custom-call(bf16[6,64,128]{2,1,0:T(8,128)(2,1)} %bitcast.43, bf16[6,64,4096]{2,1,0:T(8,128)(2,1)} %weight_ref.1, bf16[6,4096]{1,0:T(8,128)(2,1)} %shift_ref.1, bf16[32,4096]{1,0:T(8,128)(2,1)} %bitcast.41, bf16[256,4096]{1,0:T(8,128)(2,1)} %rows_ref.1), custom_call_target="tpu_custom_call" | custom-call | flops 603979776 | bytes 6291456 | tf_op jit(solution)/shard_map/embed/pallas_call | solution.py:131
  22.0 0.0 collective-permute-done.cot_got_ref
  22.0 1.0 collective-permute-start.1
  23.0 0.0 copy-start
  23.0 1.2 copy-done
  24.3 0.1 stage.1.mine_ref
  24.4 1.2 collective-permute-done.1.other_ref
  25.6 0.0 copy-done.1
  25.6 1.3 pair.1
  26.9 0.0 copy-start.3
  26.9 0.0 all-gather.3.cloned.1.call-update
  26.9 0.0 all-gather.5.cloned.1.call-start
  27.0 19.6 %all_to_all.61 = f32[8,8,4224]{2,1,0:T(8,128)S(1)} all-to-all(f32[8,8,4224]{2,1,0:T(8,128)S(1)} %bitcast.31), channel_id=1, replica_groups=mesh['y'=4,'xl'=2,'c'=2,'xh'=2,'z'=8] {'y','xl'}, dimensions={0} | all-to-all | bytes 2162688 | tf_op jit(solution)/shard_map/all_to_all | solution.py:424
  46.6 0.0 all-gather.5.cloned.1.call-update
  46.6 0.0 copy-done.3
  46.6 0.8 merge.1
  47.4 11.6 %all_to_all.62 = bf16[8,8,4096]{2,1,0:T(8,128)(2,1)S(1)} all-to-all(bf16[8,8,4096]{2,1,0:T(8,128)(2,1)S(1)} %bitcast.32), channel_id=1, replica_groups=mesh['y'=4,'xl'=2,'c'=2,'xh'=2,'z'=8] {'y','xl'}, dimensions={0} | all-to-all | bytes 1048576 | tf_op jit(solution)/shard_map/all_to_all | solution.py:424
  59.0 2.2 %collective-permute-start.2 = (bf16[64,4096]{1,0:T(8,128)(2,1)S(1)}, bf16[64,4096]{1,0:T(8,128)(2,1)S(1)}, u32[]{:S(2)}, u32[]{:S(2)}) collective-permute-start(bf16[64,4096]{1,0:T(8,128)(2,1)S(1)} %bitcast.28), channel_id=1, source_target_pairs={{0,16},{16,0},{1,17},{17,1},{2,18},{18,2},{3,19},{19,3},{4,20},{20... | collective-permute-start | bytes 1572872 | tf_op jit(solution)/shard_map/ppermute | solution.py:420
  61.2 1.5 collective-permute-done.2.other_ref
  62.7 4.8 %project.1 = (bf16[2048,256]{1,0:T(8,128)(2,1)}, bf16[128,128]{1,0:T(8,128)(2,1)S(1)}, bf16[128,128]{1,0:T(8,128)(2,1)S(1)}) custom-call(bf16[64,4096]{1,0:T(8,128)(2,1)S(1)} %bitcast.29, bf16[64,4096]{1,0:T(8,128)(2,1)S(1)} %collective-permute-done.2.other_ref, bf16[3,4096,256]{2,1,0:T(8,128)(2,1)} %bitcast.35), custom_call_target="tpu_custom_call" | custom-call | tf_op jit(solution)/shard_map/project/pallas_call | solution.py:310
  67.5 9.7 %all-to-all-start.2 = ((bf16[16,128,256]{2,1,0:T(8,128)(2,1)}), bf16[16,128,256]{2,1,0:T(8,128)(2,1)S(1)}, u32[]{:S(2)}, u32[]{:S(2)}) async-start(bf16[16,128,256]{2,1,0:T(8,128)(2,1)} %bitcast.7), calls=%async_computation.2 | async-start | bytes 2097152 | tf_op jit(solution)/shard_map/all_to_all | solution.py:424
  77.3 2.9 %collective-permute-start.3 = (bf16[128,128]{1,0:T(8,128)(2,1)S(1)}, bf16[128,128]{1,0:T(8,128)(2,1)S(1)}, u32[]{:S(2)}, u32[]{:S(2)}) collective-permute-start(bf16[128,128]{1,0:T(8,128)(2,1)S(1)} %get-tuple-element.30), channel_id=1, source_target_pairs={{0,8},{8,0},{1,9},{9,1},{2,10},{10,2},{3,11},{11,3},{4,12},{12,4},... | collective-permute-start | bytes 98312 | tf_op jit(solution)/shard_map/ppermute | solution.py:420
  80.1 0.0 all-gather.3.cloned.1.call-done
  80.1 24.2 %all-to-all-done.2 = bf16[16,128,256]{2,1,0:T(8,128)(2,1)S(1)} async-done(((bf16[16,128,256]{2,1,0:T(8,128)(2,1)}), bf16[16,128,256]{2,1,0:T(8,128)(2,1)S(1)}, u32[]{:S(2)}, u32[]{:S(2)}) %all-to-all-start.2) | async-done | bytes 1048608 | tf_op jit(solution)/shard_map/all_to_all | solution.py:424
  104.3 0.0 collective-permute-done.3.got_ref
  104.3 1.3 attend.1
  105.6 12.4 %all_to_all.63 = bf16[32,8,128]{2,1,0:T(8,128)(2,1)S(1)} all-to-all(bf16[32,8,128]{2,1,0:T(8,128)(2,1)S(1)} %bitcast.33), channel_id=1, replica_groups=mesh['y'=4,'xl'=2,'c'=2,'xh'=2,'z'=8] {'y','xl','c','xh'}, dimensions={0} | all-to-all | bytes 131072 | tf_op jit(solution)/shard_map/all_to_all | solution.py:424
  118.0 0.1 broadcast_in_dim.9
  118.1 20.7 %all_to_all.64.parts_ref = bf16[8,288,128]{2,1,0:T(8,128)(2,1)S(1)} all-to-all(bf16[8,288,128]{2,1,0:T(8,128)(2,1)S(1)} %pad_maximum_fusion), channel_id=1, replica_groups=mesh['y'=4,'xl'=2,'c'=2,'xh'=2,'z'=8] {'z'}, dimensions={0} | all-to-all | bytes 1179648 | tf_op jit(solution)/shard_map/all_to_all | solution.py:424
  138.8 0.0 all-gather.5.cloned.1.call-done.weight_ref
  138.8 0.0 copy-start.2
  138.8 2.6 %output.1 = bf16[1024,256]{1,0:T(8,128)(2,1)S(1)} custom-call(bf16[8,288,128]{2,1,0:T(8,128)(2,1)S(1)} %all_to_all.64.parts_ref, bf16[4096,512]{1,0:T(8,128)(2,1)} %all-gather.5.cloned.1.call-done.weight_ref), custom_call_target="tpu_custom_call" | custom-call | tf_op jit(solution)/shard_map/output/pallas_call | solution.py:405
  141.4 11.3 %all_to_all.65 = bf16[16,64,256]{2,1,0:T(8,128)(2,1)S(1)} all-to-all(bf16[16,64,256]{2,1,0:T(8,128)(2,1)S(1)} %bitcast.30), channel_id=1, replica_groups=mesh['y'=4,'xl'=2,'c'=2,'xh'=2,'z'=8] {'y','xl','xh'}, dimensions={0} | all-to-all | bytes 1048576 | tf_op jit(solution)/shard_map/all_to_all | solution.py:424
  152.7 3.9 %collective-permute-start.4 = (bf16[1024,256]{1,0:T(8,128)(2,1)S(1)}, bf16[1024,256]{1,0:T(8,128)(2,1)S(1)}, u32[]{:S(2)}, u32[]{:S(2)}) collective-permute-start(bf16[1024,256]{1,0:T(8,128)(2,1)S(1)} %bitcast.38), channel_id=1, source_target_pairs={{0,16},{16,0},{1,17},{17,1},{2,18},{18,2},{3,19},{19,3},{4,20},{20... | collective-permute-start | bytes 1572872 | tf_op jit(solution)/shard_map/ppermute | solution.py:420
  156.6 0.0 copy-done.2
  156.6 0.3 copy.9
  156.9 0.5 fusion.1
  157.4 0.8 collective-permute-done.4
  158.1 1.2 convolution_add_fusion
  (2 shorter events, 0.1 us)
Async XLA Ops:
  6.5 73.6 %all-gather.3.cloned.1.call-start = ((), (), s32[]{:S(2)}) async-start(), calls=%async_computation.6 | async-start | bytes 1769472 | tf_op jit(solution)/shard_map/all_gather | solution.py:437
  6.5 15.5 %collective-permute-start = (bf16[128,384]{1,0:T(8,128)(2,1)}, bf16[128,384]{1,0:T(8,128)(2,1)S(1)}, u32[]{:S(2)}, u32[]{:S(2)}) collective-permute-start(bf16[128,384]{1,0:T(8,128)(2,1)} %cot_ref.1), channel_id=1, source_target_pairs={{0,8},{8,0},{1,9},{9,1},{2,10},{10,2},{3,11},{11,3},{4,12},{12,4},... | collective-permute-start | bytes 294920 | tf_op jit(solution)/shard_map/ppermute | solution.py:420
  10.1 15.5 %copy-start.1 = (bf16[128,384]{1,0:T(8,128)(2,1)S(1)}, bf16[128,384]{1,0:T(8,128)(2,1)}, u32[]{:S(2)}) copy-start(bf16[128,384]{1,0:T(8,128)(2,1)} %cot_ref.1) | copy-start | bytes 294916
  22.0 3.6 %collective-permute-start.1 = (f32[64,4224]{1,0:T(8,128)}, f32[64,4224]{1,0:T(8,128)S(1)}, u32[]{:S(2)}, u32[]{:S(2)}) collective-permute-start(f32[64,4224]{1,0:T(8,128)} %get-tuple-element.23), channel_id=1, source_target_pairs={{0,16},{16,0},{1,17},{17,1},{2,18},{18,2},{3,19},{19,3},{4,20},{20... | collective-permute-start | bytes 3244040 | tf_op jit(solution)/shard_map/ppermute | solution.py:420
  23.0 1.2 copy-start
  26.9 19.7 %copy-start.3 = (bf16[4096]{0:T(1024)(128)(2,1)S(1)}, bf16[4096]{0:T(1024)(128)(2,1)}, u32[]{:S(2)}) copy-start(bf16[4096]{0:T(1024)(128)(2,1)} %param.12) | copy-start | bytes 24580
  26.9 111.9 %all-gather.5.cloned.1.call-start = ((), (), s32[]{:S(2)}) async-start(), calls=%async_computation.7 | async-start | bytes 4456448 | tf_op jit(solution)/shard_map/all_gather | solution.py:439
  59.0 3.8 %collective-permute-start.2 = (bf16[64,4096]{1,0:T(8,128)(2,1)S(1)}, bf16[64,4096]{1,0:T(8,128)(2,1)S(1)}, u32[]{:S(2)}, u32[]{:S(2)}) collective-permute-start(bf16[64,4096]{1,0:T(8,128)(2,1)S(1)} %bitcast.28), channel_id=1, source_target_pairs={{0,16},{16,0},{1,17},{17,1},{2,18},{18,2},{3,19},{19,3},{4,20},{20... | collective-permute-start | bytes 1572872 | tf_op jit(solution)/shard_map/ppermute | solution.py:420
  67.5 36.8 %all-to-all-start.2 = ((bf16[16,128,256]{2,1,0:T(8,128)(2,1)}), bf16[16,128,256]{2,1,0:T(8,128)(2,1)S(1)}, u32[]{:S(2)}, u32[]{:S(2)}) async-start(bf16[16,128,256]{2,1,0:T(8,128)(2,1)} %bitcast.7), calls=%async_computation.2 | async-start | bytes 2097152 | tf_op jit(solution)/shard_map/all_to_all | solution.py:424
  77.3 27.0 %collective-permute-start.3 = (bf16[128,128]{1,0:T(8,128)(2,1)S(1)}, bf16[128,128]{1,0:T(8,128)(2,1)S(1)}, u32[]{:S(2)}, u32[]{:S(2)}) collective-permute-start(bf16[128,128]{1,0:T(8,128)(2,1)S(1)} %get-tuple-element.30), channel_id=1, source_target_pairs={{0,8},{8,0},{1,9},{9,1},{2,10},{10,2},{3,11},{11,3},{4,12},{12,4},... | collective-permute-start | bytes 98312 | tf_op jit(solution)/shard_map/ppermute | solution.py:420
  138.8 17.8 %copy-start.2 = (bf16[2048,384]{1,0:T(8,128)(2,1)S(1)}, bf16[2048,384]{1,0:T(8,128)(2,1)}, u32[]{:S(2)}) copy-start(bf16[2048,384]{1,0:T(8,128)(2,1)} %all-gather.3.cloned.1.call-done) | copy-start | bytes 4718596
  152.7 5.4 %collective-permute-start.4 = (bf16[1024,256]{1,0:T(8,128)(2,1)S(1)}, bf16[1024,256]{1,0:T(8,128)(2,1)S(1)}, u32[]{:S(2)}, u32[]{:S(2)}) collective-permute-start(bf16[1024,256]{1,0:T(8,128)(2,1)S(1)} %bitcast.38), channel_id=1, source_target_pairs={{0,16},{16,0},{1,17},{17,1},{2,18},{18,2},{3,19},{19,3},{4,20},{20... | collective-permute-start | bytes 1572872 | tf_op jit(solution)/shard_map/ppermute | solution.py:420
Sparse Core Ops, SparseCore 0:
  27.1 36.6 all-gather.2
  65.6 49.4 all-gather.4

commit v13 on v12

--- a/solution.py
+++ b/solution.py
@@ -39,7 +39,7 @@
 
 def embed_kernel(
     pixels_hbm, weight_ref, shift_ref, query_hbm, rows_ref, keep_ref, send_ref, cols_ref,
-    pixels_ref, query_ref, embedded, scores, held, keep, send, sems, small_sems, out_sems,
+    pixels_ref, shifts, query_ref, embedded, scores, held, keep, send, sems, small_sems, out_sems,
 ):
     core = lax.axis_index("c")
     z = lax.axis_index("z")
@@ -72,8 +72,7 @@
     group = (new % half) // 8 * 2 + jnp.where(new < half, core, 1 - core)
     order = jnp.where(old == group * 8 + new % 8, 1.0, 0.0).astype(BF16)
     step = 1024
-    shifts = shift_ref[...].astype(F32)
-    row = lax.broadcasted_iota(jnp.int32, shifts.shape, 0)
+    shifts[...] = shift_ref[...].astype(F32)
     small[0].wait()
     for v in range(count):
         tokens = dot(order, pixels_ref[v], NT).astype(BF16)
@@ -83,10 +82,9 @@
             for copy in copies[v : v + 2]:
                 copy.wait()
         total = jnp.zeros((rows, heads), F32)
-        shift = jnp.sum(jnp.where(row == v, shifts, 0.0), axis=0, keepdims=True)
         for at in range(0, width, step):
             block = dot(tokens, held[v, :, at : at + step], NN)
-            block = (block + shift[:, at : at + step]).astype(BF16)
+            block = (block + shifts[v : v + 1, at : at + step]).astype(BF16)
             embedded[v, :, at : at + step] = block
             total = total + dot(block, query_ref[:, at : at + step], NT)
         scores[v] = total / math.sqrt(HD)
@@ -135,6 +133,7 @@
         out_shape=(part, part, jax.ShapeDtypeStruct((out_weight.shape[0], width // 8), BF16)),
         scratch_shapes=[
             pltpu.VMEM((count, depth, rows), BF16),
+            pltpu.VMEM((count, width), F32),
             pltpu.VMEM((heads, width), BF16),
             pltpu.VMEM((count, rows, width), BF16),
             pltpu.VMEM((count, rows, heads), F32),

time: 167 us -> 167 us (level)
  no operation moved by 1% of the time
where the time goes in v13:
time: 167 us; the launch traced here: 166 us
  blocking collectives  75.6 us (45%)
  waiting for transfers between devices  27.7 us (17%)
  starting transfers between devices  23.4 us (14%)
  Pallas kernels  22.6 us (14%)
  between operations  13.5 us (8%)
  matrix products  1.7 us (1%)
    all_to_all x5, blocking collectives, exchange(): return lax.all_to_all(x, axes, 0, 0, tiled=True)  75.6 us
    all_to_all x1, waiting for transfers between devices, exchange(): return lax.all_to_all(x, axes, 0, 0, tiled=True)  24.2 us
    ppermute x5, starting transfers between devices, swap(): return lax.ppermute(x, axis, [(0, 1), (1, 0)])  13.6 us
    pallas_call x1, Pallas kernels, embed(): pl.pallas_call(embed_kernel, in_specs=[hbm, hbm, pl.BlockSpec(memory_spac...  11.8 us
    all_to_all x1, starting transfers between devices, exchange(): return lax.all_to_all(x, axes, 0, 0, tiled=True)  9.74 us
    pallas_call x1, Pallas kernels, project(): pl.pallas_call(qkv_kernel, in_specs=[vmem, vmem, hbm], out_shape=[jax.Sha...  4.75 us
    ppermute x5, waiting for transfers between devices, swap(): return lax.ppermute(x, axis, [(0, 1), (1, 0)])  3.55 us
  transfers between devices with their start and end apart: 8, of which 4 were waited for; matrix products, arithmetic and copies ran while one was open for 1% of the time, Pallas kernels for 11%

profile of v13, /device:TPU:1, one launch (start us, length us, event | category | flops | bytes accessed | tf_op | source)
XLA Modules:
  0.0 166.2 jit_solution(5218238038105775765)
XLA Ops:
  6.5 0.0 all-gather.3.cloned.1.call-start
  6.5 3.6 %collective-permute-start = (bf16[128,384]{1,0:T(8,128)(2,1)}, bf16[128,384]{1,0:T(8,128)(2,1)S(1)}, u32[]{:S(2)}, u32[]{:S(2)}) collective-permute-start(bf16[128,384]{1,0:T(8,128)(2,1)} %cot_ref.1), channel_id=1, source_target_pairs={{0,8},{8,0},{1,9},{9,1},{2,10},{10,2},{3,11},{11,3},{4,12},{12,4},... | collective-permute-start | bytes 294920 | tf_op jit(solution)/shard_map/ppermute | solution.py:419
  10.1 0.0 copy-start.1
  10.1 11.8 %embed.1 = (f32[64,4224]{1,0:T(8,128)}, f32[64,4224]{1,0:T(8,128)}, bf16[256,512]{1,0:T(8,128)(2,1)}) custom-call(bf16[6,64,128]{2,1,0:T(8,128)(2,1)} %bitcast.43, bf16[6,64,4096]{2,1,0:T(8,128)(2,1)} %weight_ref.1, bf16[6,4096]{1,0:T(8,128)(2,1)} %shift_ref.1, bf16[32,4096]{1,0:T(8,128)(2,1)} %bitcast.41, bf16[256,4096]{1,0:T(8,128)(2,1)} %rows_ref.1), custom_call_target="tpu_custom_call" | custom-call | flops 603979776 | bytes 6291456 | tf_op jit(solution)/shard_map/embed/pallas_call | solution.py:129
  22.0 0.0 collective-permute-done.cot_got_ref
  22.0 1.0 collective-permute-start.1
  23.0 0.0 copy-start
  23.0 1.2 copy-done
  24.2 0.1 stage.1.mine_ref
  24.3 1.2 collective-permute-done.1.other_ref
  25.5 0.0 copy-done.1
  25.6 1.3 pair.1
  26.9 0.0 copy-start.3
  26.9 0.0 all-gather.3.cloned.1.call-update
  26.9 0.0 all-gather.5.cloned.1.call-start
  26.9 19.6 %all_to_all.61 = f32[8,8,4224]{2,1,0:T(8,128)S(1)} all-to-all(f32[8,8,4224]{2,1,0:T(8,128)S(1)} %bitcast.31), channel_id=1, replica_groups=mesh['y'=4,'xl'=2,'c'=2,'xh'=2,'z'=8] {'y','xl'}, dimensions={0} | all-to-all | bytes 2162688 | tf_op jit(solution)/shard_map/all_to_all | solution.py:423
  46.6 0.0 all-gather.5.cloned.1.call-update
  46.6 0.0 copy-done.3
  46.6 0.8 merge.1
  47.4 11.6 %all_to_all.62 = bf16[8,8,4096]{2,1,0:T(8,128)(2,1)S(1)} all-to-all(bf16[8,8,4096]{2,1,0:T(8,128)(2,1)S(1)} %bitcast.32), channel_id=1, replica_groups=mesh['y'=4,'xl'=2,'c'=2,'xh'=2,'z'=8] {'y','xl'}, dimensions={0} | all-to-all | bytes 1048576 | tf_op jit(solution)/shard_map/all_to_all | solution.py:423
  59.0 2.2 %collective-permute-start.2 = (bf16[64,4096]{1,0:T(8,128)(2,1)S(1)}, bf16[64,4096]{1,0:T(8,128)(2,1)S(1)}, u32[]{:S(2)}, u32[]{:S(2)}) collective-permute-start(bf16[64,4096]{1,0:T(8,128)(2,1)S(1)} %bitcast.28), channel_id=1, source_target_pairs={{0,16},{16,0},{1,17},{17,1},{2,18},{18,2},{3,19},{19,3},{4,20},{20... | collective-permute-start | bytes 1572872 | tf_op jit(solution)/shard_map/ppermute | solution.py:419
  61.2 1.5 collective-permute-done.2.other_ref
  62.7 4.7 %project.1 = (bf16[2048,256]{1,0:T(8,128)(2,1)}, bf16[128,128]{1,0:T(8,128)(2,1)S(1)}, bf16[128,128]{1,0:T(8,128)(2,1)S(1)}) custom-call(bf16[64,4096]{1,0:T(8,128)(2,1)S(1)} %bitcast.29, bf16[64,4096]{1,0:T(8,128)(2,1)S(1)} %collective-permute-done.2.other_ref, bf16[3,4096,256]{2,1,0:T(8,128)(2,1)} %bitcast.35), custom_call_target="tpu_custom_call" | custom-call | tf_op jit(solution)/shard_map/project/pallas_call | solution.py:309
  67.5 9.7 %all-to-all-start.2 = ((bf16[16,128,256]{2,1,0:T(8,128)(2,1)}), bf16[16,128,256]{2,1,0:T(8,128)(2,1)S(1)}, u32[]{:S(2)}, u32[]{:S(2)}) async-start(bf16[16,128,256]{2,1,0:T(8,128)(2,1)} %bitcast.7), calls=%async_computation.2 | async-start | bytes 2097152 | tf_op jit(solution)/shard_map/all_to_all | solution.py:423
  77.2 2.9 %collective-permute-start.3 = (bf16[128,128]{1,0:T(8,128)(2,1)S(1)}, bf16[128,128]{1,0:T(8,128)(2,1)S(1)}, u32[]{:S(2)}, u32[]{:S(2)}) collective-permute-start(bf16[128,128]{1,0:T(8,128)(2,1)S(1)} %get-tuple-element.30), channel_id=1, source_target_pairs={{0,8},{8,0},{1,9},{9,1},{2,10},{10,2},{3,11},{11,3},{4,12},{12,4},... | collective-permute-start | bytes 98312 | tf_op jit(solution)/shard_map/ppermute | solution.py:419
  80.1 0.0 all-gather.3.cloned.1.call-done
  80.1 24.2 %all-to-all-done.2 = bf16[16,128,256]{2,1,0:T(8,128)(2,1)S(1)} async-done(((bf16[16,128,256]{2,1,0:T(8,128)(2,1)}), bf16[16,128,256]{2,1,0:T(8,128)(2,1)S(1)}, u32[]{:S(2)}, u32[]{:S(2)}) %all-to-all-start.2) | async-done | bytes 1048608 | tf_op jit(solution)/shard_map/all_to_all | solution.py:423
  104.3 0.0 collective-permute-done.3.got_ref
  104.3 1.3 attend.1
  105.6 12.4 %all_to_all.63 = bf16[32,8,128]{2,1,0:T(8,128)(2,1)S(1)} all-to-all(bf16[32,8,128]{2,1,0:T(8,128)(2,1)S(1)} %bitcast.33), channel_id=1, replica_groups=mesh['y'=4,'xl'=2,'c'=2,'xh'=2,'z'=8] {'y','xl','c','xh'}, dimensions={0} | all-to-all | bytes 131072 | tf_op jit(solution)/shard_map/all_to_all | solution.py:423
  117.9 0.1 broadcast_in_dim.9
  118.1 20.7 %all_to_all.64.parts_ref = bf16[8,288,128]{2,1,0:T(8,128)(2,1)S(1)} all-to-all(bf16[8,288,128]{2,1,0:T(8,128)(2,1)S(1)} %pad_maximum_fusion), channel_id=1, replica_groups=mesh['y'=4,'xl'=2,'c'=2,'xh'=2,'z'=8] {'z'}, dimensions={0} | all-to-all | bytes 1179648 | tf_op jit(solution)/shard_map/all_to_all | solution.py:423
  138.8 0.0 all-gather.5.cloned.1.call-done.weight_ref
  138.8 0.0 copy-start.2
  138.8 2.6 %output.1 = bf16[1024,256]{1,0:T(8,128)(2,1)S(1)} custom-call(bf16[8,288,128]{2,1,0:T(8,128)(2,1)S(1)} %all_to_all.64.parts_ref, bf16[4096,512]{1,0:T(8,128)(2,1)} %all-gather.5.cloned.1.call-done.weight_ref), custom_call_target="tpu_custom_call" | custom-call | tf_op jit(solution)/shard_map/output/pallas_call | solution.py:404
  141.4 11.3 %all_to_all.65 = bf16[16,64,256]{2,1,0:T(8,128)(2,1)S(1)} all-to-all(bf16[16,64,256]{2,1,0:T(8,128)(2,1)S(1)} %bitcast.30), channel_id=1, replica_groups=mesh['y'=4,'xl'=2,'c'=2,'xh'=2,'z'=8] {'y','xl','xh'}, dimensions={0} | all-to-all | bytes 1048576 | tf_op jit(solution)/shard_map/all_to_all | solution.py:423
  152.7 3.9 %collective-permute-start.4 = (bf16[1024,256]{1,0:T(8,128)(2,1)S(1)}, bf16[1024,256]{1,0:T(8,128)(2,1)S(1)}, u32[]{:S(2)}, u32[]{:S(2)}) collective-permute-start(bf16[1024,256]{1,0:T(8,128)(2,1)S(1)} %bitcast.38), channel_id=1, source_target_pairs={{0,16},{16,0},{1,17},{17,1},{2,18},{18,2},{3,19},{19,3},{4,20},{20... | collective-permute-start | bytes 1572872 | tf_op jit(solution)/shard_map/ppermute | solution.py:419
  156.6 0.0 copy-done.2
  156.6 0.3 copy.9
  156.8 0.5 fusion.1
  157.3 0.8 collective-permute-done.4
  158.1 1.2 convolution_add_fusion
  (2 shorter events, 0.1 us)
Async XLA Ops:
  6.5 73.6 %all-gather.3.cloned.1.call-start = ((), (), s32[]{:S(2)}) async-start(), calls=%async_computation.6 | async-start | bytes 1769472 | tf_op jit(solution)/shard_map/all_gather | solution.py:436
  6.5 15.4 %collective-permute-start = (bf16[128,384]{1,0:T(8,128)(2,1)}, bf16[128,384]{1,0:T(8,128)(2,1)S(1)}, u32[]{:S(2)}, u32[]{:S(2)}) collective-permute-start(bf16[128,384]{1,0:T(8,128)(2,1)} %cot_ref.1), channel_id=1, source_target_pairs={{0,8},{8,0},{1,9},{9,1},{2,10},{10,2},{3,11},{11,3},{4,12},{12,4},... | collective-permute-start | bytes 294920 | tf_op jit(solution)/shard_map/ppermute | solution.py:419
  10.1 15.4 %copy-start.1 = (bf16[128,384]{1,0:T(8,128)(2,1)S(1)}, bf16[128,384]{1,0:T(8,128)(2,1)}, u32[]{:S(2)}) copy-start(bf16[128,384]{1,0:T(8,128)(2,1)} %cot_ref.1) | copy-start | bytes 294916
  22.0 3.6 %collective-permute-start.1 = (f32[64,4224]{1,0:T(8,128)}, f32[64,4224]{1,0:T(8,128)S(1)}, u32[]{:S(2)}, u32[]{:S(2)}) collective-permute-start(f32[64,4224]{1,0:T(8,128)} %get-tuple-element.23), channel_id=1, source_target_pairs={{0,16},{16,0},{1,17},{17,1},{2,18},{18,2},{3,19},{19,3},{4,20},{20... | collective-permute-start | bytes 3244040 | tf_op jit(solution)/shard_map/ppermute | solution.py:419
  23.0 1.2 copy-start
  26.9 19.7 %copy-start.3 = (bf16[4096]{0:T(1024)(128)(2,1)S(1)}, bf16[4096]{0:T(1024)(128)(2,1)}, u32[]{:S(2)}) copy-start(bf16[4096]{0:T(1024)(128)(2,1)} %param.12) | copy-start | bytes 24580
  26.9 111.9 %all-gather.5.cloned.1.call-start = ((), (), s32[]{:S(2)}) async-start(), calls=%async_computation.7 | async-start | bytes 4456448 | tf_op jit(solution)/shard_map/all_gather | solution.py:438
  59.0 3.8 %collective-permute-start.2 = (bf16[64,4096]{1,0:T(8,128)(2,1)S(1)}, bf16[64,4096]{1,0:T(8,128)(2,1)S(1)}, u32[]{:S(2)}, u32[]{:S(2)}) collective-permute-start(bf16[64,4096]{1,0:T(8,128)(2,1)S(1)} %bitcast.28), channel_id=1, source_target_pairs={{0,16},{16,0},{1,17},{17,1},{2,18},{18,2},{3,19},{19,3},{4,20},{20... | collective-permute-start | bytes 1572872 | tf_op jit(solution)/shard_map/ppermute | solution.py:419
  67.5 36.8 %all-to-all-start.2 = ((bf16[16,128,256]{2,1,0:T(8,128)(2,1)}), bf16[16,128,256]{2,1,0:T(8,128)(2,1)S(1)}, u32[]{:S(2)}, u32[]{:S(2)}) async-start(bf16[16,128,256]{2,1,0:T(8,128)(2,1)} %bitcast.7), calls=%async_computation.2 | async-start | bytes 2097152 | tf_op jit(solution)/shard_map/all_to_all | solution.py:423
  77.2 27.0 %collective-permute-start.3 = (bf16[128,128]{1,0:T(8,128)(2,1)S(1)}, bf16[128,128]{1,0:T(8,128)(2,1)S(1)}, u32[]{:S(2)}, u32[]{:S(2)}) collective-permute-start(bf16[128,128]{1,0:T(8,128)(2,1)S(1)} %get-tuple-element.30), channel_id=1, source_target_pairs={{0,8},{8,0},{1,9},{9,1},{2,10},{10,2},{3,11},{11,3},{4,12},{12,4},... | collective-permute-start | bytes 98312 | tf_op jit(solution)/shard_map/ppermute | solution.py:419
  138.8 17.8 %copy-start.2 = (bf16[2048,384]{1,0:T(8,128)(2,1)S(1)}, bf16[2048,384]{1,0:T(8,128)(2,1)}, u32[]{:S(2)}) copy-start(bf16[2048,384]{1,0:T(8,128)(2,1)} %all-gather.3.cloned.1.call-done) | copy-start | bytes 4718596
  152.7 5.4 %collective-permute-start.4 = (bf16[1024,256]{1,0:T(8,128)(2,1)S(1)}, bf16[1024,256]{1,0:T(8,128)(2,1)S(1)}, u32[]{:S(2)}, u32[]{:S(2)}) collective-permute-start(bf16[1024,256]{1,0:T(8,128)(2,1)S(1)} %bitcast.38), channel_id=1, source_target_pairs={{0,16},{16,0},{1,17},{17,1},{2,18},{18,2},{3,19},{19,3},{4,20},{20... | collective-permute-start | bytes 1572872 | tf_op jit(solution)/shard_map/ppermute | solution.py:419
Sparse Core Ops, SparseCore 0:
  27.0 36.6 all-gather.2
  65.6 49.4 all-gather.4
